TPU v7x, 32 devices: a whole 2x2x4 slice. The times are simulated.
32 devices in a mesh: dp: 8 (over z, y), tensor: 4 (over x, core).
Axes of the slice: x: 2, y: 2, z: 4, core: 2. Of those that a mesh axis runs over, the one named last changes fastest.
Arguments:
- tokens: bfloat16 [32768, 768], P(('dp', 'tensor')), may hold values from -6 to 6
- cotangent: bfloat16 [32768, 768], P(('dp', 'tensor')), may hold values from -6 to 6
- segments: int32 [64, 512], P('dp'), may hold values from 0 to 3, never falling along the last dimension, each value on 1 to 256 neighbouring positions
- qkv_weight: float32 [3, 768, 768], P(None, 'dp', 'tensor'), may hold values from -0.21875 to 0.21875
- out_weight: float32 [768, 768], P('tensor', 'dp'), may hold values from -1.75 to 1.75
- inner_weight: float32 [768, 3072], P('dp', 'tensor'), may hold values from -0.21875 to 0.21875
- outer_weight: float32 [3072, 768], P('tensor', 'dp'), may hold values from -0.109375 to 0.109375
- vectors: float32 [12, 768], P(None, ('dp', 'tensor')), may hold values from -1 to 3
- qkv_mean: float32 [3, 768, 768], P(None, 'dp', 'tensor'), may hold values from -512 to 512
- out_mean: float32 [768, 768], P('tensor', 'dp'), may hold values from -224 to 224
- inner_mean: float32 [768, 3072], P('dp', 'tensor'), may hold values from -512 to 512
- outer_mean: float32 [3072, 768], P('tensor', 'dp'), may hold values from -512 to 512
- vector_mean: float32 [12, 768], P(None, ('dp', 'tensor')), may hold values from -1024 to 1024
- qkv_square: float32 [3, 768, 768], P(None, 'dp', 'tensor'), may hold values from 8192 to 32768
- out_square: float32 [768, 768], P('tensor', 'dp'), may hold values from 1310.72 to 5242.88
- inner_square: float32 [768, 3072], P('dp', 'tensor'), may hold values from 8192 to 32768
- outer_square: float32 [3072, 768], P('tensor', 'dp'), may hold values from 8192 to 32768
- vector_square: float32 [12, 768], P(None, ('dp', 'tensor')), may hold values from 32768 to 131072
Outputs:
- layer_output: bfloat16 [32768, 768], P(('dp', 'tensor'))
- input_grad: float32 [32768, 768], P(('dp', 'tensor'))
- new_qkv_mean: float32 [3, 768, 768], P(None, 'dp', 'tensor')
- new_qkv_square: float32 [3, 768, 768], P(None, 'dp', 'tensor')
- new_qkv_weight: float32 [3, 768, 768], P(None, 'dp', 'tensor')
- new_out_mean: float32 [768, 768], P('tensor', 'dp')
- new_out_square: float32 [768, 768], P('tensor', 'dp')
- new_out_weight: float32 [768, 768], P('tensor', 'dp')
- new_inner_mean: float32 [768, 3072], P('dp', 'tensor')
- new_inner_square: float32 [768, 3072], P('dp', 'tensor')
- new_inner_weight: float32 [768, 3072], P('dp', 'tensor')
- new_outer_mean: float32 [3072, 768], P('tensor', 'dp')
- new_outer_square: float32 [3072, 768], P('tensor', 'dp')
- new_outer_weight: float32 [3072, 768], P('tensor', 'dp')
- new_vector_mean: float32 [12, 768], P(None, ('dp', 'tensor'))
- new_vector_square: float32 [12, 768], P(None, ('dp', 'tensor'))
- new_vectors: float32 [12, 768], P(None, ('dp', 'tensor'))
- lamb_norms: float32 [2, 15], replicated
Inputs may be any that keep to these rules, and one draw needn't show every extreme that they name: `segments`: along a sequence the segment numbers never fall; a segment holds 1 to 256 tokens, and in every draw some segment holds exactly that many.
All inputs are finite; a program needn't handle non-finite values.
Results may differ from a plain program's by a relative error of at most 0.02.
Values may be sent and summed in bfloat16 or wider, within the bound.
A program may use at most 192 MiB of HBM per device.

v0:
```python
import jax
import jax.numpy as jnp
from jax import lax
from jax.sharding import PartitionSpec as P

HD = 64
STEP = 5


NORM_EPS = 1e-05
ADAM_EPS = 1e-06
MOMENT_DECAY = 0.5
LEARN_RATE = 0.5
WEIGHT_DECAY = 0.01
MASKED = -1e30


def norm_forward(values, gain_row, shift_row):
    row_mean = jnp.mean(values, axis=-1, keepdims=True)
    centred = values - row_mean
    row_var = jnp.mean(centred * centred, axis=-1, keepdims=True)
    inverse = lax.rsqrt(row_var + NORM_EPS)
    normal = centred * inverse
    return (normal * gain_row + shift_row, normal, inverse)


def norm_backward(incoming, normal, inverse, gain_row):
    scaled = incoming * gain_row
    mean_one = jnp.mean(scaled, axis=-1, keepdims=True)
    mean_two = jnp.mean(scaled * normal, axis=-1, keepdims=True)
    passed = inverse * (scaled - mean_one - normal * mean_two)
    return (passed, jnp.sum(incoming * normal, axis=0), jnp.sum(incoming, axis=0))


def masked_scores(query_rows, key_rows, seg_row):
    raw_scores = jnp.einsum(
        "qhe,khe->hqk", query_rows, key_rows, preferred_element_type=jnp.float32
    ) * HD ** (-0.5)
    same_doc = (seg_row[:, None] == seg_row[None, :])[None, :, :]
    return jnp.where(same_doc, raw_scores, MASKED)


def attend_forward(pieces):
    query_rows, key_rows, value_rows, seg_row = pieces
    scores = masked_scores(query_rows, key_rows, seg_row)
    row_max = jnp.max(scores, axis=-1, keepdims=True)
    expo_terms = jnp.exp(scores - row_max)
    row_total = jnp.sum(expo_terms, axis=-1, keepdims=True)
    attn_probs = (expo_terms / row_total).astype(jnp.bfloat16)
    attn_mixed = jnp.einsum(
        "hqk,khe->qhe", attn_probs, value_rows, preferred_element_type=jnp.float32
    )
    return (attn_mixed.astype(jnp.bfloat16), row_max + jnp.log(row_total))


def attend_backward(pieces):
    query_rows, key_rows, value_rows, seg_row, log_total, grad_mixed = pieces
    scores = masked_scores(query_rows, key_rows, seg_row)
    attn_probs = jnp.exp(scores - log_total)
    grad_value = jnp.einsum(
        "hqk,qhe->khe",
        attn_probs.astype(jnp.bfloat16),
        grad_mixed,
        preferred_element_type=jnp.float32,
    )
    grad_probs = jnp.einsum(
        "qhe,khe->hqk", grad_mixed, value_rows, preferred_element_type=jnp.float32
    )
    row_dot = jnp.sum(attn_probs * grad_probs, axis=-1, keepdims=True)
    grad_scores = (attn_probs * (grad_probs - row_dot)).astype(jnp.bfloat16)
    score_scale = HD ** (-0.5)
    grad_query = (
        jnp.einsum("hqk,khe->qhe", grad_scores, key_rows, preferred_element_type=jnp.float32)
        * score_scale
    )
    grad_key = (
        jnp.einsum("hqk,qhe->khe", grad_scores, query_rows, preferred_element_type=jnp.float32)
        * score_scale
    )
    return (
        grad_query.astype(jnp.bfloat16),
        grad_key.astype(jnp.bfloat16),
        grad_value.astype(jnp.bfloat16),
    )


def adam_direction(grad_sum, old_mean, old_square):
    new_mean = MOMENT_DECAY * old_mean + (1.0 - MOMENT_DECAY) * grad_sum
    new_square = MOMENT_DECAY * old_square + (1.0 - MOMENT_DECAY) * grad_sum * grad_sum
    correction = 1.0 - MOMENT_DECAY**STEP
    direction = new_mean / correction / (jnp.sqrt(new_square / correction) + ADAM_EPS)
    return (new_mean, new_square, direction)


def group_squares(qkv_part, out_part, inner_part, outer_part, vector_part):
    return jnp.concatenate(
        [
            jnp.sum(qkv_part * qkv_part, axis=(1, 2)),
            jnp.sum(out_part * out_part)[None],
            jnp.sum(inner_part * inner_part)[None],
            jnp.sum(outer_part * outer_part)[None],
            jnp.sum(vector_part[:8] * vector_part[:8], axis=1),
            jnp.sum(vector_part[8:] * vector_part[8:])[None],
        ]
    )


def lamb_apply(weight_list, update_list, trust_ratio, row_number):
    qkv_new = weight_list[0] - LEARN_RATE * trust_ratio[0:3, None, None] * update_list[0]
    out_new = weight_list[1] - LEARN_RATE * trust_ratio[3] * update_list[1]
    inner_new = weight_list[2] - LEARN_RATE * trust_ratio[4] * update_list[2]
    outer_new = weight_list[3] - LEARN_RATE * trust_ratio[5] * update_list[3]
    row_ratio = jnp.concatenate(
        [trust_ratio[6:14], jnp.broadcast_to(trust_ratio[14], (row_number - 8,))]
    )
    vector_new = weight_list[4] - LEARN_RATE * row_ratio[:, None] * update_list[4]
    return (qkv_new, out_new, inner_new, outer_new, vector_new)


def reduce_ffn(grad_inner_w, grad_outer_w):
    return (
        lax.psum_scatter(grad_inner_w, "dp", scatter_dimension=0, tiled=True),
        lax.psum_scatter(grad_outer_w, "dp", scatter_dimension=1, tiled=True),
    )


def body(
    tokens,
    cotangent,
    segments,
    qkv_weight,
    out_weight,
    inner_weight,
    outer_weight,
    vectors,
    qkv_mean,
    out_mean,
    inner_mean,
    outer_mean,
    vector_mean,
    qkv_square,
    out_square,
    inner_square,
    outer_square,
    vector_square,
):
    qkv_low, out_low, inner_low, outer_low = (
        lax.all_gather(qkv_weight.astype(jnp.bfloat16), "dp", axis=1, tiled=True),
        lax.all_gather(out_weight.astype(jnp.bfloat16), "dp", axis=1, tiled=True),
        lax.all_gather(inner_weight.astype(jnp.bfloat16), "dp", axis=0, tiled=True),
        lax.all_gather(outer_weight.astype(jnp.bfloat16), "dp", axis=1, tiled=True),
    )
    full_vectors = lax.all_gather(vectors, ("dp", "tensor"), axis=1, tiled=True)
    width = full_vectors.shape[1]
    tensor_index = lax.axis_index("tensor")
    zero_index = tensor_index * 0
    head_cols = qkv_low.shape[2]
    hidden_cols = inner_low.shape[1]
    head_bias = lax.dynamic_slice_in_dim(full_vectors[6:8], tensor_index * head_cols, head_cols, 1)
    inner_bias = lax.dynamic_slice_in_dim(
        full_vectors[8:].reshape(-1), tensor_index * hidden_cols, hidden_cols, 0
    )
    every_token = lax.all_gather(tokens, "tensor", axis=0, tiled=True)
    token_count = every_token.shape[0]
    seq_count, seq_length = segments.shape
    projected = jnp.einsum("td,kdc->ktc", every_token, qkv_low, preferred_element_type=jnp.float32)
    proj_bias = jnp.stack([head_bias[0], jnp.zeros_like(head_bias[0]), head_bias[1]])
    projected = (projected + proj_bias[:, None, :]).astype(jnp.bfloat16)
    split_heads = projected.reshape(3, seq_count, seq_length, head_cols // HD, HD)
    attn_mixed, log_total = lax.map(
        attend_forward, (split_heads[0], split_heads[1], split_heads[2], segments)
    )
    attn_mixed = attn_mixed.reshape(token_count, head_cols)
    piece = attn_mixed
    branch = lax.psum_scatter(
        jnp.dot(piece, out_low, preferred_element_type=jnp.float32).astype(jnp.bfloat16),
        "tensor",
        scatter_dimension=0,
        tiled=True,
    ).astype(jnp.float32)
    normed, normal_one, inverse_one = norm_forward(
        tokens.astype(jnp.float32) + branch + full_vectors[4], full_vectors[0], full_vectors[1]
    )
    normed_low = lax.all_gather(normed.astype(jnp.bfloat16), "tensor", axis=0, tiled=True)
    inner_pre = jnp.dot(normed_low, inner_low, preferred_element_type=jnp.float32) + inner_bias
    activation, gelu_pull = jax.vjp(
        lambda entries: jax.nn.gelu(entries, approximate=False), inner_pre
    )
    hidden = activation.astype(jnp.bfloat16)
    piece = hidden
    second_branch = lax.psum_scatter(
        jnp.dot(piece, outer_low, preferred_element_type=jnp.float32).astype(jnp.bfloat16),
        "tensor",
        scatter_dimension=0,
        tiled=True,
    ).astype(jnp.float32)
    result, normal_two, inverse_two = norm_forward(
        normed + second_branch + full_vectors[5], full_vectors[2], full_vectors[3]
    )
    grad_second, grad_gain_two, grad_shift_two = norm_backward(
        cotangent.astype(jnp.float32), normal_two, inverse_two, full_vectors[2]
    )
    grad_outer_bias = jnp.sum(grad_second, axis=0)
    grad_rows = lax.all_gather(grad_second.astype(jnp.bfloat16), "tensor", axis=0, tiled=True)
    grad_outer_w = jnp.einsum("tf,td->fd", hidden, grad_rows, preferred_element_type=jnp.float32)
    grad_hidden = jnp.einsum("td,fd->tf", grad_rows, outer_low, preferred_element_type=jnp.float32)
    grad_inner = gelu_pull(grad_hidden)[0].astype(jnp.bfloat16)
    grad_inner_bias = jnp.sum(grad_inner, axis=0, dtype=jnp.float32)
    grad_inner_w = jnp.einsum(
        "td,tf->df", normed_low, grad_inner, preferred_element_type=jnp.float32
    )
    piece = grad_inner
    grad_normed = grad_second + lax.psum_scatter(
        jnp.einsum("tf,df->td", piece, inner_low, preferred_element_type=jnp.float32).astype(
            jnp.bfloat16
        ),
        "tensor",
        scatter_dimension=0,
        tiled=True,
    ).astype(jnp.float32)
    grad_branch, grad_gain_one, grad_shift_one = norm_backward(
        grad_normed, normal_one, inverse_one, full_vectors[0]
    )
    grad_out_bias = jnp.sum(grad_branch, axis=0)
    branch_rows = lax.all_gather(grad_branch.astype(jnp.bfloat16), "tensor", axis=0, tiled=True)
    grad_out_w = jnp.einsum(
        "tc,td->cd", attn_mixed, branch_rows, preferred_element_type=jnp.float32
    )
    grad_mixed = jnp.einsum(
        "td,cd->tc", branch_rows, out_low, preferred_element_type=jnp.float32
    ).astype(jnp.bfloat16)
    grad_mixed = grad_mixed.reshape(seq_count, seq_length, head_cols // HD, HD)
    grad_query, grad_key, grad_value = lax.map(
        attend_backward,
        (split_heads[0], split_heads[1], split_heads[2], segments, log_total, grad_mixed),
    )
    grad_proj = jnp.stack([grad_query, grad_key, grad_value]).reshape(3, token_count, head_cols)
    grad_qkv_w = jnp.einsum(
        "td,ktc->kdc", every_token, grad_proj, preferred_element_type=jnp.float32
    )
    grad_head_bias = jnp.sum(grad_proj, axis=1, dtype=jnp.float32)
    piece = grad_proj
    input_grad = grad_branch + lax.psum_scatter(
        jnp.einsum("ktc,kdc->td", piece, qkv_low, preferred_element_type=jnp.float32).astype(
            jnp.bfloat16
        ),
        "tensor",
        scatter_dimension=0,
        tiled=True,
    ).astype(jnp.float32)
    inner_sum, outer_sum = reduce_ffn(grad_inner_w, grad_outer_w)
    qkv_sum, out_sum = (
        lax.psum_scatter(grad_qkv_w, "dp", scatter_dimension=1, tiled=True),
        lax.psum_scatter(grad_out_w, "dp", scatter_dimension=1, tiled=True),
    )
    row_grads = jnp.stack(
        [
            grad_gain_one,
            grad_shift_one,
            grad_gain_two,
            grad_shift_two,
            grad_out_bias,
            grad_outer_bias,
        ]
    )
    head_full = lax.dynamic_update_slice(
        jnp.zeros((2, width), jnp.float32),
        jnp.stack([grad_head_bias[0], grad_head_bias[2]]),
        (zero_index, tensor_index * head_cols),
    )
    inner_full = lax.dynamic_update_slice(
        jnp.zeros((full_vectors.shape[0] - 8) * width, jnp.float32),
        grad_inner_bias,
        (tensor_index * hidden_cols,),
    ).reshape(-1, width)
    vector_grad = jnp.concatenate([row_grads, head_full, inner_full], axis=0)
    vector_sum = lax.psum_scatter(vector_grad, ("dp", "tensor"), scatter_dimension=1, tiled=True)
    params = (qkv_weight, out_weight, inner_weight, outer_weight, vectors)
    grad_sums = (qkv_sum, out_sum, inner_sum, outer_sum, vector_sum)
    old_means = (qkv_mean, out_mean, inner_mean, outer_mean, vector_mean)
    old_squares = (qkv_square, out_square, inner_square, outer_square, vector_square)
    decays = (WEIGHT_DECAY, WEIGHT_DECAY, WEIGHT_DECAY, WEIGHT_DECAY, 0.0)
    adam_stats = [
        adam_direction(grad_sums[index], old_means[index], old_squares[index]) for index in range(5)
    ]
    updates = [adam_stats[index][2] + decays[index] * params[index] for index in range(5)]
    weight_squares, update_squares = lax.psum(
        (group_squares(*params), group_squares(*updates)), ("dp", "tensor")
    )
    weight_norms = jnp.sqrt(weight_squares)
    update_norms = jnp.sqrt(update_squares)
    trust_ratio = weight_norms / (update_norms + ADAM_EPS)
    new_weights = lamb_apply(params, updates, trust_ratio, vectors.shape[0])
    return (
        result.astype(jnp.bfloat16),
        input_grad,
        adam_stats[0][0],
        adam_stats[0][1],
        new_weights[0],
        adam_stats[1][0],
        adam_stats[1][1],
        new_weights[1],
        adam_stats[2][0],
        adam_stats[2][1],
        new_weights[2],
        adam_stats[3][0],
        adam_stats[3][1],
        new_weights[3],
        adam_stats[4][0],
        adam_stats[4][1],
        new_weights[4],
        jnp.stack([weight_norms, update_norms]),
    )


def solution(mesh):
    return jax.shard_map(
        body,
        mesh=mesh,
        in_specs=(
            P(("dp", "tensor"), None),
            P(("dp", "tensor"), None),
            P("dp", None),
            P(None, "dp", "tensor"),
            P("tensor", "dp"),
            P("dp", "tensor"),
            P("tensor", "dp"),
            P(None, ("dp", "tensor")),
            P(None, "dp", "tensor"),
            P("tensor", "dp"),
            P("dp", "tensor"),
            P("tensor", "dp"),
            P(None, ("dp", "tensor")),
            P(None, "dp", "tensor"),
            P("tensor", "dp"),
            P("dp", "tensor"),
            P("tensor", "dp"),
            P(None, ("dp", "tensor")),
        ),
        out_specs=(
            P(("dp", "tensor"), None),
            P(("dp", "tensor"), None),
            P(None, "dp", "tensor"),
            P(None, "dp", "tensor"),
            P(None, "dp", "tensor"),
            P("tensor", "dp"),
            P("tensor", "dp"),
            P("tensor", "dp"),
            P("dp", "tensor"),
            P("dp", "tensor"),
            P("dp", "tensor"),
            P("tensor", "dp"),
            P("tensor", "dp"),
            P("tensor", "dp"),
            P(None, ("dp", "tensor")),
            P(None, ("dp", "tensor")),
            P(None, ("dp", "tensor")),
            P(),
        ),
        check_vma=False,
    )
```

profile of v0, /device:TPU:0, one launch (start us, length us, event | category | flops | bytes accessed | tf_op | source)
XLA Modules:
  0.0 950.1 jit_solution(7194563906851807931)
XLA Ops:
  8.8 44.9 %all-gather = f32[32,24,12]{1,2,0:T(8,128)S(1)} all-gather(f32[1,24,12]{1,2,0:T(8,128)} %bitcast.233), channel_id=1, replica_groups=mesh['dp'=8,'tensor'=4] {'dp','tensor'}, dimensions={0}, use_global_device_ids=true | all-gather | bytes 38016 | tf_op jit(solution)/shard_map/all_gather | solution.py:153
  56.1 31.1 %all_gather.30 = bf16[192,768]{0,1:T(8,128)(2,1)S(1)} all-gather(bf16[192,96]{0,1:T(8,128)(2,1)S(1)} %copy.122), channel_id=1, replica_groups=mesh['dp'=8,'tensor'=4] {'dp'}, dimensions={1}, use_global_device_ids=true | all-gather | bytes 331776 | tf_op jit(solution)/shard_map/all_gather | solution.py:149
  87.3 36.0 %all_gather.27 = bf16[3,768,192]{2,0,1:T(4,128)(2,1)S(1)} all-gather(bf16[3,96,192]{2,0,1:T(4,128)(2,1)S(1)} %copy.115), channel_id=1, replica_groups=mesh['dp'=8,'tensor'=4] {'dp'}, dimensions={1}, use_global_device_ids=true | all-gather | bytes 995328 | tf_op jit(solution)/shard_map/all_gather | solution.py:148
  123.3 10.3 %fusion.66 = bf16[3,4096,192]{1,2,0:T(8,128)(2,1)S(1)} fusion(bf16[4096,768]{1,0:T(8,128)(2,1)} %all-gather.8.cloned.1.call-done, f32[3,192]{1,0:T(4,128)S(1)} %pad_maximum_fusion, bf16[3,768,192]{2,0,1:T(4,128)(2,1)S(1)} %all_gather.27), kind=kOutput, calls=%fused_computation.90 | convolution fusion | flops 3628597248 | bytes 11897088 | tf_op jit(solution)/shard_map/td,kdc->ktc/dot_general | solution.py:166
  140.2 45.7 %while.26 = (s32[]{:T(128)}, bf16[8,512,3,64]{1,3,2,0:T(8,128)(2,1)}, f32[8,3,512,1]{2,1,3,0:T(4,128)}, bf16[8,512,3,64]{1,3,2,0:T(8,128)(2,1)}, s32[8,512]{1,0:...) while((s32[]{:T(128)}, ...), condition=%wide.region_3.4_spmd, body=%wide.region_0.3_spmd.sunk | while | flops 211122688 | bytes 11332185 | solution.py:170
  143.3 2.7 fusion.147
  149.0 2.7 fusion.147
  154.7 2.7 fusion.147
  160.4 2.7 fusion.147
  166.1 2.7 fusion.147
  171.9 2.7 fusion.147
  177.6 2.7 fusion.147
  183.3 2.7 fusion.147
  186.0 3.4 copy.121
  191.3 4.6 convolution_convert_fusion
  197.6 55.3 %reduce-scatter.14.cloned.1.call-done = bf16[1024,768]{1,0:T(8,128)(2,1)} async-done(((bf16[4096,768]{1,0:T(8,128)(2,1)}), bf16[1024,768]{1,0:T(8,128)(2,1)}) %reduce-scatter.14.cloned.1.call-update) | async-done | bytes 1572880 | tf_op jit(solution)/shard_map/reduce_scatter | solution.py:175
  258.9 45.4 %all-gather.10.cloned.1.call-done = bf16[4096,768]{1,0:T(8,128)(2,1)} async-done(((bf16[1024,768]{1,0:T(8,128)(2,1)}), bf16[4096,768]{1,0:T(8,128)(2,1)}) %all-gather.10.cloned.1.call-update) | async-done | bytes 6291472 | tf_op jit(solution)/shard_map/all_gather | solution.py:184
  304.3 34.8 %multiply_convert_fusion.1 = (bf16[4096,768]{1,0:T(8,128)(2,1)}, f32[4096,768]{1,0:T(8,128)}, f32[4096,768]{1,0:T(8,128)}) fusion(f32[768]{0:T(1024)S(1)} %dynamic_slice.40, bf16[4096,768]{1,0:T(8,128)(2,1)} %all-gather.10.cloned.1.call-done, bf16[768,768]{1,0:T(8,128)(2,1)} %all-gather.12.cloned.1.call-done), kind=kOutput, calls=%fused_computation.67 | convolution fusion | flops 5039456256 | bytes 38931456 | tf_op jit(solution)/shard_map/dot_general | solution.py:185
  339.1 9.6 %all-gather.14.cloned.1.call-done = bf16[768,768]{0,1:T(8,128)(2,1)} async-done(((bf16[768,96]{0,1:T(8,128)(2,1)}), bf16[768,768]{0,1:T(8,128)(2,1)}) %all-gather.14.cloned.1.call-update) | async-done | bytes 1179664 | tf_op jit(solution)/shard_map/all_gather | solution.py:151
  348.7 9.2 convolution_convert_fusion.2
  358.4 56.3 %reduce-scatter.16.cloned.1.call-done = bf16[1024,768]{1,0:T(8,128)(2,1)} async-done(((bf16[4096,768]{1,0:T(8,128)(2,1)}), bf16[1024,768]{1,0:T(8,128)(2,1)}) %reduce-scatter.16.cloned.1.call-update) | async-done | bytes 1572880 | tf_op jit(solution)/shard_map/reduce_scatter | solution.py:191
  414.7 2.9 fusion.99
  419.1 2.3 fusion.75
  421.4 3.3 fusion.97
  424.8 46.5 %all-gather.16.cloned.1.call-done = bf16[4096,768]{1,0:T(8,128)(2,1)} async-done(((bf16[1024,768]{1,0:T(8,128)(2,1)}), bf16[4096,768]{1,0:T(8,128)(2,1)}) %all-gather.16.cloned.1.call-update) | async-done | bytes 6291472 | tf_op jit(solution)/shard_map/all_gather | solution.py:204
  471.3 18.5 %convert_reduce_fusion = (f32[768]{0:T(1024)S(1)}, bf16[4096,768]{1,0:T(8,128)(2,1)}) fusion(f32[4096,768]{1,0:T(8,128)} %get-tuple-element.333, f32[4096,768]{1,0:T(8,128)} %get-tuple-element.355, f32[768]{0:T(1024)S(1)} %dynamic_slice.40, bf16[4096,768]{1,0:T(8,128)(2,1)} %all-gather.16.cloned.1.call-done, bf16[768,768]{0,1:T(8,128)(2,1)} %all-gather.14.cloned.1.call-done), kind=kOutput, calls=%fused_computation.65 | convolution fusion | flops 4885314560 | bytes 38934528 | tf_op jit(solution)/shard_map/td,fd->tf/dot_general | solution.py:206
  489.8 9.7 %convolution_convert_fusion.1 = bf16[4096,768]{1,0:T(8,128)(2,1)} fusion(bf16[4096,768]{1,0:T(8,128)(2,1)} %get-tuple-element.316, bf16[768,768]{1,0:T(8,128)(2,1)S(1)} %copy-done.43), kind=kOutput, calls=%fused_computation.84 | convolution fusion | flops 4834983936 | bytes 13762560 | tf_op jit(solution)/shard_map/tf,df->td/dot_general | solution.py:214
  499.6 58.3 %reduce-scatter.18.cloned.1.call-done = bf16[1024,768]{1,0:T(8,128)(2,1)} async-done(((bf16[4096,768]{1,0:T(8,128)(2,1)}), bf16[1024,768]{1,0:T(8,128)(2,1)}) %reduce-scatter.18.cloned.1.call-update) | async-done | bytes 1572880 | tf_op jit(solution)/shard_map/reduce_scatter | solution.py:213
  557.9 4.6 multiply_reduce_fusion.1
  562.5 2.3 fusion.92
  568.0 10.1 %fusion.105 = f32[768,768]{0,1:T(8,128)} fusion(bf16[4096,768]{1,0:T(8,128)(2,1)} %get-tuple-element.332, bf16[4096,768]{1,0:T(8,128)(2,1)} %all-gather.16.cloned.1.call-done), kind=kOutput, calls=%fused_computation.195 | convolution fusion | flops 4831838208 | bytes 14942208 | tf_op jit(solution)/shard_map/tf,td->fd/dot_general | solution.py:205
  578.2 10.3 %fusion.104 = f32[768,768]{1,0:T(8,128)} fusion(bf16[4096,768]{1,0:T(8,128)(2,1)} %all-gather.10.cloned.1.call-done, bf16[4096,768]{1,0:T(8,128)(2,1)} %get-tuple-element.316), kind=kOutput, calls=%fused_computation.194 | convolution fusion | flops 4831838208 | bytes 14942208 | tf_op jit(solution)/shard_map/td,tf->df/dot_general | solution.py:209
  588.5 25.8 %all-gather.18.cloned.1.call-done = bf16[4096,768]{1,0:T(8,128)(2,1)} async-done(((bf16[1024,768]{1,0:T(8,128)(2,1)}), bf16[4096,768]{1,0:T(8,128)(2,1)}) %all-gather.18.cloned.1.call-update) | async-done | bytes 6291472 | tf_op jit(solution)/shard_map/all_gather | solution.py:225
  614.3 5.0 convolution_convert_fusion.3
  623.4 88.7 %while.27 = (s32[]{:T(128)}, bf16[8,512,3,64]{1,3,2,0:T(8,128)(2,1)S(1)}, bf16[8,512,3,64]{1,3,2,0:T(8,128)(2,1)}, bf16[8,512,3,64]{1,3,2,0:T(8,128)(2,1)}, bf16...) while((s32[]{:T(128)}, ...), condition=%wide.region_17.18_spmd, body=%wide.region_15.17_spmd.sunk | while | flops 511146496 | bytes 26125428 | solution.py:233
  629.8 2.2 fusion.158
  640.8 2.2 fusion.158
  651.9 2.2 fusion.158
  663.0 2.2 fusion.158
  671.0 2.2 multiply_reduce_fusion.17
  674.0 2.2 fusion.158
  682.1 2.2 multiply_reduce_fusion.17
  685.1 2.2 fusion.158
  696.2 2.2 fusion.158
  707.2 2.2 fusion.158
  714.1 3.7 stack.46
  719.8 2.6 stack.47
  722.4 3.4 copy.129
  725.8 3.9 stack.48
  729.7 2.7 constant_dynamic-update-slice_fusion.2
  732.4 6.2 convolution_bitcast_fusion
  741.6 9.2 fusion.78
  750.8 3.0 copy.142
  753.8 2.8 reshape.208
  756.7 9.3 bitcast_convert_fusion
  768.6 2.6 multiply_reduce_fusion.9
  771.3 2.7 multiply_reduce_fusion.10
  774.0 3.1 convert_reduce_fusion.1
  777.3 40.0 %all-reduce.1 = f32[12,768]{1,0:T(8,128)S(1)} all-reduce(f32[12,768]{1,0:T(8,128)S(1)} %concatenate.14), channel_id=10, replica_groups=mesh['dp'=8,'tensor'=4] {'dp','tensor'}, use_global_device_ids=true, to_apply=%region_42.43.clone | all-reduce | flops 9216 | bytes 73728
  821.8 3.2 concatenate.13
  825.0 45.9 %reduce-scatter.26.cloned.1.call-done = f32[96,576]{1,0:T(8,128)} async-done(((f32[768,576]{1,0:T(8,128)}), f32[96,576]{1,0:T(8,128)}) %reduce-scatter.26.cloned.1.call-update) | async-done | bytes 221200
  873.7 4.1 concatenate.15
  877.7 40.2 %all-reduce.2 = (f32[15]{0:T(128)}, f32[15]{0:T(128)}) all-reduce(f32[15]{0:T(128)} %concatenate.15, f32[15]{0:T(128)} %concatenate.13), channel_id=1, replica_groups=mesh['dp'=8,'tensor'=4] {'dp','tensor'}, use_global_device_ids=true, to_apply=%region_45.46 | all-reduce | flops 30 | bytes 240 | tf_op jit(solution)/shard_map/psum | solution.py:287
  939.2 3.4 convert_add_fusion
  (311 shorter events, 155.1 us)
Async XLA Ops:
  8.0 47.8 %copy-start.22 = (f32[192,96]{1,0:T(8,128)S(1)}, f32[192,96]{1,0:T(8,128)}, u32[]{:S(2)}) copy-start(f32[192,96]{1,0:T(8,128)} %param.26) | copy-start | bytes 221188
  8.0 115.3 %all-gather.8.cloned.1.call-start = ((), (), s32[]{:S(2)}) async-start(), calls=%async_computation.8 | async-start | bytes 7864320 | tf_op jit(solution)/shard_map/all_gather | solution.py:163
  8.8 244.1 %reduce-scatter.14.cloned.1.call-start = ((), (), s32[]{:S(2)}) async-start(), calls=%async_computation.9 | async-start | bytes 7864320 | tf_op jit(solution)/shard_map/reduce_scatter | solution.py:175
  54.0 33.2 %copy-start.30 = (f32[768,12]{0,1:T(8,128)}, f32[768,12]{0,1:T(8,128)S(1)}, u32[]{:S(2)}) copy-start(f32[768,12]{0,1:T(8,128)S(1)} %reshape.205) | copy-start | bytes 110596
  87.2 102.9 %copy-start.13 = (bf16[192,768]{0,1:T(8,128)(2,1)}, bf16[192,768]{0,1:T(8,128)(2,1)S(1)}, u32[]{:S(2)}) copy-start(bf16[192,768]{0,1:T(8,128)(2,1)S(1)} %all_gather.30) | copy-start | bytes 884740
  123.3 10.4 %copy-start.20 = (bf16[3,768,192]{2,0,1:T(4,128)(2,1)}, bf16[3,768,192]{2,0,1:T(4,128)(2,1)S(1)}, u32[]{:S(2)}) copy-start(bf16[3,768,192]{2,0,1:T(4,128)(2,1)S(1)} %all_gather.27) | copy-start | bytes 2654212
  186.0 4.1 copy-start.5
  186.0 4.1 copy-start.6
  190.1 1.2 copy-start.7
  195.8 1.0 copy-start.17
  195.8 1.7 copy-start.31
  195.8 57.1 %copy-start = (bf16[1024,768]{1,0:T(8,128)(2,1)S(1)}, bf16[1024,768]{1,0:T(8,128)(2,1)}, u32[]{:S(2)}) copy-start(bf16[1024,768]{1,0:T(8,128)(2,1)} %param.22) | copy-start | bytes 4718596
  195.8 63.0 %all-gather.12.cloned.1.call-start = ((), (), s32[]{:S(2)}) async-start(), calls=%async_computation.11 | async-start | bytes 1327104 | tf_op jit(solution)/shard_map/all_gather | solution.py:150
  197.5 106.8 %all-gather.10.cloned.1.call-start = ((), (), s32[]{:S(2)}) async-start(), calls=%async_computation.10 | async-start | bytes 7864320 | tf_op jit(solution)/shard_map/all_gather | solution.py:184
  252.9 2.1 copy-start.1
  255.9 2.1 copy-start.15
  258.0 90.8 %all-gather.14.cloned.1.call-start = ((), (), s32[]{:S(2)}) async-start(), calls=%async_computation.12 | async-start | bytes 1327104 | tf_op jit(solution)/shard_map/all_gather | solution.py:151
  258.7 156.0 %reduce-scatter.16.cloned.1.call-start = ((), (), s32[]{:S(2)}) async-start(), calls=%async_computation.13 | async-start | bytes 7864320 | tf_op jit(solution)/shard_map/reduce_scatter | solution.py:191
  357.9 113.4 %all-gather.16.cloned.1.call-start = ((), (), s32[]{:S(2)}) async-start(), calls=%async_computation.14 | async-start | bytes 7864320 | tf_op jit(solution)/shard_map/all_gather | solution.py:204
  417.7 1.4 copy-start.9
  424.8 133.1 %reduce-scatter.18.cloned.1.call-start = ((), (), s32[]{:S(2)}) async-start(), calls=%async_computation.15 | async-start | bytes 7864320 | tf_op jit(solution)/shard_map/reduce_scatter | solution.py:213
  471.3 18.5 %copy-start.43 = (bf16[768,768]{1,0:T(8,128)(2,1)S(1)}, bf16[768,768]{1,0:T(8,128)(2,1)}, u32[]{:S(2)}) copy-start(bf16[768,768]{1,0:T(8,128)(2,1)} %all-gather.12.cloned.1.call-done) | copy-start | bytes 3538948
  499.6 114.8 %all-gather.18.cloned.1.call-start = ((), (), s32[]{:S(2)}) async-start(), calls=%async_computation.16 | async-start | bytes 7864320 | tf_op jit(solution)/shard_map/all_gather | solution.py:225
  557.9 4.6 copy-start.2
  557.9 4.6 copy-start.12
  564.8 1.7 copy-start.3
  567.8 200.8 %reduce-scatter.24.cloned.1.call-start = ((), (), s32[]{:S(2)}) async-start(), calls=%async_computation.19 | async-start | bytes 2654208 | tf_op jit(solution)/shard_map/reduce_scatter | solution.py:123
  578.2 193.1 %reduce-scatter.22.cloned.1.call-start = ((), (), s32[]{:S(2)}) async-start(), calls=%async_computation.18 | async-start | bytes 2654208 | tf_op jit(solution)/shard_map/reduce_scatter | solution.py:122
  578.2 36.1 %copy-start.14 = (bf16[192,768]{0,1:T(8,128)(2,1)S(1)}, bf16[192,768]{0,1:T(8,128)(2,1)}, u32[]{:S(2)}) copy-start(bf16[192,768]{0,1:T(8,128)(2,1)} %copy-done.13) | copy-start | bytes 884740
  588.5 230.9 %reduce-scatter.28.cloned.1.call-start = ((), (), s32[]{:S(2)}) async-start(), calls=%async_computation.21 | async-start | bytes 884736
  712.0 5.8 copy-start.11
  725.8 6.6 copy-start.8
  738.6 1.7 copy-start.10
  738.7 132.2 %reduce-scatter.26.cloned.1.call-start = ((), (), s32[]{:S(2)}) async-start(), calls=%async_computation.20 | async-start | bytes 2211840
  756.6 182.6 %reduce-scatter.20.cloned.1.call-start = ((), (), s32[]{:S(2)}) async-start(), calls=%async_computation.17 | async-start | bytes 7864320 | tf_op jit(solution)/shard_map/reduce_scatter | solution.py:243
  766.0 1.0 copy-start.21
  766.0 1.1 copy-start.24
  766.0 1.3 copy-start.25
  766.0 1.4 copy-start.32
  766.0 2.2 copy-start.38
  766.0 2.2 copy-start.37
  766.1 2.5 copy-start.16
  766.1 2.5 copy-start.26
  766.1 2.5 copy-start.27
  766.1 5.1 copy-start.18
  766.1 5.1 copy-start.28
  766.1 5.1 copy-start.29
  766.2 7.8 copy-start.36
  766.2 7.8 copy-start.35
  767.1 105.0 %copy-start.19 = (f32[3,96,192]{1,2,0:T(8,128)}, f32[3,96,192]{1,2,0:T(8,128)S(1)}, u32[]{:S(2)}) copy-start(f32[3,96,192]{1,2,0:T(8,128)S(1)} %copy.134) | copy-start | bytes 663556
  771.2 46.2 %copy-start.40 = (f32[12,24]{1,0:T(8,128)S(1)}, f32[12,24]{1,0:T(8,128)}, u32[]{:S(2)}) copy-start(f32[12,24]{1,0:T(8,128)} %param.34) | copy-start | bytes 3460
  771.2 46.2 %copy-start.41 = (f32[12,24]{1,0:T(8,128)S(1)}, f32[12,24]{1,0:T(8,128)}, u32[]{:S(2)}) copy-start(f32[12,24]{1,0:T(8,128)} %param.39) | copy-start | bytes 3460
  771.2 49.2 %copy-start.23 = (f32[192,96]{1,0:T(8,128)S(1)}, f32[192,96]{1,0:T(8,128)}, u32[]{:S(2)}) copy-start(f32[192,96]{1,0:T(8,128)} %param.26) | copy-start | bytes 221188
  771.2 49.2 %copy-start.33 = (f32[192,96]{1,0:T(8,128)S(1)}, f32[192,96]{1,0:T(8,128)}, u32[]{:S(2)}) copy-start(f32[192,96]{1,0:T(8,128)} %param.31) | copy-start | bytes 221188
  771.2 49.2 %copy-start.34 = (f32[192,96]{1,0:T(8,128)S(1)}, f32[192,96]{1,0:T(8,128)}, u32[]{:S(2)}) copy-start(f32[192,96]{1,0:T(8,128)} %param.36) | copy-start | bytes 221188
  774.0 47.8 %copy-start.42 = (f32[3]{0:T(128)S(1)}, f32[3]{0:T(128)}, u32[]{:S(2)}) copy-start(f32[3]{0:T(128)} %get-tuple-element.342) | copy-start | bytes 40
  873.7 65.5 %copy-start.4 = (f32[1024,768]{1,0:T(8,128)S(1)}, f32[1024,768]{1,0:T(8,128)}, u32[]{:S(2)}) copy-start(f32[1024,768]{1,0:T(8,128)} %copy-done.3) | copy-start | bytes 9437188
  919.2 0.6 copy-start.39
Sparse Core Ops, SparseCore 0:
  10.4 50.6 all-gather.7
  196.0 56.8 reduce-scatter.13
  424.9 46.3 all-gather.15
  567.9 46.3 all-gather.17
Sparse Core Ops, SparseCore 1:
  199.1 40.0 all-gather.11
  258.0 46.2 all-gather.9
  307.2 41.5 all-gather.13
  358.0 56.7 reduce-scatter.15
  499.6 58.2 reduce-scatter.17
  578.2 69.1 reduce-scatter.23
  651.2 67.9 reduce-scatter.21
  738.7 62.7 reduce-scatter.27
  804.9 65.9 reduce-scatter.25
  873.5 58.1 reduce-scatter.19
where the time goes:
time: 963 us; the launch traced here: 950 us
  waiting for transfers between devices  344 us (36%)
  matrix products  233 us (24%)
  blocking collectives  192 us (20%)
  local copies, waits for them, and re-layouts  84 us (9%)
  other arithmetic  75.9 us (8%)
  between operations  18.4 us (2%)
    reduce_scatter x1, waiting for transfers between devices, body(): lax.psum_scatter(jnp.einsum('tf,df->td', piece, inner_low, preferred_elem...  58.3 us
    reduce_scatter x1, waiting for transfers between devices, body(): lax.psum_scatter(jnp.dot(piece, outer_low, preferred_element_type=jnp.flo...  56.3 us
    reduce_scatter x1, waiting for transfers between devices, body(): lax.psum_scatter(jnp.dot(piece, out_low, preferred_element_type=jnp.float...  55.3 us
    unnamed x16, waiting for transfers between devices  46.8 us
    all_gather x1, waiting for transfers between devices, body(): lax.all_gather(grad_second.astype(jnp.bfloat16), 'tensor', axis=0, tiled=...  46.5 us
    all_gather x1, waiting for transfers between devices, body(): lax.all_gather(normed.astype(jnp.bfloat16), 'tensor', axis=0, tiled=True)  45.4 us
    all_gather x1, blocking collectives, body(): full_vectors = lax.all_gather(vectors, ('dp', 'tensor'), axis=1, tiled=True)  44.9 us
    psum x1, blocking collectives, body(): lax.psum((group_squares(*params), group_squares(*updates)), ('dp', 'tenso...  40.2 us
  transfers between devices with their start and end apart: 14, of which 8 were waited for; matrix products, arithmetic and copies ran while one was open for 27% of the time, Pallas kernels for 0%

commit v1 on v0

v1 whole, which is shorter than its diff:
```python
import functools

import jax
import jax.numpy as jnp
from jax import lax
from jax.experimental import pallas as pl
from jax.experimental.pallas import tpu as pltpu
from jax.sharding import PartitionSpec as P

HD = 64
STEP = 5
NORM_EPS = 1e-05
ADAM_EPS = 1e-06
MOMENT_DECAY = 0.5
LEARN_RATE = 0.5
WEIGHT_DECAY = 0.01
MASKED = -1e30
SCALE = HD ** (-0.5)
F32 = jnp.float32
BF16 = jnp.bfloat16
NT = (((1,), (1,)), ((), ()))
NN = (((1,), (0,)), ((), ()))
TN = (((0,), (0,)), ((), ()))
VMEM_LIMIT = 60 * 1024 * 1024


def dot(a, b, dims=NN):
    return lax.dot_general(a, b, dims, preferred_element_type=F32)


def params(**kw):
    return pltpu.CompilerParams(vmem_limit_bytes=VMEM_LIMIT, **kw)


HEADS = 3
DOCS = 4
LANES = 768
Q_AT, K_AT, V_AT, O_AT = (0, 64, 384), (128, 192, 640), (256, 320, 448), (512, 576, 704)
Q_TILE, K_TILE, V_TILE = (0, 0, 3), (1, 1, 5), (2, 2, 3)
UPPER = (False, True, False)
V_UPPER = (False, True, True)


def spread(q, k, v, o):
    parts = {}
    for places, values in ((Q_AT, q), (K_AT, k), (V_AT, v), (O_AT, o)):
        for h, at in enumerate(places):
            parts[at] = values[:, h * HD : (h + 1) * HD]
    return jnp.concatenate([parts[at] for at in sorted(parts)], axis=1)


def collect(values, places):
    return jnp.concatenate([values[:, at : at + HD] for at in places], axis=1)


def tile_of(ref, n, rows=slice(None)):
    return ref[rows, n * 128 : (n + 1) * 128]


def is_low(shape):
    return lax.broadcasted_iota(jnp.int32, shape, 1) < HD


def halves(low, high):
    return jnp.where(is_low(low.shape), low, high)


def document_lanes(row):
    length = row.shape[1]
    number = jnp.broadcast_to(row.astype(F32), (128, length)).T
    lane = lax.broadcasted_iota(jnp.int32, (length, 128), 1) % HD
    same = number == lane.astype(F32)
    for_query = jnp.where(same, 1.0, 0.0).astype(BF16)
    for_key = jnp.where(same, 0.0, jnp.where(lane < DOCS, MASKED, 0.0)).astype(BF16)
    return for_query, for_key


def attend_heads(pm_ref, row, lse_ref, chunk):
    length = pm_ref.shape[0]
    chunks = length // chunk
    doc_q, doc_k = document_lanes(row)
    ones = jnp.ones((16, length), BF16)
    units = [(h, c) for h in range(HEADS) for c in range(chunks)]
    keys, queries, values = {}, {}, {}
    for h in range(HEADS):
        q, k = tile_of(pm_ref, Q_TILE[h]) * SCALE, tile_of(pm_ref, K_TILE[h])
        queries[h] = halves(doc_q, q) if UPPER[h] else halves(q, doc_q)
        keys[h] = halves(doc_k, k) if UPPER[h] else halves(k, doc_k)
        vt = tile_of(pm_ref, V_TILE[h]).T
        vt = vt[HD:] if V_UPPER[h] else vt[:HD]
        values[h] = jnp.concatenate([vt, ones], axis=0)

    def scores(unit):
        h, c = unit
        return dot(keys[h], queries[h][c * chunk : (c + 1) * chunk], NT)

    outs = {h: [] for h in range(HEADS)}
    ahead = scores(units[0])
    for n, (h, c) in enumerate(units):
        s = ahead
        if n + 1 < len(units):
            ahead = scores(units[n + 1])
        m = jnp.max(s, axis=0, keepdims=True)
        p = jnp.exp(s - m).astype(BF16)
        ot = dot(values[h], p)
        total = ot[HD : HD + 1]
        outs[h].append((ot[:HD] * (1.0 / total)).astype(BF16))
        lse_ref[0, 0, h : h + 1, c * chunk : (c + 1) * chunk] = m + jnp.log(total)
    out = [jnp.concatenate(outs[h], axis=1) for h in range(HEADS)]
    pm_ref[:, 512:640] = jnp.concatenate([out[0], out[1]], axis=0).T
    last = jnp.concatenate([jnp.zeros_like(out[2]), out[2]], axis=0).T
    pm_ref[:, 640:768] = halves(tile_of(pm_ref, 5), last)


def attend_fwd_kernel(x_ref, w_ref, bias_ref, seg_ref, pm_ref, lse_ref, *, chunk):
    proj = dot(x_ref[...], w_ref[0]) + bias_ref[0, 0:1, :]
    pm_ref[0] = proj.astype(BF16)
    attend_heads(pm_ref.at[0], seg_ref[0, 0:1], lse_ref, chunk)


def attend_fwd(x, wa, bias, seg, length):
    tokens, width = x.shape
    groups, _, lanes = wa.shape
    seqs = tokens // length
    return pl.pallas_call(
        functools.partial(attend_fwd_kernel, chunk=min(256, length)),
        grid=(groups, seqs),
        in_specs=[
            pl.BlockSpec((length, width), lambda t, s: (s, 0)),
            pl.BlockSpec((1, width, lanes), lambda t, s: (t, 0, 0)),
            pl.BlockSpec((1, 8, lanes), lambda t, s: (t, 0, 0)),
            pl.BlockSpec((1, 8, length), lambda t, s: (s, 0, 0)),
        ],
        out_specs=[
            pl.BlockSpec((1, length, lanes), lambda t, s: (t, s, 0)),
            pl.BlockSpec((1, 1, 8, length), lambda t, s: (t, s, 0, 0)),
        ],
        out_shape=[
            jax.ShapeDtypeStruct((groups, tokens, lanes), BF16),
            jax.ShapeDtypeStruct((groups, seqs, 8, length), F32),
        ],
        compiler_params=params(),
        name="attend_fwd",
    )(x, wa, bias, seg)


def attend_back(pm_ref, gm_ref, lse_ref, row, gp_ref, chunk):
    length = pm_ref.shape[0]
    chunks = length // chunk
    prod = gm_ref[...].astype(F32) * pm_ref[:, 512:768].astype(F32)
    hi = prod.astype(BF16)
    lo = (prod - hi.astype(F32)).astype(BF16)
    lane = lax.broadcasted_iota(jnp.int32, (8, 256), 1)
    line = lax.broadcasted_iota(jnp.int32, (8, 256), 0)
    start = jnp.where(line == 2, O_AT[2] - 512, line * HD)
    pick = jnp.where((lane >= start) & (lane < start + HD) & (line < HEADS), 1.0, 0.0).astype(BF16)
    dsum = dot(pick, hi, NT) + dot(pick, lo, NT)
    doc_q, doc_k = document_lanes(row)
    none = jnp.zeros((length, 128), BF16)
    units = [(h, c) for h in range(HEADS) for c in range(chunks)]
    keys, queries, plain, values, kts, grads = {}, {}, {}, {}, {}, {}
    for h in range(HEADS):
        q, k = tile_of(pm_ref, Q_TILE[h]) * SCALE, tile_of(pm_ref, K_TILE[h])
        plain[h] = q
        queries[h] = halves(doc_q, q) if UPPER[h] else halves(q, doc_q)
        keys[h] = halves(doc_k, k) if UPPER[h] else halves(k, doc_k)
        kt = k.T
        kts[h] = kt[HD:] if UPPER[h] else kt[:HD]
        v = tile_of(pm_ref, V_TILE[h])
        values[h] = halves(none, v) if V_UPPER[h] else halves(v, none)
        grads[h] = tile_of(gm_ref, 0 if h < 2 else 1)

    def rows_of(c):
        return slice(c * chunk, (c + 1) * chunk)

    def products(unit):
        h, c = unit
        return dot(keys[h], queries[h][rows_of(c)], NT), dot(values[h], grads[h][rows_of(c)], NT)

    dqs = {h: [] for h in range(HEADS)}
    dks, dvs = {}, {}
    ahead = products(units[0])
    for n, (h, c) in enumerate(units):
        s, dp = ahead
        if n + 1 < len(units):
            ahead = products(units[n + 1])
        rows = rows_of(c)
        p = jnp.exp(s - lse_ref[0, 0, h : h + 1, rows])
        ds = (p * (dp - dsum[h : h + 1, rows])).astype(BF16)
        dv = dot(p.astype(BF16), grads[h][rows])
        dk = dot(ds, plain[h][rows])
        dvs[h] = dv if c == 0 else dvs[h] + dv
        dks[h] = dk if c == 0 else dks[h] + dk
        dqs[h].append((dot(kts[h], ds) * SCALE).astype(BF16))
    dq = [jnp.concatenate(dqs[h], axis=1) for h in range(HEADS)]
    gp_ref[:, 0:128] = jnp.concatenate([dq[0], dq[1]], axis=0).T
    gp_ref[:, 128:256] = halves(dks[0], dks[1]).astype(BF16)
    gp_ref[:, 256:384] = halves(dvs[0], dvs[1]).astype(BF16)
    last = jnp.concatenate([dq[2], jnp.zeros_like(dq[2])], axis=0).T
    gp_ref[:, 384:512] = halves(last, dvs[2].astype(BF16))
    gp_ref[:, 512:640] = tile_of(pm_ref, 4)
    gp_ref[:, 640:768] = halves(dks[2].astype(BF16), tile_of(pm_ref, 5))


def attend_bwd_kernel(pm_ref, gm_ref, lse_ref, seg_ref, gp_ref, gsum_ref, *, chunk):
    attend_back(pm_ref.at[0], gm_ref.at[0], lse_ref, seg_ref[0, 0:1], gp_ref.at[0], chunk)

    @pl.when(pl.program_id(1) == 0)
    def _():
        gsum_ref[...] = jnp.zeros_like(gsum_ref)

    gsum_ref[0, 0:1, :] += jnp.sum(gp_ref[0].astype(F32), axis=0, keepdims=True)


def attend_bwd(pm, gm, lse, seg):
    groups, tokens, lanes = pm.shape
    seqs, length = lse.shape[1], lse.shape[3]
    return pl.pallas_call(
        functools.partial(attend_bwd_kernel, chunk=min(256, length)),
        grid=(groups, seqs),
        in_specs=[
            pl.BlockSpec((1, length, lanes), lambda t, s: (t, s, 0)),
            pl.BlockSpec((1, length, gm.shape[2]), lambda t, s: (t, s, 0)),
            pl.BlockSpec((1, 1, 8, length), lambda t, s: (t, s, 0, 0)),
            pl.BlockSpec((1, 8, length), lambda t, s: (s, 0, 0)),
        ],
        out_specs=[
            pl.BlockSpec((1, length, lanes), lambda t, s: (t, s, 0)),
            pl.BlockSpec((1, 8, lanes), lambda t, s: (t, 0, 0)),
        ],
        out_shape=[
            jax.ShapeDtypeStruct((groups, tokens, lanes), BF16),
            jax.ShapeDtypeStruct((groups, 8, lanes), F32),
        ],
        compiler_params=params(),
        name="attend_bwd",
    )(pm, gm, lse, seg)


def mixed_only(tail):
    lane = lax.broadcasted_iota(jnp.int32, tail.shape, 1)
    return jnp.where((lane < 128) | (lane >= 192), tail, jnp.zeros((), BF16))


def gelu_parts(pre):
    cdf = 0.5 * (1.0 + lax.erf(pre * (2.0**-0.5)))
    pdf = jnp.exp(-0.5 * pre * pre) * 0.3989422804014327
    return pre * cdf, cdf + pre * pdf


def mean_of(values):
    return jnp.mean(values, axis=-1, keepdims=True)


def norm_parts(values):
    centred = values - mean_of(values)
    inverse = lax.rsqrt(mean_of(centred * centred) + NORM_EPS)
    return centred * inverse, inverse


def norm_back(incoming, normal, inverse, gain):
    scaled = incoming * gain
    return inverse * (scaled - mean_of(scaled) - normal * mean_of(scaled * normal))


def ffn_kernel(
    x_ref, cot_ref, pm_ref, wo_ref, wb_ref, wc_ref, vec_ref, bias_ref,
    out_ref, hid_ref, gi_ref, nl_ref, gsl_ref, gbl_ref, gb_ref, gm_ref, vg_ref, bg_ref,
    slope_ref,
):
    groups = wb_ref.shape[0]

    @pl.when(pl.program_id(0) == 0)
    def _():
        vg_ref[...] = jnp.zeros_like(vg_ref)
        bg_ref[...] = jnp.zeros_like(bg_ref)

    total = x_ref[...].astype(F32) + vec_ref[4:5, :]
    for t in range(groups):
        total = total + dot(mixed_only(pm_ref[t]), wo_ref[t], NT)
    normal_one, inverse_one = norm_parts(total)
    normed = normal_one * vec_ref[0:1, :] + vec_ref[1:2, :]
    low = normed.astype(BF16)
    nl_ref[...] = low
    second = normed + vec_ref[5:6, :]
    for t in range(groups):
        pre = dot(low, wb_ref[t]) + bias_ref[t : t + 1, :]
        act, slope = gelu_parts(pre)
        act = act.astype(BF16)
        hid_ref[t] = act
        slope_ref[t] = slope
        second = second + dot(act, wc_ref[t], NT)
    normal_two, inverse_two = norm_parts(second)
    out_ref[...] = (normal_two * vec_ref[2:3, :] + vec_ref[3:4, :]).astype(BF16)
    cot = cot_ref[...].astype(F32)
    grad_second = norm_back(cot, normal_two, inverse_two, vec_ref[2:3, :])
    vg_ref[2:3, :] += jnp.sum(cot * normal_two, axis=0, keepdims=True)
    vg_ref[3:4, :] += jnp.sum(cot, axis=0, keepdims=True)
    vg_ref[5:6, :] += jnp.sum(grad_second, axis=0, keepdims=True)
    gs_low = grad_second.astype(BF16)
    gsl_ref[...] = gs_low
    grad_normed = grad_second
    for t in range(groups):
        grad_inner = (dot(gs_low, wc_ref[t]) * slope_ref[t]).astype(BF16)
        gi_ref[t] = grad_inner
        bg_ref[t : t + 1, :] += jnp.sum(grad_inner.astype(F32), axis=0, keepdims=True)
        grad_normed = grad_normed + dot(grad_inner, wb_ref[t], NT)
    grad_branch = norm_back(grad_normed, normal_one, inverse_one, vec_ref[0:1, :])
    vg_ref[0:1, :] += jnp.sum(grad_normed * normal_one, axis=0, keepdims=True)
    vg_ref[1:2, :] += jnp.sum(grad_normed, axis=0, keepdims=True)
    vg_ref[4:5, :] += jnp.sum(grad_branch, axis=0, keepdims=True)
    gb_ref[...] = grad_branch
    gb_low = grad_branch.astype(BF16)
    gbl_ref[...] = gb_low
    for t in range(groups):
        gm_ref[t] = dot(gb_low, wo_ref[t]).astype(BF16)


def ffn(x, cot, pm, wa, wb, wc, vec, bias):
    tokens, width = x.shape
    groups, _, lanes = wa.shape
    hidden = wb.shape[2]
    tail = 256
    tile = 256
    last = lanes // tail - 1
    once = pl.Buffered(1)
    row = pl.BlockSpec((tile, width), lambda i: (i, 0))
    wide = pl.BlockSpec((groups, tile, hidden), lambda i: (0, i, 0))
    return pl.pallas_call(
        ffn_kernel,
        grid=(tokens // tile,),
        in_specs=[
            row,
            row,
            pl.BlockSpec((groups, tile, tail), lambda i: (0, i, last)),
            pl.BlockSpec((groups, width, tail), lambda i: (0, 0, last), pipeline_mode=once),
            pl.BlockSpec((groups, width, hidden), lambda i: (0, 0, 0), pipeline_mode=once),
            pl.BlockSpec((groups, width, hidden), lambda i: (0, 0, 0), pipeline_mode=once),
            pl.BlockSpec(vec.shape, lambda i: (0, 0)),
            pl.BlockSpec(bias.shape, lambda i: (0, 0)),
        ],
        out_specs=[
            row,
            wide,
            wide,
            row,
            row,
            row,
            row,
            pl.BlockSpec((groups, tile, tail), lambda i: (0, i, 0)),
            pl.BlockSpec((8, width), lambda i: (0, 0)),
            pl.BlockSpec((8, hidden), lambda i: (0, 0)),
        ],
        out_shape=[
            jax.ShapeDtypeStruct((tokens, width), BF16),
            jax.ShapeDtypeStruct((groups, tokens, hidden), BF16),
            jax.ShapeDtypeStruct((groups, tokens, hidden), BF16),
            jax.ShapeDtypeStruct((tokens, width), BF16),
            jax.ShapeDtypeStruct((tokens, width), BF16),
            jax.ShapeDtypeStruct((tokens, width), BF16),
            jax.ShapeDtypeStruct((tokens, width), F32),
            jax.ShapeDtypeStruct((groups, tokens, tail), BF16),
            jax.ShapeDtypeStruct((8, width), F32),
            jax.ShapeDtypeStruct((8, hidden), F32),
        ],
        scratch_shapes=[pltpu.VMEM((groups, tile, hidden), F32)],
        compiler_params=params(),
        name="ffn",
    )(x, cot, pm, wa, wb, wc, vec, bias)


MESH = pl.DeviceIdType.MESH


class Place:
    def __init__(self, sizes):
        dp, tensor = lax.axis_index("dp"), lax.axis_index("tensor")
        self.deep = sizes[0] // 2
        self.z, self.y = dp // 2, dp % 2
        self.x, self.c = tensor // 2, tensor % 2

    def to_z(self, step):
        return {"dp": lax.rem(self.z + step, self.deep) * 2 + self.y}

    def to_y(self):
        return {"dp": self.z * 2 + 1 - self.y}

    def to_x(self):
        return {"tensor": (1 - self.x) * 2 + self.c}

    def to_c(self):
        return {"tensor": self.x * 2 + 1 - self.c}

    def from_z(self, step):
        return lax.rem(self.z + self.deep - step, self.deep)

    def partners(self):
        return [self.to_z(j) for j in range(1, self.deep)] + [self.to_y(), self.to_x(), self.to_c()]

    def peers(self):
        found = []
        for r in range(1, 8):
            x = 1 - self.x if r & 4 else self.x
            y = 1 - self.y if r & 2 else self.y
            c = 1 - self.c if r & 1 else self.c
            found.append((x * 4 + y * 2 + c, {"dp": self.z * 2 + y, "tensor": x * 2 + c}))
        return found

    def greet(self, everyone=False):
        barrier = pltpu.get_barrier_semaphore()
        partners = self.partners()
        if everyone:
            partners = partners[: self.deep - 1] + [device for _, device in self.peers()]
        for partner in partners:
            pl.semaphore_signal(barrier, inc=1, device_id=partner, device_id_type=MESH)
        pl.semaphore_wait(barrier, len(partners))


class Links:
    def __init__(self, send, recv):
        self.send, self.recv = send, recv

    def copy(self, k, ref, to, dst=None):
        return pltpu.make_async_remote_copy(
            src_ref=ref,
            dst_ref=ref if dst is None else dst,
            send_sem=self.send.at[k],
            recv_sem=self.recv.at[k],
            device_id=to,
            device_id_type=MESH,
        )

    def landed(self, k, ref, to):
        self.copy(k, ref, to).wait_recv()


def add_everywhere(place, links, base, own, slots):
    deep = place.deep
    hops = [place.to_c(), place.to_y(), place.to_x()]

    def start(i):
        def run():
            if i:
                links.copy(base + i - 1, own, hops[i - 1], slots.at[i - 1]).wait_send()
                links.landed(base + i - 1, slots.at[i - 1], hops[i - 1])
                own[...] = own[...] + slots[i - 1]
            if i < 3:
                links.copy(base + i, own, hops[i], slots.at[i]).start()
            else:
                for j in range(1, deep):
                    links.copy(base + 2 + j, own, place.to_z(j), slots.at[2 + j]).start()

        return run

    def last():
        for j in range(1, deep):
            links.copy(base + 2 + j, own, place.to_z(j), slots.at[2 + j]).wait_send()
            links.landed(base + 2 + j, slots.at[2 + j], place.to_z(j))
        slots[2] = own[...]
        total = slots[2 + lax.rem(place.z + deep, deep)]
        for z in range(1, deep):
            total = total + slots[2 + lax.rem(place.z + deep - z, deep)]
        own[...] = total

    return [start(0), start(1), start(2), start(3), last]


def add_in_two(place, links, base, own, slots):
    p, deep = place, place.deep
    me = p.x * 4 + p.y * 2 + p.c
    peers = p.peers()

    def near(r):
        return links.copy(base + r, own, peers[r - 1][1], slots.at[me])

    def far(j):
        return links.copy(base + 7 + j, own, p.to_z(j), slots.at[8 + p.z])

    def start():
        for r in range(1, 8):
            near(r).start()
        slots[me] = own[...]

    def middle():
        for r in range(1, 8):
            near(r).wait_send()
            links.landed(base + r, slots.at[peers[r - 1][0]], peers[r - 1][1])
        total = slots[0]
        for k in range(1, 8):
            total = total + slots[k]
        own[...] = total
        for j in range(1, deep):
            far(j).start()
        slots[8 + p.z] = total

    def last():
        for j in range(1, deep):
            far(j).wait_send()
            links.landed(base + 7 + j, slots.at[8 + p.from_z(j)], p.to_z(j))
        total = slots[8]
        for k in range(1, deep):
            total = total + slots[8 + k]
        own[...] = total

    return [start, middle, last]


def gather_small(place, links, base, whole):
    p, deep = place, place.deep
    mine, line, plane = whole.at[p.x, p.c, p.z, p.y], whole.at[p.x, p.c, :, p.y], whole.at[p.x, p.c]
    half = whole.at[:, p.c]

    def over_z(j):
        return links.copy(base + j, mine, p.to_z(j))

    def stage0():
        for j in range(1, deep):
            over_z(j).start()

    def stage1():
        for j in range(1, deep):
            links.landed(base + j, whole.at[p.x, p.c, p.from_z(j), p.y], p.to_z(j))
        links.copy(base + deep, line, p.to_y()).start()

    def stage2():
        links.landed(base + deep, whole.at[p.x, p.c, :, 1 - p.y], p.to_y())
        links.copy(base + deep + 1, plane, p.to_x()).start()

    def stage3():
        links.landed(base + deep + 1, whole.at[1 - p.x, p.c], p.to_x())
        links.copy(base + deep + 2, half, p.to_c()).start()

    def stage4():
        links.landed(base + deep + 2, whole.at[:, 1 - p.c], p.to_c())
        for j in range(1, deep):
            over_z(j).wait_send()
        links.copy(base + deep, line, p.to_y()).wait_send()
        links.copy(base + deep + 1, plane, p.to_x()).wait_send()
        links.copy(base + deep + 2, half, p.to_c()).wait_send()

    return [stage0, stage1, stage2, stage3, stage4]


def gather_stages(place, links, base, own, whole, start=0, count=None):
    p, deep = place, place.deep
    count = own.shape[0] if count is None else count
    half = count // 2
    rows, first, later = pl.ds(start, count), pl.ds(start, half), pl.ds(start + half, half)
    own = own.at[rows]
    mine = whole.at[p.x, p.c, p.z, p.y, rows]
    line = whole.at[p.x, p.c, :, p.y, rows]
    ax = whole.at[p.x, p.c, :, p.y, first]
    ax_in = whole.at[1 - p.x, p.c, :, p.y, first]
    by = whole.at[p.x, p.c, :, p.y, later]
    by_in = whole.at[p.x, p.c, :, 1 - p.y, later]
    ay = whole.at[:, p.c, :, p.y, first]
    ay_in = whole.at[:, p.c, :, 1 - p.y, first]
    bx = whole.at[p.x, p.c, :, :, later]
    bx_in = whole.at[1 - p.x, p.c, :, :, later]
    kz, ka, kb, ks = base, base + deep, base + deep + 2, base + deep + 4

    def keep():
        return pltpu.make_async_copy(own, mine, links.send.at[kz])

    def stage0():
        keep().start()
        for j in range(1, deep):
            links.copy(kz + j, own, p.to_z(j), mine).start()

    def sent():
        for j in range(1, deep):
            links.copy(kz + j, own, p.to_z(j), mine).wait_send()

    def stage1():
        keep().wait()
        for j in range(1, deep):
            links.landed(kz + j, whole.at[p.x, p.c, p.from_z(j), p.y, rows], p.to_z(j))
        links.copy(ka, ax, p.to_x()).start()
        links.copy(kb, by, p.to_y()).start()
        links.copy(ks, line, p.to_c()).start()

    def stage2():
        links.landed(ka, ax_in, p.to_x())
        links.copy(ka + 1, ay, p.to_y()).start()
        links.copy(ks + 1, ax_in, p.to_c()).start()
        links.landed(kb, by_in, p.to_y())
        links.copy(kb + 1, bx, p.to_x()).start()
        links.copy(ks + 2, by_in, p.to_c()).start()

    def stage3():
        links.landed(ka + 1, ay_in, p.to_y())
        links.copy(ks + 3, ay_in, p.to_c()).start()
        links.landed(kb + 1, bx_in, p.to_x())
        links.copy(ks + 4, bx_in, p.to_c()).start()

    def stage4():
        o = 1 - p.c
        links.landed(ks, whole.at[p.x, o, :, p.y, rows], p.to_c())
        links.landed(ks + 1, whole.at[1 - p.x, o, :, p.y, first], p.to_c())
        links.landed(ks + 2, whole.at[p.x, o, :, 1 - p.y, later], p.to_c())
        links.landed(ks + 3, whole.at[:, o, :, 1 - p.y, first], p.to_c())
        links.landed(ks + 4, whole.at[1 - p.x, o, :, :, later], p.to_c())
        links.copy(ka, ax, p.to_x()).wait_send()
        links.copy(kb, by, p.to_y()).wait_send()
        links.copy(ka + 1, ay, p.to_y()).wait_send()
        links.copy(kb + 1, bx, p.to_x()).wait_send()
        links.copy(ks, line, p.to_c()).wait_send()
        links.copy(ks + 1, ax_in, p.to_c()).wait_send()
        links.copy(ks + 2, by_in, p.to_c()).wait_send()
        links.copy(ks + 3, ay_in, p.to_c()).wait_send()
        links.copy(ks + 4, bx_in, p.to_c()).wait_send()

    return [stage0, stage1, stage2, stage3, stage4, sent]


def gather_stages_late(place, links, base, own, whole, start=0, count=None):
    p, deep = place, place.deep
    count = own.shape[0] if count is None else count
    half = count // 2
    rows, first, later = pl.ds(start, count), pl.ds(start, half), pl.ds(start + half, half)
    mine = whole.at[p.x, p.c, p.z, p.y]
    pair_f, pair_l = whole.at[:, p.c, p.z, p.y, first], whole.at[p.x, p.c, p.z, :, later]
    line_f, line_l = whole.at[:, p.c, :, p.y, first], whole.at[p.x, p.c, :, :, later]
    line_f_in = whole.at[:, p.c, :, 1 - p.y, first]
    line_l_in = whole.at[1 - p.x, p.c, :, :, later]
    kf, kl = base + 8, base + 8 + deep

    def keep():
        return pltpu.make_async_copy(own.at[rows], mine.at[rows], links.send.at[base])

    def to_x():
        return links.copy(base + 1, own.at[first], p.to_x(), mine.at[first])

    def to_y():
        return links.copy(base + 2, own.at[later], p.to_y(), mine.at[later])

    def stage0():
        keep().start()
        to_x().start()
        to_y().start()

    def stage1():
        keep().wait()
        links.landed(base + 1, whole.at[1 - p.x, p.c, p.z, p.y, first], p.to_x())
        links.landed(base + 2, whole.at[p.x, p.c, p.z, 1 - p.y, later], p.to_y())
        for j in range(1, deep):
            links.copy(kf + j, pair_f, p.to_z(j)).start()
            links.copy(kl + j, pair_l, p.to_z(j)).start()

    def sent():
        for j in range(1, deep):
            links.copy(kf + j, pair_f, p.to_z(j)).wait_send()
            links.copy(kl + j, pair_l, p.to_z(j)).wait_send()

    def stage2():
        for j in range(1, deep):
            z = p.from_z(j)
            links.landed(kf + j, whole.at[:, p.c, z, p.y, first], p.to_z(j))
            links.landed(kl + j, whole.at[p.x, p.c, z, :, later], p.to_z(j))
        links.copy(base + 3, line_f, p.to_y()).start()
        links.copy(base + 4, line_l, p.to_x()).start()
        links.copy(base + 5, line_f, p.to_c()).start()
        links.copy(base + 6, line_l, p.to_c()).start()

    def stage3():
        links.landed(base + 3, line_f_in, p.to_y())
        links.copy(base + 7, line_f_in, p.to_c()).start()
        links.landed(base + 4, line_l_in, p.to_x())
        links.copy(base + 8, line_l_in, p.to_c()).start()

    def stage4():
        o = 1 - p.c
        links.landed(base + 5, whole.at[:, o, :, p.y, first], p.to_c())
        links.landed(base + 6, whole.at[p.x, o, :, :, later], p.to_c())
        links.landed(base + 7, whole.at[:, o, :, 1 - p.y, first], p.to_c())
        links.landed(base + 8, whole.at[1 - p.x, o, :, :, later], p.to_c())
        to_x().wait_send()
        to_y().wait_send()
        links.copy(base + 3, line_f, p.to_y()).wait_send()
        links.copy(base + 4, line_l, p.to_x()).wait_send()
        links.copy(base + 5, line_f, p.to_c()).wait_send()
        links.copy(base + 6, line_l, p.to_c()).wait_send()
        links.copy(base + 7, line_f_in, p.to_c()).wait_send()
        links.copy(base + 8, line_l_in, p.to_c()).wait_send()

    return [stage0, stage1, stage2, stage3, stage4, sent]


GATHER_COPIES = 9


def add_into(out, one, two):
    out[...] = one[...] + two[...]


def scatter_core(place, links, base, acc, in_c):
    def move(part):
        return links.copy(base + part, acc.at[2 + part], place.to_c(), in_c.at[part])

    def send(part):
        return lambda: move(part).start()

    def add(part, x):
        def run():
            move(part).wait_send()
            links.landed(base + part, in_c.at[part], place.to_c())

            def one(z, _):
                for y in range(2):
                    there = acc.at[x, z, y]
                    add_into(there, there, in_c.at[part, z, y])
                return 0

            lax.fori_loop(0, place.deep, one, 0)

        return run

    return send, add


def add_line(place, acc, x, y, rows, arrived):
    def add(z, _):
        there = acc.at[x, z, y, rows]
        add_into(there, there, arrived.at[z])
        return 0

    lax.fori_loop(0, place.deep, add, 0)


def scatter_plane(place, links, base, acc, ay_in, ax_in, bx_in, by_in):
    p = place
    half = acc.shape[3] // 2
    first, later, both = pl.ds(0, half), pl.ds(half, half), pl.ds(0, 2)

    def ay():
        return links.copy(base, acc.at[both, :, 1 - p.y, first], p.to_y(), ay_in)

    def bx():
        return links.copy(base + 1, acc.at[1 - p.x, :, :, later], p.to_x(), bx_in)

    def ax():
        return links.copy(base + 2, acc.at[1 - p.x, :, p.y, first], p.to_x(), ax_in)

    def by():
        return links.copy(base + 3, acc.at[p.x, :, 1 - p.y, later], p.to_y(), by_in)

    def start():
        ay().start()
        bx().start()

    def middle():
        links.landed(base, ay_in, p.to_y())
        for x in range(2):
            add_line(p, acc, x, p.y, first, ay_in.at[x])
        ax().start()
        links.landed(base + 1, bx_in, p.to_x())
        for y in range(2):
            add_line(p, acc, p.x, y, later, bx_in.at[:, y])
        by().start()

    def finish():
        links.landed(base + 2, ax_in, p.to_x())
        add_line(p, acc, p.x, p.y, first, ax_in)
        links.landed(base + 3, by_in, p.to_y())
        add_line(p, acc, p.x, p.y, later, by_in)

    def settle():
        for move in (ay, bx, ax, by):
            move().wait_send()

    return start, middle, finish, settle


def scatter_in_pairs(place, links, base, acc, in_c, ay_in, ax_in, bx_in, by_in, in_z, out):
    p, deep = place, place.deep
    half = acc.shape[3] // 2
    first, later = pl.ds(0, half), pl.ds(half, half)
    far, near = 1 - p.x, p.x
    kf, kl = base + 6, base + 6 + deep
    send, add = scatter_core(place, links, base, acc, in_c)

    def over_y(part, x):
        return links.copy(base + 2 + part, acc.at[x, :, 1 - p.y, first], p.to_y(), ay_in.at[part])

    def far_later():
        return links.copy(base + 4, acc.at[far, :, :, later], p.to_x(), bx_in)

    def far_first():
        return links.copy(base + 5, acc.at[far, :, p.y, first], p.to_x(), ax_in)

    def near_later():
        return links.copy(base + 6, acc.at[near, :, 1 - p.y, later], p.to_y(), by_in)

    def over_z(k, j, rows):
        to = lax.rem(p.z + j, deep)
        return links.copy(k + j, acc.at[near, to, p.y, rows], p.to_z(j), in_z.at[j, rows])

    def far1():
        add(0, far)()
        over_y(0, far).start()
        far_later().start()

    def far2():
        links.landed(base + 2, ay_in.at[0], p.to_y())
        add_line(p, acc, far, p.y, first, ay_in.at[0])
        far_first().start()

    def near1():
        over_y(1, near).start()

    def near_x():
        links.landed(base + 4, bx_in, p.to_x())
        for y in range(2):
            add_line(p, acc, near, y, later, bx_in.at[:, y])
        near_later().start()

    def near2():
        links.landed(base + 3, ay_in.at[1], p.to_y())
        add_line(p, acc, near, p.y, first, ay_in.at[1])
        links.landed(base + 5, ax_in, p.to_x())
        add_line(p, acc, near, p.y, first, ax_in)
        for j in range(1, deep):
            over_z(kf, j, first).start()

    def near3():
        links.landed(base + 6, by_in, p.to_y())
        add_line(p, acc, near, p.y, later, by_in)
        for j in range(1, deep):
            over_z(kl, j, later).start()

    def near4():
        for k, rows in ((kf, first), (kl, later)):
            total = acc[near, p.z, p.y, rows].astype(F32)
            for j in range(1, deep):
                links.landed(k + j, in_z.at[j, rows], p.to_z(j))
                total = total + in_z[j, rows].astype(F32)
            out[rows] = total
            for j in range(1, deep):
                over_z(k, j, rows).wait_send()
        over_y(0, far).wait_send()
        over_y(1, near).wait_send()
        far_later().wait_send()
        far_first().wait_send()
        near_later().wait_send()

    return [send(0), far1, far2, send(1), add(1, near), near1, near_x, near2, near3, near4]


def scatter_tail(place, links, base, part, in_z, out):
    deep = place.deep

    def send(j):
        return links.copy(
            base + j, part.at[lax.rem(place.z + j, deep)], place.to_z(j), in_z.at[j]
        )

    def stage0():
        for j in range(1, deep):
            send(j).start()

    def stage1():
        for j in range(1, deep):
            links.landed(base + j, in_z.at[j], place.to_z(j))
        total = part[place.z].astype(F32)
        for j in range(1, deep):
            total = total + in_z[j].astype(F32)
        out[...] = total
        for j in range(1, deep):
            send(j).wait_send()

    return [stage0, stage1]


def core_buffers(deep, rows, lanes):
    return [
        pltpu.VMEM((4, deep, 2, rows, lanes), BF16),
        pltpu.VMEM((2, deep, 2, rows, lanes), BF16),
    ]


def plane_buffers(deep, rows, lanes):
    half = rows // 2
    return [
        pltpu.VMEM((2, deep, half, lanes), BF16),
        pltpu.VMEM((deep, half, lanes), BF16),
        pltpu.VMEM((deep, 2, half, lanes), BF16),
        pltpu.VMEM((deep, half, lanes), BF16),
    ]


def gather_blocks(block, sizes):
    whole = lax.all_gather(block, ("dp", "tensor"), axis=0, tiled=False)
    whole = whole.reshape(sizes + block.shape)
    return jnp.swapaxes(whole, 0, 1).reshape((sizes[1], -1) + block.shape[1:])


def scatter_blocks(grads, sizes):
    parts = grads.reshape((sizes[1], sizes[0], -1) + grads.shape[2:])
    parts = jnp.swapaxes(parts, 0, 1).reshape((sizes[0] * sizes[1],) + parts.shape[2:])
    return lax.psum_scatter(parts, ("dp", "tensor"), scatter_dimension=0, tiled=False)


def adam_parts(grad, mean, square):
    new_mean = MOMENT_DECAY * mean + (1.0 - MOMENT_DECAY) * grad
    new_square = MOMENT_DECAY * square + (1.0 - MOMENT_DECAY) * grad * grad
    correction = 1.0 - MOMENT_DECAY**STEP
    direction = new_mean / correction / (jnp.sqrt(new_square / correction) + ADAM_EPS)
    return new_mean, new_square, direction


def sum_all(values):
    return jnp.sum(jnp.sum(values, axis=1, keepdims=True), axis=0, keepdims=True)


def group_squares(qkv_part, out_part, inner_part, outer_part, vector_part):
    return jnp.concatenate(
        [
            jnp.sum(qkv_part * qkv_part, axis=(1, 2)),
            jnp.sum(out_part * out_part)[None],
            jnp.sum(inner_part * inner_part)[None],
            jnp.sum(outer_part * outer_part)[None],
            jnp.sum(vector_part[:8] * vector_part[:8], axis=1),
            jnp.sum(vector_part[8:] * vector_part[8:])[None],
        ]
    )


def lamb_apply(weight_list, update_list, trust_ratio, row_number):
    qkv_new = weight_list[0] - LEARN_RATE * trust_ratio[0:3, None, None] * update_list[0]
    out_new = weight_list[1] - LEARN_RATE * trust_ratio[3] * update_list[1]
    inner_new = weight_list[2] - LEARN_RATE * trust_ratio[4] * update_list[2]
    outer_new = weight_list[3] - LEARN_RATE * trust_ratio[5] * update_list[3]
    row_ratio = jnp.concatenate(
        [trust_ratio[6:14], jnp.broadcast_to(trust_ratio[14], (row_number - 8,))]
    )
    vector_new = weight_list[4] - LEARN_RATE * row_ratio[:, None] * update_list[4]
    return (qkv_new, out_new, inner_new, outer_new, vector_new)


def lamb_plain(sum_a, sum_b, sum_c, vector_sum, weights, old_means, old_squares):
    qkv_sum = jnp.stack([collect(sum_a, at) for at in (Q_AT, K_AT, V_AT)])
    grad_sums = (qkv_sum, collect(sum_a, O_AT).T, sum_b, sum_c.T, vector_sum)
    decays = (WEIGHT_DECAY, WEIGHT_DECAY, WEIGHT_DECAY, WEIGHT_DECAY, 0.0)
    stats = [adam_parts(*entry) for entry in zip(grad_sums, old_means, old_squares)]
    updates = [stats[i][2] + decays[i] * weights[i] for i in range(5)]
    weight_squares, update_squares = lax.psum(
        (group_squares(*weights), group_squares(*updates)), ("dp", "tensor")
    )
    weight_norms = jnp.sqrt(weight_squares)
    update_norms = jnp.sqrt(update_squares)
    trust_ratio = weight_norms / (update_norms + ADAM_EPS)
    new = lamb_apply(weights, updates, trust_ratio, weights[4].shape[0])
    outs = []
    for i in range(5):
        outs += [stats[i][0], stats[i][1], new[i]]
    return outs + [jnp.stack([weight_norms, update_norms])]


A_ROWS = ((0, 32), (32, 32), (64, 32))
B_ROWS = ((0, 64), (64, 32))


def gather_attend_kernel(
    qkv_ref, out_ref, inner_ref, outer_ref, vec_ref, x_ref, seg_ref,
    wa_hbm, wb_hbm, wc_hbm, full, pm_ref, lse_ref, hid_ref, slope_ref, nlt_ref, xt_ref, n1_ref,
    inv_ref,
    send, recv, slots, pack_a, pack_b, pack_c, wa, wb, wc, bias, low, out_sem,
    *, sizes, chunk,
):
    step = pl.program_id(0)
    groups, deep = sizes[1], sizes[0] // 2
    place = Place(sizes)
    links = Links(send, recv)
    each = GATHER_COPIES + deep
    cols = qkv_ref.shape[2]
    tokens, width = x_ref.shape
    lanes = pack_a.shape[1]
    length = tokens // 2
    tail = 256
    ga = [
        gather_stages(place, links, k * each, pack_a, wa, *rows) for k, rows in enumerate(A_ROWS)
    ]
    more = len(A_ROWS) * each
    gb = [
        gather_stages(place, links, more + k * each, pack_b, wb, *rows)
        for k, rows in enumerate(B_ROWS)
    ]
    more += len(B_ROWS) * each
    small = gather_small(place, links, more, slots)
    more += deep + 3
    gc = [
        gather_stages_late(place, links, more + k * (each + deep), pack_c, wc, *rows)
        for k, rows in enumerate(B_ROWS)
    ]
    sent = 5
    t, s = step // 2, step % 2
    last = 2 * groups + groups - 1

    def keep(k):
        pairs = ((wa, wa_hbm), (wb, wb_hbm), (wc, wc_hbm))
        return pltpu.make_async_copy(*pairs[k], out_sem.at[k])

    @pl.when(step == 0)
    def _():
        out_rows = out_ref[...].T
        pack_a[...] = spread(qkv_ref[0], qkv_ref[1], qkv_ref[2], out_rows).astype(BF16)
        count, mine = vec_ref.shape
        slots[place.x, place.c, place.z, place.y, 0:count, 0:mine] = vec_ref[...]
        place.greet()
        small[0]()
        ga[0][0]()
        pack_c[...] = outer_ref[...].astype(BF16)
        gc[0][0]()
        gc[1][0]()
        ga[0][sent]()
        ga[1][0]()
        small[1]()
        ga[0][1]()
        ga[1][sent]()
        ga[2][0]()
        pack_b[...] = inner_ref[...].astype(BF16)
        small[2]()
        ga[1][1]()
        ga[0][2]()
        ga[2][sent]()
        gb[0][0]()
        small[3]()
        ga[2][1]()
        ga[1][2]()
        ga[0][3]()
        xt_ref[...] = x_ref[...].T
        ga[2][2]()
        gb[0][sent]()
        gb[1][0]()
        ga[1][3]()
        small[4]()
        full[...] = jnp.zeros_like(full)
        for k in range(sizes[0] * groups):
            dp, tensor = k // groups, k % groups
            block = slots[tensor // 2, tensor % 2, dp // 2, dp % 2, 0:count, 0:mine]
            full[0:count, k * mine : (k + 1) * mine] = block
        gb[1][sent]()
        gc[0][1]()
        gb[0][1]()
        ga[2][3]()
        for g in range(groups):
            bias[g] = jnp.zeros(bias.shape[1:], F32)
            for h in range(HEADS):
                here = slice(g * cols + h * HD, g * cols + (h + 1) * HD)
                bias[g, 0:1, Q_AT[h] : Q_AT[h] + HD] = full[6:7, here]
                bias[g, 0:1, V_AT[h] : V_AT[h] + HD] = full[7:8, here]
        n1_ref[...] = x_ref[...].astype(F32) + full[4:5, :]
        gb[1][1]()
        for piece in ga:
            piece[4]()
        keep(0).start()

    @pl.when(step == 1)
    def _():
        gb[0][2]()
        gb[1][2]()

    @pl.when(step == 3)
    def _():
        gc[0][sent]()
        gc[1][1]()

    @pl.when(step == 4)
    def _():
        gc[0][2]()

    @pl.when(step == 5)
    def _():
        gb[0][3]()

    @pl.when(step == 7)
    def _():
        gb[1][3]()
        gc[1][sent]()
        gc[1][2]()

    @pl.when(step == 2 * groups + 2)
    def _():
        gc[0][3]()
        keep(1).start()

    @pl.when((step < 2 * groups) & (s == 0))
    def _():
        weight = wa[t // 2, t % 2].reshape(width, lanes)
        for n in range(lanes // 256):
            here = slice(n * 256, (n + 1) * 256)
            proj = dot(x_ref[...], weight[:, here]) + bias[t, 0:1, here]
            pm_ref[0, :, here] = proj.astype(BF16)

    @pl.when(step < 2 * groups)
    def _():
        rows = pl.ds(pl.multiple_of(s * length, length), length)
        row = seg_ref[pl.ds(lax.axis_index("tensor") * 2 + s, 1)]
        attend_heads(pm_ref.at[0, rows], row, lse_ref, chunk)

    @pl.when((step < 2 * groups) & (s == 1))
    def _():
        mixed = mixed_only(pm_ref[0, :, lanes - tail :])
        weight = wa[t // 2, t % 2, :, :, :, lanes - tail :].reshape(width, tail)
        for n in range(width // 256):
            here = slice(n * 256, (n + 1) * 256)
            n1_ref[:, here] += dot(mixed, weight[here], NT)

    @pl.when(step == 2 * groups)
    def _():
        for r in range(tokens // 256):
            rows = slice(r * 256, (r + 1) * 256)
            normal_one, inverse_one = norm_parts(n1_ref[rows])
            n1_ref[rows] = normal_one
            inv_ref[rows] = inverse_one
            part = (normal_one * full[0:1, :] + full[1:2, :]).astype(BF16)
            low[rows] = part
            nlt_ref[:, rows] = part.T
        gb[0][4]()
        gb[1][4]()

    @pl.when(step >= 2 * groups)
    def _():
        g = step - 2 * groups
        weight = wb[g // 2, g % 2].reshape(width, lanes)
        for n in range(lanes // 256):
            here = slice(n * 256, (n + 1) * 256)
            pre = dot(low[...], weight[:, here]) + full[pl.ds(8 + g, 1), here]
            act, turn = gelu_parts(pre)
            hid_ref[0, :, here] = act.astype(BF16)
            slope_ref[0, :, here] = turn.astype(BF16)

    @pl.when(step == last)
    def _():
        gc[1][3]()
        gc[0][4]()
        gc[1][4]()
        keep(2).start()
        for k in range(3):
            keep(k).wait()


def once(shape):
    return pl.BlockSpec(shape, lambda *_: (0,) * len(shape), pipeline_mode=pl.Buffered(1))


def gather_attend(weights, x, seg, sizes):
    qkv, out, inner, outer, vec = weights
    deep, groups = sizes[0] // 2, sizes[1]
    each = GATHER_COPIES + deep
    copies = len(A_ROWS) * each + len(B_ROWS) * (2 * each + deep) + deep + 3
    tokens, width = x.shape
    length = seg.shape[1]
    seqs = tokens // length
    rows, lanes = inner.shape
    steps = groups * seqs
    anywhere = pl.BlockSpec(memory_space=pl.ANY)
    parts = (2, 2, deep, 2, rows, lanes)
    whole = jax.ShapeDtypeStruct(parts, BF16)

    def now(i):
        return jnp.minimum(i, steps - 1)

    def part(i):
        return jnp.clip(i - steps, 0, groups - 1)

    wa, wb, wc, *rest = pl.pallas_call(
        functools.partial(gather_attend_kernel, sizes=sizes, chunk=min(256, length)),
        grid=(steps + groups,),
        in_specs=[once(w.shape) for w in weights]
        + [
            once(x.shape),
            once(seg.shape),
        ],
        out_specs=[anywhere] * 3
        + [
            once((16, width)),
            pl.BlockSpec((1, tokens, lanes), lambda i: (now(i) // 2, 0, 0)),
            pl.BlockSpec((1, 1, 8, length), lambda i: (now(i) // 2, now(i) % 2, 0, 0)),
            pl.BlockSpec((1, tokens, lanes), lambda i: (part(i), 0, 0)),
            pl.BlockSpec((1, tokens, lanes), lambda i: (part(i), 0, 0)),
            once((width, tokens)),
            once((width, tokens)),
            once((tokens, width)),
            once((tokens, 1)),
        ],
        out_shape=[whole] * 3
        + [
            jax.ShapeDtypeStruct((16, width), F32),
            jax.ShapeDtypeStruct((groups, tokens, lanes), BF16),
            jax.ShapeDtypeStruct((groups, seqs, 8, length), F32),
            jax.ShapeDtypeStruct((groups, tokens, lanes), BF16),
            jax.ShapeDtypeStruct((groups, tokens, lanes), BF16),
            jax.ShapeDtypeStruct((width, tokens), BF16),
            jax.ShapeDtypeStruct((width, tokens), BF16),
            jax.ShapeDtypeStruct((tokens, width), F32),
            jax.ShapeDtypeStruct((tokens, 1), F32),
        ],
        scratch_shapes=[
            pltpu.SemaphoreType.DMA((copies,)),
            pltpu.SemaphoreType.DMA((copies,)),
            pltpu.VMEM((2, 2, deep, 2, 16, 128), F32),
            pltpu.VMEM((rows, lanes), BF16),
            pltpu.VMEM((rows, lanes), BF16),
            pltpu.VMEM((rows, lanes), BF16),
            pltpu.VMEM(parts, BF16),
            pltpu.VMEM(parts, BF16),
            pltpu.VMEM(parts, BF16),
            pltpu.VMEM((groups, 8, lanes), F32),
            pltpu.VMEM((tokens, width), BF16),
            pltpu.SemaphoreType.DMA((3,)),
        ],
        compiler_params=params(collective_id=0, has_side_effects=True),
        name="gather_attend",
    )(*weights, x, seg)
    shape = (groups, sizes[0] * rows, lanes)
    return [wa.reshape(shape), wb.reshape(shape), wc.reshape(shape)] + rest


def other_first(order):
    c = lax.axis_index("tensor") % 2
    return order % 2 * 2 + jnp.where(order < 2, 1 - c, c)


def layer_kernel(
    cot_ref, hid_ref, slope_ref, inv_ref, vec_ref, n1_hbm, nlt_hbm, wa_hbm, wb_hbm, wc_hbm,
    out_hbm, gb_hbm, gm_hbm, gbt_hbm, accb_hbm, part_ref, vg_ref, bg_ref,
    n1_ref, nlt_ref, wo_ref, wb_ref, wc_ref, acc, low, gst, gi, out_ref, gm_ref, gbt_ref,
    in_sem, out_sem, send, recv, accc, in_cc, accb, in_cb, ay_in, ax_in, bx_in, by_in, *, sizes,
):
    step = pl.program_id(0)
    tokens, width = acc.shape
    groups, deep = sizes[1], sizes[0] // 2
    lanes = wa_hbm.shape[2]
    tail = wo_ref.shape[2]
    last = 3 * groups - 1
    place = Place(sizes)
    links = Links(send, recv)
    send_c, add_c = scatter_core(place, links, 0, accc, in_cc)
    send_b, add_b = scatter_core(place, links, 2, accb, in_cb)
    start, middle, finish, settle = scatter_plane(
        place, links, 4, accc, ay_in, ax_in, bx_in, by_in
    )
    blocks = [slice(r * 256, (r + 1) * 256) for r in range(tokens // 256)]
    columns = [slice(n * 256, (n + 1) * 256) for n in range(width // 256)]

    def outer(t):
        return pltpu.make_async_copy(wc_hbm.at[t], wc_ref.at[t], in_sem.at[t])

    def inner(t):
        return pltpu.make_async_copy(wb_hbm.at[t], wb_ref.at[t], in_sem.at[groups + t])

    def load(k):
        pairs = (
            (n1_hbm, n1_ref), (nlt_hbm, nlt_ref), (wa_hbm.at[:, :, pl.ds(lanes - tail, tail)], wo_ref)
        )
        return pltpu.make_async_copy(*pairs[k], in_sem.at[2 * groups + k])

    def store(k):
        pairs = (
            (out_ref, out_hbm), (gbt_ref, gbt_hbm), (accb.at[pl.ds(0, 2)], accb_hbm), (acc, gb_hbm)
        )
        return pltpu.make_async_copy(*pairs[k], out_sem.at[k])

    def store_mixed(t):
        return pltpu.make_async_copy(gm_ref.at[t], gm_hbm.at[t], out_sem.at[4 + t])

    @pl.when(step == 0)
    def _():
        for t in range(groups):
            outer(t).start()
        load(0).start()
        for t in range(groups):
            inner(t).start()
        load(1).start()
        load(2).start()
        place.greet()
        vg_ref[...] = jnp.zeros_like(vg_ref)
        bg_ref[...] = jnp.zeros_like(bg_ref)
        acc[...] = jnp.zeros_like(acc)

    @pl.when(step < groups)
    def _():
        outer(step).wait()
        for here in columns:
            acc[:, here] += dot(hid_ref[0], wc_ref[step, here], NT)

    @pl.when(step == groups - 1)
    def _():
        load(0).wait()
        for rows in blocks:
            second = n1_ref[rows] * vec_ref[0:1, :] + vec_ref[1:2, :] + vec_ref[5:6, :]
            normal_two, inverse_two = norm_parts(second + acc[rows])
            out_ref[rows] = (normal_two * vec_ref[2:3, :] + vec_ref[3:4, :]).astype(BF16)
            cot = cot_ref[rows].astype(F32)
            grad_second = norm_back(cot, normal_two, inverse_two, vec_ref[2:3, :])
            vg_ref[2:3, :] += jnp.sum(cot * normal_two, axis=0, keepdims=True)
            vg_ref[3:4, :] += jnp.sum(cot, axis=0, keepdims=True)
            vg_ref[5:6, :] += jnp.sum(grad_second, axis=0, keepdims=True)
            acc[rows] = grad_second
            part = grad_second.astype(BF16)
            low[rows] = part
            gst[:, rows] = part.T
        store(0).start()

    @pl.when((step >= groups) & (step < 2 * groups))
    def _():
        slot = lax.rem(step - groups + 2, 4)
        for here in columns:
            part = dot(gst[...], hid_ref[0, :, here]).astype(BF16)
            accc[slot, :, :, :, here] = part.reshape(deep, 2, -1, 256)

    @pl.when(step == groups + 1)
    def _():
        send_c(0)()

    @pl.when(step == groups + 2)
    def _():
        send_c(1)()

    @pl.when(step == 2 * groups)
    def _():
        add_c(0, 0)()
        add_c(1, 1)()
        start()
        for t in range(groups):
            inner(t).wait()
        load(1).wait()
        load(2).wait()

    @pl.when(step == last)
    def _():
        middle()

    @pl.when(step >= 2 * groups)
    def _():
        order = step - 2 * groups
        slot = lax.rem(order + 2, 4)
        t = other_first(order)
        for here in columns:
            grad_hidden = dot(low[...], wc_ref[t, :, here])
            part = (grad_hidden * slope_ref[0, :, here].astype(F32)).astype(BF16)
            gi[:, here] = part
            bg_ref[pl.ds(t, 1), here] = jnp.sum(part.astype(F32), axis=0, keepdims=True)
        for here in columns:
            acc[:, here] += dot(gi[...], wb_ref[t, here], NT)
        for here in columns:
            part = dot(nlt_ref[...], gi[:, here]).astype(BF16)
            accb[slot, :, :, :, here] = part.reshape(deep, 2, -1, 256)

    @pl.when(step == 2 * groups + 1)
    def _():
        send_b(0)()

    @pl.when(step == 2 * groups + 2)
    def _():
        send_b(1)()

    @pl.when(step == last)
    def _():
        for rows in blocks:
            grad_normed = acc[rows]
            normal_one = n1_ref[rows]
            grad_branch = norm_back(grad_normed, normal_one, inv_ref[rows], vec_ref[0:1, :])
            vg_ref[0:1, :] += jnp.sum(grad_normed * normal_one, axis=0, keepdims=True)
            vg_ref[1:2, :] += jnp.sum(grad_normed, axis=0, keepdims=True)
            vg_ref[4:5, :] += jnp.sum(grad_branch, axis=0, keepdims=True)
            acc[rows] = grad_branch
            part = grad_branch.astype(BF16)
            low[rows] = part
            gbt_ref[:, rows] = part.T
        store(3).start()
        store(1).start()
        for t in range(groups):
            gm_ref[t] = dot(low[...], wo_ref[t]).astype(BF16)
            store_mixed(t).start()
        add_b(0, 0)()
        add_b(1, 1)()
        store(2).start()
        finish()
        part_ref[...] = accc[place.x, :, place.y]
        settle()
        for k in range(4):
            store(k).wait()
        for t in range(groups):
            store_mixed(t).wait()


def layer(cot, hid, slope, n1, inv1, nlt, wa, wb, wc, vec, sizes):
    tokens, width = cot.shape
    groups, _, lanes = wa.shape
    hidden = wb.shape[2]
    deep = sizes[0] // 2
    rows = width // sizes[0]
    tail = 256
    anywhere = pl.BlockSpec(memory_space=pl.ANY)

    def used(i):
        return jnp.where(i < groups, i, other_first(jnp.clip(i - groups, 0, groups - 1)))

    def back_group(i):
        return other_first(jnp.clip(i - 2 * groups, 0, groups - 1))

    copies = 8
    parts = (2, deep, 2, rows, hidden)
    matrix = pltpu.VMEM((groups, width, hidden), BF16)
    return pl.pallas_call(
        functools.partial(layer_kernel, sizes=sizes),
        grid=(3 * groups,),
        in_specs=[
            once(cot.shape),
            pl.BlockSpec((1, tokens, hidden), lambda i: (used(i), 0, 0)),
            pl.BlockSpec((1, tokens, hidden), lambda i: (back_group(i), 0, 0)),
            once(inv1.shape),
            once(vec.shape),
        ]
        + [anywhere] * 5,
        out_specs=[anywhere] * 5
        + [once((deep, rows, hidden)), once((8, width)), once((8, hidden))],
        out_shape=[
            jax.ShapeDtypeStruct((tokens, width), BF16),
            jax.ShapeDtypeStruct((tokens, width), F32),
            jax.ShapeDtypeStruct((groups, tokens, tail), BF16),
            jax.ShapeDtypeStruct((width, tokens), BF16),
            jax.ShapeDtypeStruct(parts, BF16),
            jax.ShapeDtypeStruct((deep, rows, hidden), BF16),
            jax.ShapeDtypeStruct((8, width), F32),
            jax.ShapeDtypeStruct((8, hidden), F32),
        ],
        scratch_shapes=[
            pltpu.VMEM(n1.shape, F32),
            pltpu.VMEM(nlt.shape, BF16),
            pltpu.VMEM((groups, width, tail), BF16),
            matrix,
            matrix,
            pltpu.VMEM((tokens, width), F32),
            pltpu.VMEM((tokens, width), BF16),
            pltpu.VMEM((width, tokens), BF16),
            pltpu.VMEM((tokens, hidden), BF16),
            pltpu.VMEM((tokens, width), BF16),
            pltpu.VMEM((groups, tokens, tail), BF16),
            pltpu.VMEM((width, tokens), BF16),
            pltpu.SemaphoreType.DMA((2 * groups + 3,)),
            pltpu.SemaphoreType.DMA((4 + groups,)),
            pltpu.SemaphoreType.DMA((copies,)),
            pltpu.SemaphoreType.DMA((copies,)),
        ]
        + core_buffers(deep, rows, hidden) * 2
        + plane_buffers(deep, rows, hidden),
        compiler_params=params(collective_id=1, has_side_effects=True),
        name="layer",
    )(cot, hid, slope, inv1, vec, n1, nlt, wa, wb, wc)


def far_first(step, groups):
    tensor = lax.axis_index("tensor")
    x, c = tensor // 2, tensor % 2
    return jnp.where(step < groups, 1 - x, x) * 2 + jnp.where(step % groups < 2, 1 - c, c)


def back_kernel(
    pm_ref, gm_ref, lse_ref, seg_ref, wa_hbm, xt_hbm, gbt_hbm, gb_hbm,
    accb_hbm, part_ref, vg_ref, bg_ref, *refs, sizes, chunk,
):
    weights, means, squares = refs[0:5], refs[5:10], refs[10:15]
    grads, updates, norms, ig_ref = refs[15:20], refs[20:25], refs[25], refs[26]
    gp, gsum, send, recv, slots, hslots, nslots, vec, hvec, load_sem, sa = refs[27:38]
    wa_ref, xt_ref, gbt_ref, gb_ref, accb, inz_b, inz_c = refs[38:45]
    bufs_b, bufs_a, acc = refs[45:49], refs[49:56], refs[49]
    sb, sc = grads[2], grads[3]
    step = pl.program_id(0)
    groups, deep = sizes[1], sizes[0] // 2
    cols = HEADS * HD
    tokens, width = gb_ref.shape
    lanes = pm_ref.shape[2]
    last = 2 * groups - 1
    length = pm_ref.shape[1]
    place = Place(sizes)
    links = Links(send, recv)
    a = scatter_in_pairs(place, links, 0, *bufs_a, sa)
    more = 7 + 2 * deep
    start, middle, finish, settle = scatter_plane(place, links, more, accb, *bufs_b)
    b = scatter_tail(place, links, more + 4, accb.at[place.x, :, place.y], inz_b, sb)
    c = scatter_tail(place, links, more + 4 + deep, part_ref, inz_c, sc)
    early = add_everywhere(place, links, more + 4 + 2 * deep, vec, slots)
    small = add_everywhere(place, links, more + 6 + 3 * deep, hvec, hslots)
    final = add_in_two(place, links, more + 8 + 4 * deep, norms, nslots)
    t, s = far_first(step, groups), step % 2

    def load(k):
        pairs = ((accb_hbm, accb), (xt_hbm, xt_ref), (gbt_hbm, gbt_ref), (wa_hbm, wa_ref), (gb_hbm, gb_ref))
        return pltpu.make_async_copy(*pairs[k], load_sem.at[k])

    @pl.when(step == 0)
    def _():
        load(0).start()
        place.greet(everyone=True)
        c[0]()
        load(0).wait()
        start()
        for k in range(1, 5):
            load(k).start()
        gsum[...] = jnp.zeros_like(gsum)
        vec[...] = jnp.zeros_like(vec)
        hvec[...] = jnp.zeros_like(hvec)
        vec[0:6] = vg_ref[0:6]
        vec[8 : 8 + groups] = bg_ref[0:groups]
        early[0]()

    @pl.when(step == 1)
    def _():
        load(1).wait()
        load(2).wait()

    @pl.when(step == 2)
    def _():
        a[0]()
        early[1]()

    @pl.when(step == 4)
    def _():
        early[2]()
        middle()
        a[1]()

    @pl.when(step == 5)
    def _():
        c[1]()

    @pl.when(step == 6)
    def _():
        a[3]()
        early[3]()

    @pl.when(step == 7)
    def _():
        finish()
        b[0]()

    rows = pl.ds(pl.multiple_of(s * length, length), length)
    row = seg_ref[pl.ds(lax.axis_index("tensor") * 2 + s, 1)]
    attend_back(pm_ref.at[0], gm_ref.at[0], lse_ref, row, gp.at[t, rows], chunk)
    gsum[t, 0:1, :] += jnp.sum(gp[t, rows].astype(F32), axis=0, keepdims=True)

    @pl.when(s == 1)
    def _():
        order = step // 2
        slot = jnp.where(order % 2 == 0, 2 + order // 2, t // 2)
        for n in range(lanes // 256):
            here = slice(n * 256, (n + 1) * 256)
            if n < lanes // 256 - 1:
                part = dot(xt_ref[...], gp[t, :, here])
            else:
                from_x = dot(xt_ref[...], gp[t, :, here])
                part = dot(gbt_ref[...], gp[t, :, here])
                lane = lax.broadcasted_iota(jnp.int32, part.shape, 1)
                part = jnp.where((lane >= 128) & (lane < 192), from_x, part)
            acc[slot, :, :, :, here] = part.astype(BF16).reshape(deep, 2, -1, 256)

    def input_columns(n):
        here = slice(n * 256, (n + 1) * 256)
        total = gb_ref[:, here]
        for g in range(groups):
            part = gp[g, :, 640:768]
            part = halves(part, jnp.zeros_like(part))
            total = total + dot(gp[g, :, 0:512], wa_ref[g, here, 0:512], NT)
            total = total + dot(part, wa_ref[g, here, 640:768], NT)
        ig_ref[:, here] = total

    @pl.when(step == last)
    def _():
        for g in range(groups):
            for h in range(HEADS):
                at = g * cols + h * HD
                line, lane = at // 256, slice(at % 256, at % 256 + HD)
                hvec[line : line + 1, lane] = gsum[g, 0:1, Q_AT[h] : Q_AT[h] + HD]
                hvec[3 + line : 4 + line, lane] = gsum[g, 0:1, V_AT[h] : V_AT[h] + HD]
        small[0]()
        a[4]()
        a[5]()
        a[2]()
        load(3).wait()
        load(4).wait()
        input_columns(0)
        small[1]()
        a[6]()
        early[4]()
        input_columns(1)
        small[2]()
        a[7]()
        input_columns(2)
        a[8]()
        small[3]()
        b[1]()
        settle()
        found = group_sums([None] * 4 + [sb[...], sc[...], None], weights, means, squares, updates)
        small[4]()
        for k in range(3):
            lanes_of = slice(k * 256, (k + 1) * 256)
            vec[6:7, lanes_of] = hvec[k : k + 1]
            vec[7:8, lanes_of] = hvec[3 + k : 4 + k]
        count, mine = weights[4].shape
        index = lax.axis_index("dp") * groups + lax.axis_index("tensor")
        turned = pltpu.roll(vec[...], width - index * mine, 1)
        grads[4][...] = turned[0:count, 0:mine]
        found = found + group_sums(
            [None] * 6 + [grads[4][...]], weights, means, squares, updates
        )
        a[9]()
        total = sa[...]
        for k, at in enumerate((Q_AT, K_AT, V_AT)):
            grads[0][k] = collect(total, at)
        grads[1][...] = collect(total, O_AT).T
        parts = [grads[0][k] for k in range(3)] + [grads[1][...]]
        norms[...] = found + group_sums(parts + [None] * 3, weights, means, squares, updates)
        for run in final:
            run()


def group_sums(grads, weights, means, squares, updates):
    lane = lax.broadcasted_iota(jnp.int32, (8, 128), 1)
    line = lax.broadcasted_iota(jnp.int32, (8, 128), 0)
    found = jnp.zeros((8, 128), F32)
    for group, grad in enumerate(grads):
        if grad is None:
            continue
        i, k = (0, group) if group < 3 else (group - 2, ...)
        weight, mean, square = (ref[i][k] for ref in (weights, means, squares))
        update = adam_parts(grad, mean, square)[2]
        if i < 4:
            update = update + WEIGHT_DECAY * weight
        updates[i][k] = update
        if i < 4:
            pair = (sum_all(weight * weight), sum_all(update * update))
            for which in range(2):
                hit = (lane == group) & (line == which)
                found = found + jnp.where(hit, pair[which], 0.0)
            continue
        for which, values in enumerate((weight, update)):
            per_row = jnp.sum(values * values, axis=1, keepdims=True)
            for row in range(weight.shape[0]):
                hit = (lane == 6 + min(row, 8)) & (line == which)
                found = found + jnp.where(hit, per_row[row : row + 1], 0.0)
    return found


def back(pm, gm, lse, seg, wa, xt, gbt, gb, accb, part, vg, bg,
         weights, means, squares, sizes):
    deep, groups = sizes[0] // 2, sizes[1]
    tokens, width = gb.shape
    lanes = pm.shape[2]
    length = seg.shape[1]
    seqs = tokens // length
    rows = width // sizes[0]
    copies = 7 + 2 * deep + 4 + 2 * deep + 2 * (deep + 2) + 7 + deep
    small = [weights, means, squares]
    anywhere = pl.BlockSpec(memory_space=pl.ANY)
    outs = [jax.ShapeDtypeStruct(weight.shape, F32) for weight in weights] * 2 + [
        jax.ShapeDtypeStruct((8, 128), F32),
        jax.ShapeDtypeStruct((tokens, width), F32),
    ]
    return pl.pallas_call(
        functools.partial(back_kernel, sizes=sizes, chunk=min(256, length)),
        grid=(groups * seqs,),
        in_specs=[
            pl.BlockSpec((1, length, lanes), lambda i: (far_first(i, groups), i % 2, 0)),
            pl.BlockSpec((1, length, gm.shape[2]), lambda i: (far_first(i, groups), i % 2, 0)),
            pl.BlockSpec((1, 1, 8, length), lambda i: (far_first(i, groups), i % 2, 0, 0)),
            once(seg.shape),
            anywhere,
            anywhere,
            anywhere,
            anywhere,
            anywhere,
            once(part.shape),
            once(vg.shape),
            once(bg.shape),
        ]
        + [once(ref.shape) for group in small for ref in group],
        out_specs=[once(ref.shape) for ref in outs],
        out_shape=outs,
        scratch_shapes=[
            pltpu.VMEM((groups, tokens, lanes), BF16),
            pltpu.VMEM((groups, 8, lanes), F32),
            pltpu.SemaphoreType.DMA((copies,)),
            pltpu.SemaphoreType.DMA((copies,)),
            pltpu.VMEM((deep + 2, 16, width), F32),
            pltpu.VMEM((deep + 2, 8, 256), F32),
            pltpu.VMEM((8 + deep, 8, 128), F32),
            pltpu.VMEM((16, width), F32),
            pltpu.VMEM((8, 256), F32),
            pltpu.SemaphoreType.DMA((5,)),
            pltpu.VMEM((rows, lanes), F32),
            pltpu.VMEM(wa.shape, BF16),
            pltpu.VMEM(xt.shape, BF16),
            pltpu.VMEM(gbt.shape, BF16),
            pltpu.VMEM(gb.shape, F32),
            pltpu.VMEM(accb.shape, BF16),
            pltpu.VMEM((deep, rows, lanes), BF16),
            pltpu.VMEM((deep, rows, lanes), BF16),
        ]
        + plane_buffers(deep, rows, lanes)
        + core_buffers(deep, rows, lanes)
        + plane_buffers(deep, rows, lanes)
        + [pltpu.VMEM((deep, rows, lanes), BF16)],
        compiler_params=params(collective_id=2, has_side_effects=True),
        name="back",
    )(
        pm, gm, lse, seg, wa, xt, gbt, gb,
        accb, part, vg, bg,
        *weights, *means, *squares,
    )


def apply_kernel(*refs):
    grads, updates, sums = refs[0:5], refs[5:10], refs[10]
    weights, means, squares = refs[11:16], refs[16:21], refs[21:26]
    passed, outs, norms = refs[26:28], refs[28:43], refs[43]
    stores = [pltpu.make_async_copy(passed[k], refs[44 + k], refs[46].at[k]) for k in range(2)]
    for move in stores:
        move.start()
    roots = jnp.sqrt(sums[...])
    norms[...] = roots[0:2, 0:15]
    ratio = LEARN_RATE * roots[0:1] / (roots[1:2] + ADAM_EPS)
    for i in range(5):
        grad = grads[i][...]
        outs[3 * i][...] = MOMENT_DECAY * means[i][...] + (1.0 - MOMENT_DECAY) * grad
        outs[3 * i + 1][...] = (
            MOMENT_DECAY * squares[i][...] + (1.0 - MOMENT_DECAY) * grad * grad
        )
        target = outs[3 * i + 2]
        if i == 0:
            for k in range(3):
                target[k] = weights[i][k] - ratio[:, k : k + 1] * updates[i][k]
        elif i < 4:
            target[...] = weights[i][...] - ratio[:, 2 + i : 3 + i] * updates[i][...]
        else:
            for row in range(target.shape[0]):
                here = slice(row, row + 1)
                step = ratio[:, 6 + min(row, 8) : 7 + min(row, 8)]
                target[here] = weights[i][here] - step * updates[i][here]
    for move in stores:
        move.wait()


def apply(grads, updates, sums, weights, means, squares, passed):
    inside = pl.BlockSpec(memory_space=pltpu.VMEM)
    shapes = []
    for weight in weights:
        shapes += [jax.ShapeDtypeStruct(weight.shape, F32)] * 3
    shapes.append(jax.ShapeDtypeStruct((2, 15), F32))
    shapes += [jax.ShapeDtypeStruct(entry.shape, entry.dtype) for entry in passed]
    anywhere = [pl.BlockSpec(memory_space=pl.ANY)] * 2
    return pl.pallas_call(
        apply_kernel,
        in_specs=[inside] * 28,
        out_specs=[inside] * 16 + anywhere,
        out_shape=shapes,
        scratch_shapes=[pltpu.SemaphoreType.DMA((2,))],
        compiler_params=params(),
        name="apply",
    )(*grads, *updates, sums, *weights, *means, *squares, *passed)


def make_body(sizes):
    def body(
        tokens, cotangent, segments,
        qkv_weight, out_weight, inner_weight, outer_weight, vectors,
        qkv_mean, out_mean, inner_mean, outer_mean, vector_mean,
        qkv_square, out_square, inner_square, outer_square, vector_square,
    ):
        groups = sizes[1]
        token_count, width = tokens.shape
        length = segments.shape[1]
        seqs = token_count // length
        cols = qkv_weight.shape[2]
        tensor_index = lax.axis_index("tensor")
        weights = (qkv_weight, out_weight, inner_weight, outer_weight, vectors)
        old_means = (qkv_mean, out_mean, inner_mean, outer_mean, vector_mean)
        old_squares = (qkv_square, out_square, inner_square, outer_square, vector_square)
        if sizes[0] % 2 == 0 and groups == 4 and qkv_weight.shape[1] % 96 == 0:
            weights, old_means, old_squares = (
                entry[:3] + (entry[3].T, entry[4]) for entry in (weights, old_means, old_squares)
            )
            wa, wb, wc, full, pm, lse, hid, slope, nlt, xt, n1, inv1 = gather_attend(
                weights, tokens, segments, sizes
            )
            result, gb, gm, gbt, accb, part, vg, bg = layer(
                cotangent, hid, slope, n1, inv1, nlt, wa, wb, wc, full, sizes
            )
            *changes, sums, input_grad = back(
                pm, gm, lse, segments, wa, xt, gbt, gb, accb, part, vg, bg,
                weights, old_means, old_squares, sizes,
            )
            passed = (result, input_grad)
            new = list(
                apply(changes[:5], changes[5:], sums, weights, old_means, old_squares, passed)
            )
            new[9:12] = [entry.T for entry in new[9:12]]
            return tuple(new[16:]) + tuple(new[:16])
        seg = lax.dynamic_slice_in_dim(segments, tensor_index * seqs, seqs, 0)
        seg = jnp.broadcast_to(seg[:, None, :], (seqs, 8, length))
        pack_a = spread(qkv_weight[0], qkv_weight[1], qkv_weight[2], out_weight.T).astype(BF16)
        pack_b = inner_weight.astype(BF16)
        pack_c = outer_weight.T.astype(BF16)
        wa, wb, wc = (gather_blocks(pack, sizes) for pack in (pack_a, pack_b, pack_c))
        full = lax.all_gather(vectors, ("dp", "tensor"), axis=1, tiled=True)
        q_bias = full[6].reshape(groups, cols)
        v_bias = full[7].reshape(groups, cols)
        none = jnp.zeros_like(q_bias)
        proj_bias = spread(q_bias, none, v_bias, none)
        proj_bias = jnp.broadcast_to(proj_bias[:, None, :], (groups, 8, 4 * cols))
        inner_bias = full[8:].reshape(groups, -1)
        pm, lse = attend_fwd(tokens, wa, proj_bias, seg, length)
        result, hid, gi, nl, gsl, gbl, gb, gm, vg, bg = ffn(
            tokens, cotangent, pm, wa, wb, wc, full, inner_bias
        )
        gp, gsum = attend_bwd(pm, gm, lse, seg)

        grad_c = jnp.einsum("td,gtf->gdf", gsl, hid, preferred_element_type=F32).astype(BF16)
        grad_b = jnp.einsum("td,gtf->gdf", nl, gi, preferred_element_type=F32).astype(BF16)
        from_tokens = jnp.einsum("td,gtc->gdc", tokens, gp, preferred_element_type=F32)
        from_branch = jnp.einsum("td,gtc->gdc", gbl, pm, preferred_element_type=F32)
        lane = lax.broadcasted_iota(jnp.int32, (1, 1, LANES), 2)
        is_mixed = (lane >= 512) & ((lane < 640) | (lane >= 704))
        grad_a = jnp.where(is_mixed, from_branch, from_tokens).astype(BF16)
        input_grad = gb + jnp.einsum(
            "gtc,gdc->td",
            jnp.where(is_mixed, jnp.zeros((), BF16), gp),
            wa,
            preferred_element_type=F32,
        )
        head_rows = jnp.stack([collect(gsum[:, 0], at).reshape(-1) for at in (Q_AT, V_AT)])
        vector_grad = jnp.concatenate([vg[:6], head_rows, bg[:groups].reshape(-1, width)], axis=0)
        sum_a, sum_b, sum_c = (
            scatter_blocks(grad, sizes).astype(F32) for grad in (grad_a, grad_b, grad_c)
        )
        vector_sum = lax.psum_scatter(
            vector_grad, ("dp", "tensor"), scatter_dimension=1, tiled=True
        )
        new = lamb_plain(sum_a, sum_b, sum_c, vector_sum, weights, old_means, old_squares)
        return (result, input_grad) + tuple(new)

    return body

def solution(mesh):
    sizes = (mesh.shape["dp"], mesh.shape["tensor"])
    rows = P(("dp", "tensor"), None)
    qkv = P(None, "dp", "tensor")
    out = P("tensor", "dp")
    inner = P("dp", "tensor")
    vec = P(None, ("dp", "tensor"))
    weights = (qkv, out, inner, out, vec)
    return jax.shard_map(
        make_body(sizes),
        mesh=mesh,
        in_specs=(rows, rows, P("dp", None)) + weights * 3,
        out_specs=(rows, rows) + (qkv,) * 3 + (out,) * 3 + (inner,) * 3 + (out,) * 3 + (vec,) * 3 + (P(),),
        check_vma=False,
    )
```

time: 963 us -> 223 us (0.23); the launches traced: 950 us -> 223 us
  waiting for transfers between devices: 344 us -> 0 us
  matrix products: 233 us -> 0 us
  Pallas kernels: 0 us -> 222 us
  blocking collectives: 192 us -> 0 us
  local copies, waits for them, and re-layouts: 84 us -> 0 us
  other arithmetic: 75.9 us -> 0 us
  between operations: 18.4 us -> 0.86 us
    dot_general x67 -> x0, matrix products: 227 us -> none  [the longest x1 34.8 us: body(): jnp.dot(normed_low, inner_low, preferred_element_type=jnp.float32)]
    pallas_call x0 -> x4, Pallas kernels: none -> 222 us  [the longest x1 91.6 us: gather_attend(): pl.pallas_call(functools.partial(gather_attend_kernel, sizes=sizes, chunk...]
    reduce_scatter x6 -> x0, waiting for transfers between devices: 170 us -> none  [the longest x1 58.3 us: body(): lax.psum_scatter(jnp.einsum('tf,df->td', piece, inner_low, preferred_elem...]
    all_gather x6 -> x0, waiting for transfers between devices: 127 us -> none  [the longest x1 46.5 us: body(): lax.all_gather(grad_second.astype(jnp.bfloat16), 'tensor', axis=0, tiled=...]
    all_gather x3 -> x0, blocking collectives: 112 us -> none  [the longest x1 44.9 us: body(): full_vectors = lax.all_gather(vectors, ('dp', 'tensor'), axis=1, tiled=True)]
    unnamed x16 -> x0, waiting for transfers between devices: 46.8 us -> none
    psum x1 -> x0, blocking collectives: 40.2 us -> none  [body(): lax.psum((group_squares(*params), group_squares(*updates)), ('dp', 'tenso...]
    unnamed x1 -> x0, blocking collectives: 40 us -> none
  transfers between devices with their start and end apart: 14 -> 0, of which waited for: 8 -> 0; matrix products, arithmetic and copies ran while one was open for 27% -> 0% of each run, Pallas kernels for 0% -> 0%
where the time goes in v1:
time: 223 us
  Pallas kernels  222 us (100%)
    pallas_call x1, Pallas kernels, gather_attend(): pl.pallas_call(functools.partial(gather_attend_kernel, sizes=sizes, chunk...  91.6 us
    pallas_call x1, Pallas kernels, back(): pl.pallas_call(functools.partial(back_kernel, sizes=sizes, chunk=min(256,...  72.2 us
    pallas_call x1, Pallas kernels, layer(): pl.pallas_call(functools.partial(layer_kernel, sizes=sizes), grid=(3 * gr...  50.1 us
    pallas_call x1, Pallas kernels, apply(): pl.pallas_call(apply_kernel, in_specs=[inside] * 28, out_specs=[inside] *...  7.84 us

profile of v1, /device:TPU:0, one launch (start us, length us, event | category | flops | bytes accessed | tf_op | source)
XLA Modules:
  0.0 222.7 jit_solution(4368012632937939177)
XLA Ops:
  0.7 91.6 %gather_attend.1 = (bf16[2,2,4,2,96,768]{5,4,3,2,1,0:T(8,128)(2,1)}, bf16[2,2,4,2,96,768]{5,4,3,2,1,0:T(8,128)(2,1)}, bf16[2,2,4,2,96,768]{5,4,3,2,1,0:T(8,128)(...) custom-call(f32[3,96,192]{2,1,0:T(8,128)} %refs_11_.3, ...), custom_call_target="tpu_custom_call" | custom-call | tf_op jit(solution)/shard_map/gather_attend/pallas_call | solution.py:1167
  92.3 50.1 %layer.1 = (bf16[1024,768]{1,0:T(8,128)(2,1)}, f32[1024,768]{1,0:T(8,128)}, bf16[4,1024,256]{2,1,0:T(8,128)(2,1)}, bf16[768,1024]{1,0:T(8,128)(2,1)}, bf16[2,4,2...) custom-call(bf16[1024,768]{1,0:T(8,128)(2,1)} %cot_ref.1, ...), custom_call_target="tpu_custom_call" | custom-call | tf_op jit(solution)/shard_map/layer/pallas_call | solution.py:1407
  142.4 72.2 %back.1 = (f32[3,96,192]{2,1,0:T(8,128)}, f32[192,96]{1,0:T(8,128)}, f32[96,768]{1,0:T(8,128)}, f32[96,768]{1,0:T(8,128)}, f32[12,24]{1,0:T(8,128)}, /*index=5*/...) custom-call(bf16[4,1024,768]{2,1,0:T(8,128)(2,1)} %get-tuple-element, ...), custom_call_target="tpu_custom_call" | custom-call | tf_op jit(solution)/shard_map/back/pallas_call | solution.py:1662
  214.7 7.8 %apply.1 = (f32[3,96,192]{2,1,0:T(8,128)}, f32[3,96,192]{2,1,0:T(8,128)}, f32[3,96,192]{2,1,0:T(8,128)}, f32[192,96]{1,0:T(8,128)}, f32[192,96]{1,0:T(8,128)}, /...) custom-call(f32[3,96,192]{2,1,0:T(8,128)} %get-tuple-element.87.refs, ...), custom_call_target="tpu_custom_call" | custom-call | tf_op jit(solution)/shard_map/apply/pallas_call | solution.py:1754

commit v2 on v1

--- a/solution.py
+++ b/solution.py
@@ -505,42 +505,6 @@
     return [start, middle, last]
 
 
-def gather_small(place, links, base, whole):
-    p, deep = place, place.deep
-    mine, line, plane = whole.at[p.x, p.c, p.z, p.y], whole.at[p.x, p.c, :, p.y], whole.at[p.x, p.c]
-    half = whole.at[:, p.c]
-
-    def over_z(j):
-        return links.copy(base + j, mine, p.to_z(j))
-
-    def stage0():
-        for j in range(1, deep):
-            over_z(j).start()
-
-    def stage1():
-        for j in range(1, deep):
-            links.landed(base + j, whole.at[p.x, p.c, p.from_z(j), p.y], p.to_z(j))
-        links.copy(base + deep, line, p.to_y()).start()
-
-    def stage2():
-        links.landed(base + deep, whole.at[p.x, p.c, :, 1 - p.y], p.to_y())
-        links.copy(base + deep + 1, plane, p.to_x()).start()
-
-    def stage3():
-        links.landed(base + deep + 1, whole.at[1 - p.x, p.c], p.to_x())
-        links.copy(base + deep + 2, half, p.to_c()).start()
-
-    def stage4():
-        links.landed(base + deep + 2, whole.at[:, 1 - p.c], p.to_c())
-        for j in range(1, deep):
-            over_z(j).wait_send()
-        links.copy(base + deep, line, p.to_y()).wait_send()
-        links.copy(base + deep + 1, plane, p.to_x()).wait_send()
-        links.copy(base + deep + 2, half, p.to_c()).wait_send()
-
-    return [stage0, stage1, stage2, stage3, stage4]
-
-
 def gather_stages(place, links, base, own, whole, start=0, count=None):
     p, deep = place, place.deep
     count = own.shape[0] if count is None else count
@@ -567,10 +531,6 @@
         for j in range(1, deep):
             links.copy(kz + j, own, p.to_z(j), mine).start()
 
-    def sent():
-        for j in range(1, deep):
-            links.copy(kz + j, own, p.to_z(j), mine).wait_send()
-
     def stage1():
         keep().wait()
         for j in range(1, deep):
@@ -600,6 +560,8 @@
         links.landed(ks + 2, whole.at[p.x, o, :, 1 - p.y, later], p.to_c())
         links.landed(ks + 3, whole.at[:, o, :, 1 - p.y, first], p.to_c())
         links.landed(ks + 4, whole.at[1 - p.x, o, :, :, later], p.to_c())
+        for j in range(1, deep):
+            links.copy(kz + j, own, p.to_z(j), mine).wait_send()
         links.copy(ka, ax, p.to_x()).wait_send()
         links.copy(kb, by, p.to_y()).wait_send()
         links.copy(ka + 1, ay, p.to_y()).wait_send()
@@ -610,14 +572,13 @@
         links.copy(ks + 3, ay_in, p.to_c()).wait_send()
         links.copy(ks + 4, bx_in, p.to_c()).wait_send()
 
-    return [stage0, stage1, stage2, stage3, stage4, sent]
-
-
-def gather_stages_late(place, links, base, own, whole, start=0, count=None):
+    return [stage0, stage1, stage2, stage3, stage4]
+
+
+def gather_stages_late(place, links, base, own, whole):
     p, deep = place, place.deep
-    count = own.shape[0] if count is None else count
-    half = count // 2
-    rows, first, later = pl.ds(start, count), pl.ds(start, half), pl.ds(start + half, half)
+    half = own.shape[0] // 2
+    first, later = pl.ds(0, half), pl.ds(half, half)
     mine = whole.at[p.x, p.c, p.z, p.y]
     pair_f, pair_l = whole.at[:, p.c, p.z, p.y, first], whole.at[p.x, p.c, p.z, :, later]
     line_f, line_l = whole.at[:, p.c, :, p.y, first], whole.at[p.x, p.c, :, :, later]
@@ -626,7 +587,7 @@
     kf, kl = base + 8, base + 8 + deep
 
     def keep():
-        return pltpu.make_async_copy(own.at[rows], mine.at[rows], links.send.at[base])
+        return pltpu.make_async_copy(own, mine, links.send.at[base])
 
     def to_x():
         return links.copy(base + 1, own.at[first], p.to_x(), mine.at[first])
@@ -646,11 +607,6 @@
         for j in range(1, deep):
             links.copy(kf + j, pair_f, p.to_z(j)).start()
             links.copy(kl + j, pair_l, p.to_z(j)).start()
-
-    def sent():
-        for j in range(1, deep):
-            links.copy(kf + j, pair_f, p.to_z(j)).wait_send()
-            links.copy(kl + j, pair_l, p.to_z(j)).wait_send()
 
     def stage2():
         for j in range(1, deep):
@@ -676,6 +632,9 @@
         links.landed(base + 8, whole.at[1 - p.x, o, :, :, later], p.to_c())
         to_x().wait_send()
         to_y().wait_send()
+        for j in range(1, deep):
+            links.copy(kf + j, pair_f, p.to_z(j)).wait_send()
+            links.copy(kl + j, pair_l, p.to_z(j)).wait_send()
         links.copy(base + 3, line_f, p.to_y()).wait_send()
         links.copy(base + 4, line_l, p.to_x()).wait_send()
         links.copy(base + 5, line_f, p.to_c()).wait_send()
@@ -683,7 +642,7 @@
         links.copy(base + 7, line_f_in, p.to_c()).wait_send()
         links.copy(base + 8, line_l_in, p.to_c()).wait_send()
 
-    return [stage0, stage1, stage2, stage3, stage4, sent]
+    return [stage0, stage1, stage2, stage3, stage4]
 
 
 GATHER_COPIES = 9
@@ -956,8 +915,13 @@
     return outs + [jnp.stack([weight_norms, update_norms])]
 
 
-A_ROWS = ((0, 32), (32, 32), (64, 32))
-B_ROWS = ((0, 64), (64, 32))
+A_PIECES = 3
+
+
+def own_first(order):
+    tensor = lax.axis_index("tensor")
+    x, c = tensor // 2, tensor % 2
+    return jnp.where(order % 2 == 0, x, 1 - x) * 2 + jnp.where(order < 2, c, 1 - c)
 
 
 def gather_attend_kernel(
@@ -977,23 +941,15 @@
     lanes = pack_a.shape[1]
     length = tokens // 2
     tail = 256
+    count = pack_a.shape[0] // A_PIECES
     ga = [
-        gather_stages(place, links, k * each, pack_a, wa, *rows) for k, rows in enumerate(A_ROWS)
+        gather_stages(place, links, k * each, pack_a, wa, k * count, count) for k in range(A_PIECES)
     ]
-    more = len(A_ROWS) * each
-    gb = [
-        gather_stages(place, links, more + k * each, pack_b, wb, *rows)
-        for k, rows in enumerate(B_ROWS)
-    ]
-    more += len(B_ROWS) * each
-    small = gather_small(place, links, more, slots)
-    more += deep + 3
-    gc = [
-        gather_stages_late(place, links, more + k * (each + deep), pack_c, wc, *rows)
-        for k, rows in enumerate(B_ROWS)
-    ]
-    sent = 5
-    t, s = step // 2, step % 2
+    gb = gather_stages(place, links, A_PIECES * each, pack_b, wb)
+    more = (A_PIECES + 1) * each
+    small = add_everywhere(place, links, more, full, slots)
+    gc = gather_stages_late(place, links, more + deep + 2, pack_c, wc)
+    t, s = own_first(jnp.minimum(step // 2, groups - 1)), step % 2
     last = 2 * groups + groups - 1
 
     def keep(k):
@@ -1004,85 +960,68 @@
     def _():
         out_rows = out_ref[...].T
         pack_a[...] = spread(qkv_ref[0], qkv_ref[1], qkv_ref[2], out_rows).astype(BF16)
-        count, mine = vec_ref.shape
-        slots[place.x, place.c, place.z, place.y, 0:count, 0:mine] = vec_ref[...]
         place.greet()
+        for k in range(A_PIECES):
+            ga[k][0]()
+        pack_c[...] = outer_ref[...].astype(BF16)
+        gc[0]()
+        pack_b[...] = inner_ref[...].astype(BF16)
+        full[...] = jnp.zeros_like(full)
+        mine = vec_ref.shape[1]
+        full[0 : vec_ref.shape[0], 0:mine] = vec_ref[...]
+        index = lax.axis_index("dp") * groups + lax.axis_index("tensor")
+        full[...] = pltpu.roll(full[...], index * mine, 1)
         small[0]()
-        ga[0][0]()
-        pack_c[...] = outer_ref[...].astype(BF16)
-        gc[0][0]()
-        gc[1][0]()
-        ga[0][sent]()
-        ga[1][0]()
         small[1]()
         ga[0][1]()
-        ga[1][sent]()
-        ga[2][0]()
-        pack_b[...] = inner_ref[...].astype(BF16)
         small[2]()
+        ga[0][2]()
         ga[1][1]()
-        ga[0][2]()
-        ga[2][sent]()
-        gb[0][0]()
         small[3]()
+        gb[0]()
         ga[2][1]()
         ga[1][2]()
+        ga[2][2]()
         ga[0][3]()
-        xt_ref[...] = x_ref[...].T
-        ga[2][2]()
-        gb[0][sent]()
-        gb[1][0]()
-        ga[1][3]()
         small[4]()
-        full[...] = jnp.zeros_like(full)
-        for k in range(sizes[0] * groups):
-            dp, tensor = k // groups, k % groups
-            block = slots[tensor // 2, tensor % 2, dp // 2, dp % 2, 0:count, 0:mine]
-            full[0:count, k * mine : (k + 1) * mine] = block
-        gb[1][sent]()
-        gc[0][1]()
-        gb[0][1]()
-        ga[2][3]()
         for g in range(groups):
             bias[g] = jnp.zeros(bias.shape[1:], F32)
             for h in range(HEADS):
-                here = slice(g * cols + h * HD, g * cols + (h + 1) * HD)
-                bias[g, 0:1, Q_AT[h] : Q_AT[h] + HD] = full[6:7, here]
-                bias[g, 0:1, V_AT[h] : V_AT[h] + HD] = full[7:8, here]
+                mine = slice(g * cols + h * HD, g * cols + (h + 1) * HD)
+                bias[g, 0:1, Q_AT[h] : Q_AT[h] + HD] = full[6:7, mine]
+                bias[g, 0:1, V_AT[h] : V_AT[h] + HD] = full[7:8, mine]
+        xt_ref[...] = x_ref[...].T
         n1_ref[...] = x_ref[...].astype(F32) + full[4:5, :]
-        gb[1][1]()
-        for piece in ga:
-            piece[4]()
+        ga[1][3]()
+        gb[1]()
+        gc[1]()
+        ga[2][3]()
+
+    @pl.when(step == groups)
+    def _():
+        for k in range(A_PIECES):
+            ga[k][4]()
         keep(0).start()
 
-    @pl.when(step == 1)
-    def _():
-        gb[0][2]()
-        gb[1][2]()
-
-    @pl.when(step == 3)
-    def _():
-        gc[0][sent]()
-        gc[1][1]()
-
-    @pl.when(step == 4)
-    def _():
-        gc[0][2]()
-
-    @pl.when(step == 5)
-    def _():
-        gb[0][3]()
-
-    @pl.when(step == 7)
-    def _():
-        gb[1][3]()
-        gc[1][sent]()
-        gc[1][2]()
+    @pl.when(step == 2)
+    def _():
+        gb[2]()
+
+    @pl.when(step == 6)
+    def _():
+        gb[3]()
+        gc[2]()
 
     @pl.when(step == 2 * groups + 2)
     def _():
-        gc[0][3]()
+        gb[4]()
         keep(1).start()
+        gc[3]()
+
+    @pl.when(step == last)
+    def _():
+        gc[4]()
+        keep(2).start()
 
     @pl.when((step < 2 * groups) & (s == 0))
     def _():
@@ -1116,12 +1055,10 @@
             part = (normal_one * full[0:1, :] + full[1:2, :]).astype(BF16)
             low[rows] = part
             nlt_ref[:, rows] = part.T
-        gb[0][4]()
-        gb[1][4]()
 
     @pl.when(step >= 2 * groups)
     def _():
-        g = step - 2 * groups
+        g = own_first(step - 2 * groups)
         weight = wb[g // 2, g % 2].reshape(width, lanes)
         for n in range(lanes // 256):
             here = slice(n * 256, (n + 1) * 256)
@@ -1132,10 +1069,6 @@
 
     @pl.when(step == last)
     def _():
-        gc[1][3]()
-        gc[0][4]()
-        gc[1][4]()
-        keep(2).start()
         for k in range(3):
             keep(k).wait()
 
@@ -1147,8 +1080,7 @@
 def gather_attend(weights, x, seg, sizes):
     qkv, out, inner, outer, vec = weights
     deep, groups = sizes[0] // 2, sizes[1]
-    each = GATHER_COPIES + deep
-    copies = len(A_ROWS) * each + len(B_ROWS) * (2 * each + deep) + deep + 3
+    copies = (A_PIECES + 1) * (GATHER_COPIES + deep) + deep + 2 + GATHER_COPIES + 2 * deep
     tokens, width = x.shape
     length = seg.shape[1]
     seqs = tokens // length
@@ -1159,10 +1091,11 @@
     whole = jax.ShapeDtypeStruct(parts, BF16)
 
     def now(i):
-        return jnp.minimum(i, steps - 1)
+        i = jnp.minimum(i, steps - 1)
+        return own_first(i // 2), i % 2
 
     def part(i):
-        return jnp.clip(i - steps, 0, groups - 1)
+        return own_first(jnp.clip(i - steps, 0, groups - 1))
 
     wa, wb, wc, *rest = pl.pallas_call(
         functools.partial(gather_attend_kernel, sizes=sizes, chunk=min(256, length)),
@@ -1175,8 +1108,8 @@
         out_specs=[anywhere] * 3
         + [
             once((16, width)),
-            pl.BlockSpec((1, tokens, lanes), lambda i: (now(i) // 2, 0, 0)),
-            pl.BlockSpec((1, 1, 8, length), lambda i: (now(i) // 2, now(i) % 2, 0, 0)),
+            pl.BlockSpec((1, tokens, lanes), lambda i: (now(i)[0], 0, 0)),
+            pl.BlockSpec((1, 1, 8, length), lambda i: (*now(i), 0, 0)),
             pl.BlockSpec((1, tokens, lanes), lambda i: (part(i), 0, 0)),
             pl.BlockSpec((1, tokens, lanes), lambda i: (part(i), 0, 0)),
             once((width, tokens)),
@@ -1199,7 +1132,7 @@
         scratch_shapes=[
             pltpu.SemaphoreType.DMA((copies,)),
             pltpu.SemaphoreType.DMA((copies,)),
-            pltpu.VMEM((2, 2, deep, 2, 16, 128), F32),
+            pltpu.VMEM((deep + 2, 16, width), F32),
             pltpu.VMEM((rows, lanes), BF16),
             pltpu.VMEM((rows, lanes), BF16),
             pltpu.VMEM((rows, lanes), BF16),
@@ -1252,7 +1185,7 @@
 
     def load(k):
         pairs = (
-            (n1_hbm, n1_ref), (nlt_hbm, nlt_ref), (wa_hbm.at[:, :, pl.ds(lanes - tail, tail)], wo_ref)
+            (n1_hbm, n1_ref), (nlt_hbm, nlt_ref.at[pl.ds(0, width)]), (wa_hbm.at[:, :, pl.ds(lanes - tail, tail)], wo_ref)
         )
         return pltpu.make_async_copy(*pairs[k], in_sem.at[2 * groups + k])
 
@@ -1278,6 +1211,7 @@
         vg_ref[...] = jnp.zeros_like(vg_ref)
         bg_ref[...] = jnp.zeros_like(bg_ref)
         acc[...] = jnp.zeros_like(acc)
+        nlt_ref[width:] = jnp.ones((nlt_ref.shape[0] - width, tokens), BF16)
 
     @pl.when(step < groups)
     def _():
@@ -1341,12 +1275,12 @@
             grad_hidden = dot(low[...], wc_ref[t, :, here])
             part = (grad_hidden * slope_ref[0, :, here].astype(F32)).astype(BF16)
             gi[:, here] = part
-            bg_ref[pl.ds(t, 1), here] = jnp.sum(part.astype(F32), axis=0, keepdims=True)
         for here in columns:
             acc[:, here] += dot(gi[...], wb_ref[t, here], NT)
         for here in columns:
-            part = dot(nlt_ref[...], gi[:, here]).astype(BF16)
-            accb[slot, :, :, :, here] = part.reshape(deep, 2, -1, 256)
+            part = dot(nlt_ref[...], gi[:, here])
+            bg_ref[pl.ds(t, 1), here] = part[width : width + 1]
+            accb[slot, :, :, :, here] = part[:width].astype(BF16).reshape(deep, 2, -1, 256)
 
     @pl.when(step == 2 * groups + 1)
     def _():
@@ -1429,7 +1363,7 @@
         ],
         scratch_shapes=[
             pltpu.VMEM(n1.shape, F32),
-            pltpu.VMEM(nlt.shape, BF16),
+            pltpu.VMEM((width + 16, tokens), BF16),
             pltpu.VMEM((groups, width, tail), BF16),
             matrix,
             matrix,
@@ -1488,7 +1422,7 @@
     t, s = far_first(step, groups), step % 2
 
     def load(k):
-        pairs = ((accb_hbm, accb), (xt_hbm, xt_ref), (gbt_hbm, gbt_ref), (wa_hbm, wa_ref), (gb_hbm, gb_ref))
+        pairs = ((accb_hbm, accb), (xt_hbm, xt_ref.at[pl.ds(0, width)]), (gbt_hbm, gbt_ref), (wa_hbm, wa_ref), (gb_hbm, gb_ref))
         return pltpu.make_async_copy(*pairs[k], load_sem.at[k])
 
     @pl.when(step == 0)
@@ -1500,7 +1434,7 @@
         start()
         for k in range(1, 5):
             load(k).start()
-        gsum[...] = jnp.zeros_like(gsum)
+        xt_ref[width:] = jnp.ones((xt_ref.shape[0] - width, tokens), BF16)
         vec[...] = jnp.zeros_like(vec)
         hvec[...] = jnp.zeros_like(hvec)
         vec[0:6] = vg_ref[0:6]
@@ -1540,7 +1474,6 @@
     rows = pl.ds(pl.multiple_of(s * length, length), length)
     row = seg_ref[pl.ds(lax.axis_index("tensor") * 2 + s, 1)]
     attend_back(pm_ref.at[0], gm_ref.at[0], lse_ref, row, gp.at[t, rows], chunk)
-    gsum[t, 0:1, :] += jnp.sum(gp[t, rows].astype(F32), axis=0, keepdims=True)
 
     @pl.when(s == 1)
     def _():
@@ -1550,8 +1483,10 @@
             here = slice(n * 256, (n + 1) * 256)
             if n < lanes // 256 - 1:
                 part = dot(xt_ref[...], gp[t, :, here])
+                gsum[t, 0:1, here] = part[width : width + 1]
+                part = part[:width]
             else:
-                from_x = dot(xt_ref[...], gp[t, :, here])
+                from_x = dot(xt_ref[0:width], gp[t, :, here])
                 part = dot(gbt_ref[...], gp[t, :, here])
                 lane = lax.broadcasted_iota(jnp.int32, part.shape, 1)
                 part = jnp.where((lane >= 128) & (lane < 192), from_x, part)
@@ -1565,7 +1500,7 @@
             part = halves(part, jnp.zeros_like(part))
             total = total + dot(gp[g, :, 0:512], wa_ref[g, here, 0:512], NT)
             total = total + dot(part, wa_ref[g, here, 640:768], NT)
-        ig_ref[:, here] = total
+        ig_ref[:, here] = total.astype(BF16)
 
     @pl.when(step == last)
     def _():
@@ -1657,7 +1592,7 @@
     anywhere = pl.BlockSpec(memory_space=pl.ANY)
     outs = [jax.ShapeDtypeStruct(weight.shape, F32) for weight in weights] * 2 + [
         jax.ShapeDtypeStruct((8, 128), F32),
-        jax.ShapeDtypeStruct((tokens, width), F32),
+        jax.ShapeDtypeStruct((tokens, width), BF16),
     ]
     return pl.pallas_call(
         functools.partial(back_kernel, sizes=sizes, chunk=min(256, length)),
@@ -1692,7 +1627,7 @@
             pltpu.SemaphoreType.DMA((5,)),
             pltpu.VMEM((rows, lanes), F32),
             pltpu.VMEM(wa.shape, BF16),
-            pltpu.VMEM(xt.shape, BF16),
+            pltpu.VMEM((width + 16, tokens), BF16),
             pltpu.VMEM(gbt.shape, BF16),
             pltpu.VMEM(gb.shape, F32),
             pltpu.VMEM(accb.shape, BF16),
@@ -1716,9 +1651,15 @@
     grads, updates, sums = refs[0:5], refs[5:10], refs[10]
     weights, means, squares = refs[11:16], refs[16:21], refs[21:26]
     passed, outs, norms = refs[26:28], refs[28:43], refs[43]
-    stores = [pltpu.make_async_copy(passed[k], refs[44 + k], refs[46].at[k]) for k in range(2)]
-    for move in stores:
-        move.start()
+    wide, sem = refs[46], refs[47]
+    stores = [pltpu.make_async_copy(passed[0], refs[44], sem.at[0])]
+    stores[0].start()
+    rows = wide.shape[0] // 4
+    for k in range(4):
+        here = pl.ds(k * rows, rows)
+        wide[here] = passed[1][here].astype(F32)
+        stores.append(pltpu.make_async_copy(wide.at[here], refs[45].at[here], sem.at[1 + k]))
+        stores[-1].start()
     roots = jnp.sqrt(sums[...])
     norms[...] = roots[0:2, 0:15]
     ratio = LEARN_RATE * roots[0:1] / (roots[1:2] + ADAM_EPS)
@@ -1749,14 +1690,18 @@
     for weight in weights:
         shapes += [jax.ShapeDtypeStruct(weight.shape, F32)] * 3
     shapes.append(jax.ShapeDtypeStruct((2, 15), F32))
-    shapes += [jax.ShapeDtypeStruct(entry.shape, entry.dtype) for entry in passed]
+    shapes += [jax.ShapeDtypeStruct(passed[0].shape, BF16)]
+    shapes += [jax.ShapeDtypeStruct(passed[1].shape, F32)]
     anywhere = [pl.BlockSpec(memory_space=pl.ANY)] * 2
     return pl.pallas_call(
         apply_kernel,
         in_specs=[inside] * 28,
         out_specs=[inside] * 16 + anywhere,
         out_shape=shapes,
-        scratch_shapes=[pltpu.SemaphoreType.DMA((2,))],
+        scratch_shapes=[
+            pltpu.VMEM(passed[1].shape, F32),
+            pltpu.SemaphoreType.DMA((5,)),
+        ],
         compiler_params=params(),
         name="apply",
     )(*grads, *updates, sums, *weights, *means, *squares, *passed)

time: 223 us -> 216 us (0.969)
  Pallas kernels: 222 us -> 215 us
    pallas_call x1, Pallas kernels: 91.6 us -> 82 us  [gather_attend(): pl.pallas_call(functools.partial(gather_attend_kernel, sizes=sizes, chunk...]
    pallas_call x1, Pallas kernels: 50.1 us -> 54.6 us  [layer(): pl.pallas_call(functools.partial(layer_kernel, sizes=sizes), grid=(3 * gr...]
where the time goes in v2:
time: 216 us
  Pallas kernels  215 us (100%)
    pallas_call x1, Pallas kernels, gather_attend(): pl.pallas_call(functools.partial(gather_attend_kernel, sizes=sizes, chunk...  82 us
    pallas_call x1, Pallas kernels, back(): pl.pallas_call(functools.partial(back_kernel, sizes=sizes, chunk=min(256,...  71.3 us
    pallas_call x1, Pallas kernels, layer(): pl.pallas_call(functools.partial(layer_kernel, sizes=sizes), grid=(3 * gr...  54.6 us
    pallas_call x1, Pallas kernels, apply(): pl.pallas_call(apply_kernel, in_specs=[inside] * 28, out_specs=[inside] *...  7.37 us

profile of v2, /device:TPU:0, one launch (start us, length us, event | category | flops | bytes accessed | tf_op | source)
XLA Modules:
  0.0 216.2 jit_solution(18304243944726424449)
XLA Ops:
  0.7 82.0 %gather_attend.1 = (bf16[2,2,4,2,96,768]{5,4,3,2,1,0:T(8,128)(2,1)}, bf16[2,2,4,2,96,768]{5,4,3,2,1,0:T(8,128)(2,1)}, bf16[2,2,4,2,96,768]{5,4,3,2,1,0:T(8,128)(...) custom-call(f32[3,96,192]{2,1,0:T(8,128)} %refs_11_.3, ...), custom_call_target="tpu_custom_call" | custom-call | tf_op jit(solution)/shard_map/gather_attend/pallas_call | solution.py:1100
  82.7 54.6 %layer.1 = (bf16[1024,768]{1,0:T(8,128)(2,1)}, f32[1024,768]{1,0:T(8,128)}, bf16[4,1024,256]{2,1,0:T(8,128)(2,1)}, bf16[768,1024]{1,0:T(8,128)(2,1)}, bf16[2,4,2...) custom-call(bf16[1024,768]{1,0:T(8,128)(2,1)} %cot_ref.1, ...), custom_call_target="tpu_custom_call" | custom-call | tf_op jit(solution)/shard_map/layer/pallas_call | solution.py:1341
  137.3 71.3 %back.1 = (f32[3,96,192]{2,1,0:T(8,128)}, f32[192,96]{1,0:T(8,128)}, f32[96,768]{1,0:T(8,128)}, f32[96,768]{1,0:T(8,128)}, f32[12,24]{1,0:T(8,128)}, /*index=5*/...) custom-call(bf16[4,1024,768]{2,1,0:T(8,128)(2,1)} %get-tuple-element, ...), custom_call_target="tpu_custom_call" | custom-call | tf_op jit(solution)/shard_map/back/pallas_call | solution.py:1597
  208.6 7.4 %apply.1 = (f32[3,96,192]{2,1,0:T(8,128)}, f32[3,96,192]{2,1,0:T(8,128)}, f32[3,96,192]{2,1,0:T(8,128)}, f32[192,96]{1,0:T(8,128)}, f32[192,96]{1,0:T(8,128)}, /...) custom-call(f32[3,96,192]{2,1,0:T(8,128)} %get-tuple-element.87.refs, ...), custom_call_target="tpu_custom_call" | custom-call | tf_op jit(solution)/shard_map/apply/pallas_call | solution.py:1696

commit v3 on v2

--- a/solution.py
+++ b/solution.py
@@ -575,10 +575,11 @@
     return [stage0, stage1, stage2, stage3, stage4]
 
 
-def gather_stages_late(place, links, base, own, whole):
+def gather_stages_late(place, links, base, own, whole, start=0, count=None):
     p, deep = place, place.deep
-    half = own.shape[0] // 2
-    first, later = pl.ds(0, half), pl.ds(half, half)
+    count = own.shape[0] if count is None else count
+    half = count // 2
+    rows, first, later = pl.ds(start, count), pl.ds(start, half), pl.ds(start + half, half)
     mine = whole.at[p.x, p.c, p.z, p.y]
     pair_f, pair_l = whole.at[:, p.c, p.z, p.y, first], whole.at[p.x, p.c, p.z, :, later]
     line_f, line_l = whole.at[:, p.c, :, p.y, first], whole.at[p.x, p.c, :, :, later]
@@ -587,7 +588,7 @@
     kf, kl = base + 8, base + 8 + deep
 
     def keep():
-        return pltpu.make_async_copy(own, mine, links.send.at[base])
+        return pltpu.make_async_copy(own.at[rows], mine.at[rows], links.send.at[base])
 
     def to_x():
         return links.copy(base + 1, own.at[first], p.to_x(), mine.at[first])
@@ -916,6 +917,7 @@
 
 
 A_PIECES = 3
+C_ROWS = ((0, 64), (64, 32))
 
 
 def own_first(order):
@@ -926,9 +928,10 @@
 
 def gather_attend_kernel(
     qkv_ref, out_ref, inner_ref, outer_ref, vec_ref, x_ref, seg_ref,
-    wa_hbm, wb_hbm, wc_hbm, full, pm_ref, lse_ref, hid_ref, slope_ref, nlt_ref, xt_ref, n1_ref,
-    inv_ref,
-    send, recv, slots, pack_a, pack_b, pack_c, wa, wb, wc, bias, low, out_sem,
+    wa_hbm, wb_hbm, wc_hbm, hid_hbm, nlt_hbm, xt_hbm, n1_hbm,
+    full, pm_ref, lse_ref, slope_ref, acc, inv_ref,
+    send, recv, slots, pack_a, pack_b, pack_c, wa, wb, wc, hid, nlt_ref, xt_ref, n1_ref,
+    bias, low, out_sem, xp, proj_acc,
     *, sizes, chunk,
 ):
     step = pl.program_id(0)
@@ -948,13 +951,26 @@
     gb = gather_stages(place, links, A_PIECES * each, pack_b, wb)
     more = (A_PIECES + 1) * each
     small = add_everywhere(place, links, more, full, slots)
-    gc = gather_stages_late(place, links, more + deep + 2, pack_c, wc)
+    more += deep + 2
+    gc = [
+        gather_stages_late(place, links, more + k * (each + deep), pack_c, wc, *rows)
+        for k, rows in enumerate(C_ROWS)
+    ]
     t, s = own_first(jnp.minimum(step // 2, groups - 1)), step % 2
-    last = 2 * groups + groups - 1
+    last = 4 * groups - 1
 
     def keep(k):
-        pairs = ((wa, wa_hbm), (wb, wb_hbm), (wc, wc_hbm))
+        pairs = (
+            (wa, wa_hbm), (wb, wb_hbm), (wc, wc_hbm), (hid, hid_hbm),
+            (nlt_ref, nlt_hbm), (xt_ref, xt_hbm), (n1_ref, n1_hbm),
+        )
         return pltpu.make_async_copy(*pairs[k], out_sem.at[k])
+
+    def project(piece):
+        here = pl.ds(piece * count, count)
+        for x in range(2):
+            part = dot(xp[piece], wa[x, place.c, :, :, here].reshape(sizes[0] * count, lanes))
+            proj_acc[x] = part if piece == 0 else proj_acc[x] + part
 
     @pl.when(step == 0)
     def _():
@@ -964,8 +980,17 @@
         for k in range(A_PIECES):
             ga[k][0]()
         pack_c[...] = outer_ref[...].astype(BF16)
-        gc[0]()
+        gc[0][0]()
+        gc[1][0]()
         pack_b[...] = inner_ref[...].astype(BF16)
+        xt_ref[...] = x_ref[...].T
+        each_dp = pack_a.shape[0]
+        for k in range(A_PIECES):
+            picked = [
+                xt_ref[dp * each_dp + k * count : dp * each_dp + (k + 1) * count]
+                for dp in range(sizes[0])
+            ]
+            xp[k] = jnp.concatenate(picked, axis=0).T
         full[...] = jnp.zeros_like(full)
         mine = vec_ref.shape[1]
         full[0 : vec_ref.shape[0], 0:mine] = vec_ref[...]
@@ -983,6 +1008,7 @@
         ga[1][2]()
         ga[2][2]()
         ga[0][3]()
+        project(0)
         small[4]()
         for g in range(groups):
             bias[g] = jnp.zeros(bias.shape[1:], F32)
@@ -990,40 +1016,51 @@
                 mine = slice(g * cols + h * HD, g * cols + (h + 1) * HD)
                 bias[g, 0:1, Q_AT[h] : Q_AT[h] + HD] = full[6:7, mine]
                 bias[g, 0:1, V_AT[h] : V_AT[h] + HD] = full[7:8, mine]
-        xt_ref[...] = x_ref[...].T
         n1_ref[...] = x_ref[...].astype(F32) + full[4:5, :]
         ga[1][3]()
-        gb[1]()
-        gc[1]()
+        project(1)
         ga[2][3]()
+        project(2)
 
     @pl.when(step == groups)
     def _():
+        gb[2]()
         for k in range(A_PIECES):
             ga[k][4]()
         keep(0).start()
 
-    @pl.when(step == 2)
-    def _():
-        gb[2]()
-
-    @pl.when(step == 6)
-    def _():
-        gb[3]()
-        gc[2]()
+    @pl.when(step == 1)
+    def _():
+        gb[1]()
+        gc[0][1]()
+
+    @pl.when(step == 5)
+    def _():
+        gc[1][1]()
 
     @pl.when(step == 2 * groups + 2)
     def _():
         gb[4]()
         keep(1).start()
-        gc[3]()
-
-    @pl.when(step == last)
-    def _():
-        gc[4]()
+        gc[1][2]()
+
+    @pl.when(step == 3 * groups)
+    def _():
+        gc[0][3]()
+        gc[1][3]()
+        keep(3).start()
+
+    @pl.when(step == 3 * groups + 2)
+    def _():
+        gc[0][4]()
+        gc[1][4]()
         keep(2).start()
 
-    @pl.when((step < 2 * groups) & (s == 0))
+    @pl.when((step < groups) & (s == 0))
+    def _():
+        pm_ref[0] = (proj_acc[t // 2] + bias[t, 0:1]).astype(BF16)
+
+    @pl.when((step >= groups) & (step < 2 * groups) & (s == 0))
     def _():
         weight = wa[t // 2, t % 2].reshape(width, lanes)
         for n in range(lanes // 256):
@@ -1041,9 +1078,7 @@
     def _():
         mixed = mixed_only(pm_ref[0, :, lanes - tail :])
         weight = wa[t // 2, t % 2, :, :, :, lanes - tail :].reshape(width, tail)
-        for n in range(width // 256):
-            here = slice(n * 256, (n + 1) * 256)
-            n1_ref[:, here] += dot(mixed, weight[here], NT)
+        n1_ref[...] += dot(mixed, weight, NT)
 
     @pl.when(step == 2 * groups)
     def _():
@@ -1052,11 +1087,17 @@
             normal_one, inverse_one = norm_parts(n1_ref[rows])
             n1_ref[rows] = normal_one
             inv_ref[rows] = inverse_one
-            part = (normal_one * full[0:1, :] + full[1:2, :]).astype(BF16)
+            normed = normal_one * full[0:1, :] + full[1:2, :]
+            acc[rows] = normed + full[5:6, :]
+            part = normed.astype(BF16)
             low[rows] = part
             nlt_ref[:, rows] = part.T
-
-    @pl.when(step >= 2 * groups)
+        for k in range(4, 7):
+            keep(k).start()
+        gc[0][2]()
+        gb[3]()
+
+    @pl.when((step >= 2 * groups) & (step < 3 * groups))
     def _():
         g = own_first(step - 2 * groups)
         weight = wb[g // 2, g % 2].reshape(width, lanes)
@@ -1064,12 +1105,18 @@
             here = slice(n * 256, (n + 1) * 256)
             pre = dot(low[...], weight[:, here]) + full[pl.ds(8 + g, 1), here]
             act, turn = gelu_parts(pre)
-            hid_ref[0, :, here] = act.astype(BF16)
+            hid[g, :, here] = act.astype(BF16)
             slope_ref[0, :, here] = turn.astype(BF16)
 
+    @pl.when(step >= 3 * groups)
+    def _():
+        g = own_first(step - 3 * groups)
+        weight = wc[g // 2, g % 2].reshape(width, lanes)
+        acc[...] += dot(hid[g], weight, NT)
+
     @pl.when(step == last)
     def _():
-        for k in range(3):
+        for k in range(7):
             keep(k).wait()
 
 
@@ -1080,7 +1127,8 @@
 def gather_attend(weights, x, seg, sizes):
     qkv, out, inner, outer, vec = weights
     deep, groups = sizes[0] // 2, sizes[1]
-    copies = (A_PIECES + 1) * (GATHER_COPIES + deep) + deep + 2 + GATHER_COPIES + 2 * deep
+    copies = (A_PIECES + 1) * (GATHER_COPIES + deep) + deep + 2
+    copies += len(C_ROWS) * (GATHER_COPIES + 2 * deep)
     tokens, width = x.shape
     length = seg.shape[1]
     seqs = tokens // length
@@ -1097,35 +1145,33 @@
     def part(i):
         return own_first(jnp.clip(i - steps, 0, groups - 1))
 
-    wa, wb, wc, *rest = pl.pallas_call(
+    wa, wb, wc, hid, nlt, xt, n1, *rest = pl.pallas_call(
         functools.partial(gather_attend_kernel, sizes=sizes, chunk=min(256, length)),
-        grid=(steps + groups,),
+        grid=(steps + 2 * groups,),
         in_specs=[once(w.shape) for w in weights]
         + [
             once(x.shape),
             once(seg.shape),
         ],
-        out_specs=[anywhere] * 3
+        out_specs=[anywhere] * 7
         + [
             once((16, width)),
             pl.BlockSpec((1, tokens, lanes), lambda i: (now(i)[0], 0, 0)),
             pl.BlockSpec((1, 1, 8, length), lambda i: (*now(i), 0, 0)),
             pl.BlockSpec((1, tokens, lanes), lambda i: (part(i), 0, 0)),
-            pl.BlockSpec((1, tokens, lanes), lambda i: (part(i), 0, 0)),
-            once((width, tokens)),
-            once((width, tokens)),
             once((tokens, width)),
             once((tokens, 1)),
         ],
         out_shape=[whole] * 3
         + [
+            jax.ShapeDtypeStruct((groups, tokens, lanes), BF16),
+            jax.ShapeDtypeStruct((width, tokens), BF16),
+            jax.ShapeDtypeStruct((width, tokens), BF16),
+            jax.ShapeDtypeStruct((tokens, width), F32),
             jax.ShapeDtypeStruct((16, width), F32),
             jax.ShapeDtypeStruct((groups, tokens, lanes), BF16),
             jax.ShapeDtypeStruct((groups, seqs, 8, length), F32),
             jax.ShapeDtypeStruct((groups, tokens, lanes), BF16),
-            jax.ShapeDtypeStruct((groups, tokens, lanes), BF16),
-            jax.ShapeDtypeStruct((width, tokens), BF16),
-            jax.ShapeDtypeStruct((width, tokens), BF16),
             jax.ShapeDtypeStruct((tokens, width), F32),
             jax.ShapeDtypeStruct((tokens, 1), F32),
         ],
@@ -1139,15 +1185,21 @@
             pltpu.VMEM(parts, BF16),
             pltpu.VMEM(parts, BF16),
             pltpu.VMEM(parts, BF16),
+            pltpu.VMEM((groups, tokens, lanes), BF16),
+            pltpu.VMEM((width, tokens), BF16),
+            pltpu.VMEM((width, tokens), BF16),
+            pltpu.VMEM((tokens, width), F32),
             pltpu.VMEM((groups, 8, lanes), F32),
             pltpu.VMEM((tokens, width), BF16),
-            pltpu.SemaphoreType.DMA((3,)),
+            pltpu.SemaphoreType.DMA((7,)),
+            pltpu.VMEM((A_PIECES, tokens, width // A_PIECES), BF16),
+            pltpu.VMEM((2, tokens, lanes), F32),
         ],
         compiler_params=params(collective_id=0, has_side_effects=True),
         name="gather_attend",
     )(*weights, x, seg)
     shape = (groups, sizes[0] * rows, lanes)
-    return [wa.reshape(shape), wb.reshape(shape), wc.reshape(shape)] + rest
+    return [wa.reshape(shape), wb.reshape(shape), wc.reshape(shape), hid, nlt, xt, n1] + rest
 
 
 def other_first(order):
@@ -1156,7 +1208,8 @@
 
 
 def layer_kernel(
-    cot_ref, hid_ref, slope_ref, inv_ref, vec_ref, n1_hbm, nlt_hbm, wa_hbm, wb_hbm, wc_hbm,
+    cot_ref, hid_ref, slope_ref, inv_ref, vec_ref, second_hbm, n1_hbm, nlt_hbm, wa_hbm, wb_hbm,
+    wc_hbm,
     out_hbm, gb_hbm, gm_hbm, gbt_hbm, accb_hbm, part_ref, vg_ref, bg_ref,
     n1_ref, nlt_ref, wo_ref, wb_ref, wc_ref, acc, low, gst, gi, out_ref, gm_ref, gbt_ref,
     in_sem, out_sem, send, recv, accc, in_cc, accb, in_cb, ay_in, ax_in, bx_in, by_in, *, sizes,
@@ -1166,7 +1219,7 @@
     groups, deep = sizes[1], sizes[0] // 2
     lanes = wa_hbm.shape[2]
     tail = wo_ref.shape[2]
-    last = 3 * groups - 1
+    last = 2 * groups - 1
     place = Place(sizes)
     links = Links(send, recv)
     send_c, add_c = scatter_core(place, links, 0, accc, in_cc)
@@ -1185,7 +1238,8 @@
 
     def load(k):
         pairs = (
-            (n1_hbm, n1_ref), (nlt_hbm, nlt_ref.at[pl.ds(0, width)]), (wa_hbm.at[:, :, pl.ds(lanes - tail, tail)], wo_ref)
+            (second_hbm, acc), (n1_hbm, n1_ref), (nlt_hbm, nlt_ref),
+            (wa_hbm.at[:, :, pl.ds(lanes - tail, tail)], wo_ref),
         )
         return pltpu.make_async_copy(*pairs[k], in_sem.at[2 * groups + k])
 
@@ -1200,31 +1254,18 @@
 
     @pl.when(step == 0)
     def _():
+        load(0).start()
         for t in range(groups):
             outer(t).start()
-        load(0).start()
-        for t in range(groups):
             inner(t).start()
-        load(1).start()
-        load(2).start()
+        for k in range(1, 4):
+            load(k).start()
         place.greet()
         vg_ref[...] = jnp.zeros_like(vg_ref)
         bg_ref[...] = jnp.zeros_like(bg_ref)
-        acc[...] = jnp.zeros_like(acc)
-        nlt_ref[width:] = jnp.ones((nlt_ref.shape[0] - width, tokens), BF16)
-
-    @pl.when(step < groups)
-    def _():
-        outer(step).wait()
-        for here in columns:
-            acc[:, here] += dot(hid_ref[0], wc_ref[step, here], NT)
-
-    @pl.when(step == groups - 1)
-    def _():
         load(0).wait()
         for rows in blocks:
-            second = n1_ref[rows] * vec_ref[0:1, :] + vec_ref[1:2, :] + vec_ref[5:6, :]
-            normal_two, inverse_two = norm_parts(second + acc[rows])
+            normal_two, inverse_two = norm_parts(acc[rows])
             out_ref[rows] = (normal_two * vec_ref[2:3, :] + vec_ref[3:4, :]).astype(BF16)
             cot = cot_ref[rows].astype(F32)
             grad_second = norm_back(cot, normal_two, inverse_two, vec_ref[2:3, :])
@@ -1237,56 +1278,56 @@
             gst[:, rows] = part.T
         store(0).start()
 
-    @pl.when((step >= groups) & (step < 2 * groups))
-    def _():
-        slot = lax.rem(step - groups + 2, 4)
+    @pl.when(step < groups)
+    def _():
+        slot = lax.rem(step + 2, 4)
         for here in columns:
             part = dot(gst[...], hid_ref[0, :, here]).astype(BF16)
             accc[slot, :, :, :, here] = part.reshape(deep, 2, -1, 256)
 
-    @pl.when(step == groups + 1)
+    @pl.when(step == 1)
     def _():
         send_c(0)()
 
-    @pl.when(step == groups + 2)
+    @pl.when(step == 2)
     def _():
         send_c(1)()
 
-    @pl.when(step == 2 * groups)
+    @pl.when(step == groups)
     def _():
         add_c(0, 0)()
         add_c(1, 1)()
         start()
         for t in range(groups):
+            outer(t).wait()
             inner(t).wait()
-        load(1).wait()
-        load(2).wait()
+        for k in range(1, 4):
+            load(k).wait()
 
     @pl.when(step == last)
     def _():
         middle()
 
-    @pl.when(step >= 2 * groups)
-    def _():
-        order = step - 2 * groups
+    @pl.when(step >= groups)
+    def _():
+        order = step - groups
         slot = lax.rem(order + 2, 4)
         t = other_first(order)
         for here in columns:
             grad_hidden = dot(low[...], wc_ref[t, :, here])
             part = (grad_hidden * slope_ref[0, :, here].astype(F32)).astype(BF16)
             gi[:, here] = part
+            bg_ref[pl.ds(t, 1), here] = jnp.sum(part.astype(F32), axis=0, keepdims=True)
+        acc[...] += dot(gi[...], wb_ref[t], NT)
         for here in columns:
-            acc[:, here] += dot(gi[...], wb_ref[t, here], NT)
-        for here in columns:
-            part = dot(nlt_ref[...], gi[:, here])
-            bg_ref[pl.ds(t, 1), here] = part[width : width + 1]
-            accb[slot, :, :, :, here] = part[:width].astype(BF16).reshape(deep, 2, -1, 256)
-
-    @pl.when(step == 2 * groups + 1)
+            part = dot(nlt_ref[...], gi[:, here]).astype(BF16)
+            accb[slot, :, :, :, here] = part.reshape(deep, 2, -1, 256)
+
+    @pl.when(step == groups + 1)
     def _():
         send_b(0)()
 
-    @pl.when(step == 2 * groups + 2)
+    @pl.when(step == groups + 2)
     def _():
         send_b(1)()
 
@@ -1320,7 +1361,7 @@
             store_mixed(t).wait()
 
 
-def layer(cot, hid, slope, n1, inv1, nlt, wa, wb, wc, vec, sizes):
+def layer(cot, hid, slope, second, n1, inv1, nlt, wa, wb, wc, vec, sizes):
     tokens, width = cot.shape
     groups, _, lanes = wa.shape
     hidden = wb.shape[2]
@@ -1330,17 +1371,17 @@
     anywhere = pl.BlockSpec(memory_space=pl.ANY)
 
     def used(i):
-        return jnp.where(i < groups, i, other_first(jnp.clip(i - groups, 0, groups - 1)))
+        return other_first(jnp.minimum(i, groups - 1))
 
     def back_group(i):
-        return other_first(jnp.clip(i - 2 * groups, 0, groups - 1))
+        return other_first(jnp.clip(i - groups, 0, groups - 1))
 
     copies = 8
     parts = (2, deep, 2, rows, hidden)
     matrix = pltpu.VMEM((groups, width, hidden), BF16)
     return pl.pallas_call(
         functools.partial(layer_kernel, sizes=sizes),
-        grid=(3 * groups,),
+        grid=(2 * groups,),
         in_specs=[
             once(cot.shape),
             pl.BlockSpec((1, tokens, hidden), lambda i: (used(i), 0, 0)),
@@ -1348,7 +1389,7 @@
             once(inv1.shape),
             once(vec.shape),
         ]
-        + [anywhere] * 5,
+        + [anywhere] * 6,
         out_specs=[anywhere] * 5
         + [once((deep, rows, hidden)), once((8, width)), once((8, hidden))],
         out_shape=[
@@ -1363,7 +1404,7 @@
         ],
         scratch_shapes=[
             pltpu.VMEM(n1.shape, F32),
-            pltpu.VMEM((width + 16, tokens), BF16),
+            pltpu.VMEM((width, tokens), BF16),
             pltpu.VMEM((groups, width, tail), BF16),
             matrix,
             matrix,
@@ -1374,7 +1415,7 @@
             pltpu.VMEM((tokens, width), BF16),
             pltpu.VMEM((groups, tokens, tail), BF16),
             pltpu.VMEM((width, tokens), BF16),
-            pltpu.SemaphoreType.DMA((2 * groups + 3,)),
+            pltpu.SemaphoreType.DMA((2 * groups + 4,)),
             pltpu.SemaphoreType.DMA((4 + groups,)),
             pltpu.SemaphoreType.DMA((copies,)),
             pltpu.SemaphoreType.DMA((copies,)),
@@ -1383,7 +1424,7 @@
         + plane_buffers(deep, rows, hidden),
         compiler_params=params(collective_id=1, has_side_effects=True),
         name="layer",
-    )(cot, hid, slope, inv1, vec, n1, nlt, wa, wb, wc)
+    )(cot, hid, slope, inv1, vec, second, n1, nlt, wa, wb, wc)
 
 
 def far_first(step, groups):
@@ -1422,7 +1463,7 @@
     t, s = far_first(step, groups), step % 2
 
     def load(k):
-        pairs = ((accb_hbm, accb), (xt_hbm, xt_ref.at[pl.ds(0, width)]), (gbt_hbm, gbt_ref), (wa_hbm, wa_ref), (gb_hbm, gb_ref))
+        pairs = ((accb_hbm, accb), (xt_hbm, xt_ref), (gbt_hbm, gbt_ref), (wa_hbm, wa_ref), (gb_hbm, gb_ref))
         return pltpu.make_async_copy(*pairs[k], load_sem.at[k])
 
     @pl.when(step == 0)
@@ -1434,7 +1475,7 @@
         start()
         for k in range(1, 5):
             load(k).start()
-        xt_ref[width:] = jnp.ones((xt_ref.shape[0] - width, tokens), BF16)
+        gsum[...] = jnp.zeros_like(gsum)
         vec[...] = jnp.zeros_like(vec)
         hvec[...] = jnp.zeros_like(hvec)
         vec[0:6] = vg_ref[0:6]
@@ -1475,22 +1516,23 @@
     row = seg_ref[pl.ds(lax.axis_index("tensor") * 2 + s, 1)]
     attend_back(pm_ref.at[0], gm_ref.at[0], lse_ref, row, gp.at[t, rows], chunk)
 
+    for n in (0, 2, 3):
+        here = slice(n * 128, (n + 1) * 128)
+        gsum[t, 0:1, here] += jnp.sum(gp[t, rows, here].astype(F32), axis=0, keepdims=True)
+
     @pl.when(s == 1)
     def _():
         order = step // 2
         slot = jnp.where(order % 2 == 0, 2 + order // 2, t // 2)
-        for n in range(lanes // 256):
+        for n in range(2):
             here = slice(n * 256, (n + 1) * 256)
-            if n < lanes // 256 - 1:
-                part = dot(xt_ref[...], gp[t, :, here])
-                gsum[t, 0:1, here] = part[width : width + 1]
-                part = part[:width]
-            else:
-                from_x = dot(xt_ref[0:width], gp[t, :, here])
-                part = dot(gbt_ref[...], gp[t, :, here])
-                lane = lax.broadcasted_iota(jnp.int32, part.shape, 1)
-                part = jnp.where((lane >= 128) & (lane < 192), from_x, part)
-            acc[slot, :, :, :, here] = part.astype(BF16).reshape(deep, 2, -1, 256)
+            part = dot(xt_ref[...], gp[t, :, here]).astype(BF16)
+            acc[slot, :, :, :, here] = part.reshape(deep, 2, -1, 256)
+        from_x = dot(xt_ref[...], gp[t, :, 512:768])
+        part = dot(gbt_ref[...], gp[t, :, 512:768])
+        lane = lax.broadcasted_iota(jnp.int32, part.shape, 1)
+        part = jnp.where((lane >= 128) & (lane < 192), from_x, part).astype(BF16)
+        acc[slot, :, :, :, 512:768] = part.reshape(deep, 2, -1, 256)
 
     def input_columns(n):
         here = slice(n * 256, (n + 1) * 256)
@@ -1627,7 +1669,7 @@
             pltpu.SemaphoreType.DMA((5,)),
             pltpu.VMEM((rows, lanes), F32),
             pltpu.VMEM(wa.shape, BF16),
-            pltpu.VMEM((width + 16, tokens), BF16),
+            pltpu.VMEM(xt.shape, BF16),
             pltpu.VMEM(gbt.shape, BF16),
             pltpu.VMEM(gb.shape, F32),
             pltpu.VMEM(accb.shape, BF16),
@@ -1648,63 +1690,83 @@
 
 
 def apply_kernel(*refs):
-    grads, updates, sums = refs[0:5], refs[5:10], refs[10]
-    weights, means, squares = refs[11:16], refs[16:21], refs[21:26]
-    passed, outs, norms = refs[26:28], refs[28:43], refs[43]
-    wide, sem = refs[46], refs[47]
-    stores = [pltpu.make_async_copy(passed[0], refs[44], sem.at[0])]
-    stores[0].start()
-    rows = wide.shape[0] // 4
-    for k in range(4):
-        here = pl.ds(k * rows, rows)
-        wide[here] = passed[1][here].astype(F32)
-        stores.append(pltpu.make_async_copy(wide.at[here], refs[45].at[here], sem.at[1 + k]))
+    sums, ins, passed = refs[0], refs[1:26], refs[26:28]
+    norms, outs, finals = refs[28], refs[29:44], refs[44:46]
+    held, kept, narrow, wide = refs[46:71], refs[71], refs[72], refs[73]
+    in_sem, out_sem = refs[74], refs[75]
+    loads = [pltpu.make_async_copy(ins[k], held[k], in_sem.at[k]) for k in range(25)]
+    result = pltpu.make_async_copy(passed[0], kept, in_sem.at[25])
+    gradient = pltpu.make_async_copy(passed[1], narrow, in_sem.at[26])
+    gradient.start()
+    order = [(i, k) for i in range(5) for k in (0, 3, 4, 1, 2)]
+    for i, k in order:
+        loads[5 * k + i].start()
+    result.start()
+    stores = []
+
+    def store(src, dst):
+        stores.append(pltpu.make_async_copy(src, dst, out_sem.at[len(stores)]))
         stores[-1].start()
+
     roots = jnp.sqrt(sums[...])
     norms[...] = roots[0:2, 0:15]
     ratio = LEARN_RATE * roots[0:1] / (roots[1:2] + ADAM_EPS)
+    rows = wide.shape[0] // 4
+    gradient.wait()
+    for k in range(4):
+        here = pl.ds(k * rows, rows)
+        wide[here] = narrow[here].astype(F32)
+        store(wide.at[here], finals[1].at[here])
     for i in range(5):
-        grad = grads[i][...]
-        outs[3 * i][...] = MOMENT_DECAY * means[i][...] + (1.0 - MOMENT_DECAY) * grad
-        outs[3 * i + 1][...] = (
-            MOMENT_DECAY * squares[i][...] + (1.0 - MOMENT_DECAY) * grad * grad
-        )
-        target = outs[3 * i + 2]
+        for k in (0, 3, 4, 1, 2):
+            loads[5 * k + i].wait()
+        grad, update, weight, mean, square = (held[5 * k + i] for k in range(5))
+        value = grad[...]
+        mean[...] = MOMENT_DECAY * mean[...] + (1.0 - MOMENT_DECAY) * value
+        square[...] = MOMENT_DECAY * square[...] + (1.0 - MOMENT_DECAY) * value * value
         if i == 0:
             for k in range(3):
-                target[k] = weights[i][k] - ratio[:, k : k + 1] * updates[i][k]
+                weight[k] = weight[k] - ratio[:, k : k + 1] * update[k]
         elif i < 4:
-            target[...] = weights[i][...] - ratio[:, 2 + i : 3 + i] * updates[i][...]
+            weight[...] = weight[...] - ratio[:, 2 + i : 3 + i] * update[...]
         else:
-            for row in range(target.shape[0]):
+            for row in range(weight.shape[0]):
                 here = slice(row, row + 1)
                 step = ratio[:, 6 + min(row, 8) : 7 + min(row, 8)]
-                target[here] = weights[i][here] - step * updates[i][here]
+                weight[here] = weight[here] - step * update[here]
+        store(mean, outs[3 * i])
+        store(square, outs[3 * i + 1])
+        store(weight, outs[3 * i + 2])
+    result.wait()
+    store(kept, finals[0])
     for move in stores:
         move.wait()
 
 
 def apply(grads, updates, sums, weights, means, squares, passed):
-    inside = pl.BlockSpec(memory_space=pltpu.VMEM)
-    shapes = []
+    inside, anywhere = pl.BlockSpec(memory_space=pltpu.VMEM), pl.BlockSpec(memory_space=pl.ANY)
+    shapes = [jax.ShapeDtypeStruct((2, 15), F32)]
     for weight in weights:
         shapes += [jax.ShapeDtypeStruct(weight.shape, F32)] * 3
-    shapes.append(jax.ShapeDtypeStruct((2, 15), F32))
     shapes += [jax.ShapeDtypeStruct(passed[0].shape, BF16)]
     shapes += [jax.ShapeDtypeStruct(passed[1].shape, F32)]
-    anywhere = [pl.BlockSpec(memory_space=pl.ANY)] * 2
-    return pl.pallas_call(
+    norms, *rest = pl.pallas_call(
         apply_kernel,
-        in_specs=[inside] * 28,
-        out_specs=[inside] * 16 + anywhere,
+        in_specs=[inside] + [anywhere] * 27,
+        out_specs=[inside] + [anywhere] * 17,
         out_shape=shapes,
-        scratch_shapes=[
+        scratch_shapes=[pltpu.VMEM(weight.shape, F32) for _ in range(5) for weight in weights]
+        + [
+            pltpu.VMEM(passed[0].shape, BF16),
+            pltpu.VMEM(passed[1].shape, BF16),
             pltpu.VMEM(passed[1].shape, F32),
-            pltpu.SemaphoreType.DMA((5,)),
+            pltpu.SemaphoreType.DMA((27,)),
+            pltpu.SemaphoreType.DMA((20,)),
         ],
         compiler_params=params(),
         name="apply",
-    )(*grads, *updates, sums, *weights, *means, *squares, *passed)
+    )(sums, *grads, *updates, *weights, *means, *squares, *passed)
+    return rest[:15] + [norms] + rest[15:]
 
 
 def make_body(sizes):
@@ -1727,11 +1789,11 @@
             weights, old_means, old_squares = (
                 entry[:3] + (entry[3].T, entry[4]) for entry in (weights, old_means, old_squares)
             )
-            wa, wb, wc, full, pm, lse, hid, slope, nlt, xt, n1, inv1 = gather_attend(
+            wa, wb, wc, hid, nlt, xt, n1, full, pm, lse, slope, second, inv1 = gather_attend(
                 weights, tokens, segments, sizes
             )
             result, gb, gm, gbt, accb, part, vg, bg = layer(
-                cotangent, hid, slope, n1, inv1, nlt, wa, wb, wc, full, sizes
+                cotangent, hid, slope, second, n1, inv1, nlt, wa, wb, wc, full, sizes
             )
             *changes, sums, input_grad = back(
                 pm, gm, lse, segments, wa, xt, gbt, gb, accb, part, vg, bg,

time: 216 us -> 209 us (0.968)
  Pallas kernels: 215 us -> 208 us
    pallas_call x2, Pallas kernels: 62 us -> 48 us  [the longest x1 39.5 us: layer(): pl.pallas_call(functools.partial(layer_kernel, sizes=sizes), grid=(2 * gr...]
    pallas_call x1, Pallas kernels: 82 us -> 87.3 us  [gather_attend(): pl.pallas_call(functools.partial(gather_attend_kernel, sizes=sizes, chunk...]
where the time goes in v3:
time: 209 us
  Pallas kernels  208 us (100%)
    pallas_call x1, Pallas kernels, gather_attend(): pl.pallas_call(functools.partial(gather_attend_kernel, sizes=sizes, chunk...  87.3 us
    pallas_call x1, Pallas kernels, back(): pl.pallas_call(functools.partial(back_kernel, sizes=sizes, chunk=min(256,...  73 us
    pallas_call x1, Pallas kernels, layer(): pl.pallas_call(functools.partial(layer_kernel, sizes=sizes), grid=(2 * gr...  39.5 us
    pallas_call x1, Pallas kernels, apply(): pl.pallas_call(apply_kernel, in_specs=[inside] + [anywhere] * 27, out_spe...  8.44 us

profile of v3, /device:TPU:0, one launch (start us, length us, event | category | flops | bytes accessed | tf_op | source)
XLA Modules:
  0.0 209.1 jit_solution(17054386936227592429)
XLA Ops:
  0.7 87.3 %gather_attend.1 = (bf16[2,2,4,2,96,768]{5,4,3,2,1,0:T(8,128)(2,1)}, bf16[2,2,4,2,96,768]{5,4,3,2,1,0:T(8,128)(2,1)}, bf16[2,2,4,2,96,768]{5,4,3,2,1,0:T(8,128)(...) custom-call(f32[3,96,192]{2,1,0:T(8,128)} %refs_11_.3, ...), custom_call_target="tpu_custom_call" | custom-call | tf_op jit(solution)/shard_map/gather_attend/pallas_call | solution.py:1148
  88.0 39.5 %layer.1 = (bf16[1024,768]{1,0:T(8,128)(2,1)}, f32[1024,768]{1,0:T(8,128)}, bf16[4,1024,256]{2,1,0:T(8,128)(2,1)}, bf16[768,1024]{1,0:T(8,128)(2,1)}, bf16[2,4,2...) custom-call(bf16[1024,768]{1,0:T(8,128)(2,1)} %cot_ref.1, ...), custom_call_target="tpu_custom_call" | custom-call | tf_op jit(solution)/shard_map/layer/pallas_call | solution.py:1382
  127.5 73.0 %back.1 = (f32[3,96,192]{2,1,0:T(8,128)}, f32[192,96]{1,0:T(8,128)}, f32[96,768]{1,0:T(8,128)}, f32[96,768]{1,0:T(8,128)}, f32[12,24]{1,0:T(8,128)}, /*index=5*/...) custom-call(bf16[4,1024,768]{2,1,0:T(8,128)(2,1)} %get-tuple-element, ...), custom_call_target="tpu_custom_call" | custom-call | tf_op jit(solution)/shard_map/back/pallas_call | solution.py:1639
  200.5 8.4 %apply.1 = (f32[2,15]{1,0:T(2,128)}, f32[3,96,192]{2,1,0:T(8,128)}, f32[3,96,192]{2,1,0:T(8,128)}, f32[3,96,192]{2,1,0:T(8,128)}, f32[192,96]{1,0:T(8,128)}, /*i...) custom-call(f32[8,128]{1,0:T(8,128)} %get-tuple-element.89.refs_0_, ...), custom_call_target="tpu_custom_call" | custom-call | tf_op jit(solution)/shard_map/apply/pallas_call | solution.py:1753

commit v4 on v3

--- a/solution.py
+++ b/solution.py
@@ -512,7 +512,7 @@
     rows, first, later = pl.ds(start, count), pl.ds(start, half), pl.ds(start + half, half)
     own = own.at[rows]
     mine = whole.at[p.x, p.c, p.z, p.y, rows]
-    line = whole.at[p.x, p.c, :, p.y, rows]
+    half_in = whole.at[:, p.c, :, :, rows]
     ax = whole.at[p.x, p.c, :, p.y, first]
     ax_in = whole.at[1 - p.x, p.c, :, p.y, first]
     by = whole.at[p.x, p.c, :, p.y, later]
@@ -537,40 +537,27 @@
             links.landed(kz + j, whole.at[p.x, p.c, p.from_z(j), p.y, rows], p.to_z(j))
         links.copy(ka, ax, p.to_x()).start()
         links.copy(kb, by, p.to_y()).start()
-        links.copy(ks, line, p.to_c()).start()
 
     def stage2():
         links.landed(ka, ax_in, p.to_x())
         links.copy(ka + 1, ay, p.to_y()).start()
-        links.copy(ks + 1, ax_in, p.to_c()).start()
         links.landed(kb, by_in, p.to_y())
         links.copy(kb + 1, bx, p.to_x()).start()
-        links.copy(ks + 2, by_in, p.to_c()).start()
 
     def stage3():
         links.landed(ka + 1, ay_in, p.to_y())
-        links.copy(ks + 3, ay_in, p.to_c()).start()
         links.landed(kb + 1, bx_in, p.to_x())
-        links.copy(ks + 4, bx_in, p.to_c()).start()
+        links.copy(ks, half_in, p.to_c()).start()
 
     def stage4():
-        o = 1 - p.c
-        links.landed(ks, whole.at[p.x, o, :, p.y, rows], p.to_c())
-        links.landed(ks + 1, whole.at[1 - p.x, o, :, p.y, first], p.to_c())
-        links.landed(ks + 2, whole.at[p.x, o, :, 1 - p.y, later], p.to_c())
-        links.landed(ks + 3, whole.at[:, o, :, 1 - p.y, first], p.to_c())
-        links.landed(ks + 4, whole.at[1 - p.x, o, :, :, later], p.to_c())
+        links.landed(ks, whole.at[:, 1 - p.c, :, :, rows], p.to_c())
         for j in range(1, deep):
             links.copy(kz + j, own, p.to_z(j), mine).wait_send()
         links.copy(ka, ax, p.to_x()).wait_send()
         links.copy(kb, by, p.to_y()).wait_send()
         links.copy(ka + 1, ay, p.to_y()).wait_send()
         links.copy(kb + 1, bx, p.to_x()).wait_send()
-        links.copy(ks, line, p.to_c()).wait_send()
-        links.copy(ks + 1, ax_in, p.to_c()).wait_send()
-        links.copy(ks + 2, by_in, p.to_c()).wait_send()
-        links.copy(ks + 3, ay_in, p.to_c()).wait_send()
-        links.copy(ks + 4, bx_in, p.to_c()).wait_send()
+        links.copy(ks, half_in, p.to_c()).wait_send()
 
     return [stage0, stage1, stage2, stage3, stage4]
 
@@ -916,8 +903,8 @@
     return outs + [jnp.stack([weight_norms, update_norms])]
 
 
-A_PIECES = 3
-C_ROWS = ((0, 64), (64, 32))
+A_ROWS = ((0, 64), (64, 32))
+C_ROWS = ((0, 96),)
 
 
 def own_first(order):
@@ -944,12 +931,11 @@
     lanes = pack_a.shape[1]
     length = tokens // 2
     tail = 256
-    count = pack_a.shape[0] // A_PIECES
     ga = [
-        gather_stages(place, links, k * each, pack_a, wa, k * count, count) for k in range(A_PIECES)
+        gather_stages(place, links, n * each, pack_a, wa, *rows) for n, rows in enumerate(A_ROWS)
     ]
-    gb = gather_stages(place, links, A_PIECES * each, pack_b, wb)
-    more = (A_PIECES + 1) * each
+    gb = gather_stages(place, links, len(A_ROWS) * each, pack_b, wb)
+    more = (len(A_ROWS) + 1) * each
     small = add_everywhere(place, links, more, full, slots)
     more += deep + 2
     gc = [
@@ -967,9 +953,11 @@
         return pltpu.make_async_copy(*pairs[k], out_sem.at[k])
 
     def project(piece):
-        here = pl.ds(piece * count, count)
+        start, count = A_ROWS[piece]
+        here, columns = pl.ds(start, count), pl.ds(start * sizes[0], count * sizes[0])
         for x in range(2):
-            part = dot(xp[piece], wa[x, place.c, :, :, here].reshape(sizes[0] * count, lanes))
+            weight = wa[x, place.c, :, :, here].reshape(sizes[0] * count, lanes)
+            part = dot(xp[:, columns], weight)
             proj_acc[x] = part if piece == 0 else proj_acc[x] + part
 
     @pl.when(step == 0)
@@ -977,20 +965,16 @@
         out_rows = out_ref[...].T
         pack_a[...] = spread(qkv_ref[0], qkv_ref[1], qkv_ref[2], out_rows).astype(BF16)
         place.greet()
-        for k in range(A_PIECES):
-            ga[k][0]()
+        for piece in ga:
+            piece[0]()
         pack_c[...] = outer_ref[...].astype(BF16)
         gc[0][0]()
-        gc[1][0]()
         pack_b[...] = inner_ref[...].astype(BF16)
         xt_ref[...] = x_ref[...].T
-        each_dp = pack_a.shape[0]
-        for k in range(A_PIECES):
-            picked = [
-                xt_ref[dp * each_dp + k * count : dp * each_dp + (k + 1) * count]
-                for dp in range(sizes[0])
-            ]
-            xp[k] = jnp.concatenate(picked, axis=0).T
+        block = pack_a.shape[0]
+        for start, count in A_ROWS:
+            picked = [xt_ref[dp * block + start : dp * block + start + count] for dp in range(sizes[0])]
+            xp[:, start * sizes[0] : (start + count) * sizes[0]] = jnp.concatenate(picked, axis=0).T
         full[...] = jnp.zeros_like(full)
         mine = vec_ref.shape[1]
         full[0 : vec_ref.shape[0], 0:mine] = vec_ref[...]
@@ -1000,13 +984,11 @@
         small[1]()
         ga[0][1]()
         small[2]()
+        ga[1][1]()
         ga[0][2]()
-        ga[1][1]()
         small[3]()
         gb[0]()
-        ga[2][1]()
         ga[1][2]()
-        ga[2][2]()
         ga[0][3]()
         project(0)
         small[4]()
@@ -1019,14 +1001,12 @@
         n1_ref[...] = x_ref[...].astype(F32) + full[4:5, :]
         ga[1][3]()
         project(1)
-        ga[2][3]()
-        project(2)
 
     @pl.when(step == groups)
     def _():
         gb[2]()
-        for k in range(A_PIECES):
-            ga[k][4]()
+        for piece in ga:
+            piece[4]()
         keep(0).start()
 
     @pl.when(step == 1)
@@ -1034,26 +1014,19 @@
         gb[1]()
         gc[0][1]()
 
-    @pl.when(step == 5)
-    def _():
-        gc[1][1]()
-
     @pl.when(step == 2 * groups + 2)
     def _():
         gb[4]()
         keep(1).start()
-        gc[1][2]()
 
     @pl.when(step == 3 * groups)
     def _():
         gc[0][3]()
-        gc[1][3]()
         keep(3).start()
 
     @pl.when(step == 3 * groups + 2)
     def _():
         gc[0][4]()
-        gc[1][4]()
         keep(2).start()
 
     @pl.when((step < groups) & (s == 0))
@@ -1127,7 +1100,7 @@
 def gather_attend(weights, x, seg, sizes):
     qkv, out, inner, outer, vec = weights
     deep, groups = sizes[0] // 2, sizes[1]
-    copies = (A_PIECES + 1) * (GATHER_COPIES + deep) + deep + 2
+    copies = (len(A_ROWS) + 1) * (GATHER_COPIES + deep) + deep + 2
     copies += len(C_ROWS) * (GATHER_COPIES + 2 * deep)
     tokens, width = x.shape
     length = seg.shape[1]
@@ -1192,7 +1165,7 @@
             pltpu.VMEM((groups, 8, lanes), F32),
             pltpu.VMEM((tokens, width), BF16),
             pltpu.SemaphoreType.DMA((7,)),
-            pltpu.VMEM((A_PIECES, tokens, width // A_PIECES), BF16),
+            pltpu.VMEM((tokens, width), BF16),
             pltpu.VMEM((2, tokens, lanes), F32),
         ],
         compiler_params=params(collective_id=0, has_side_effects=True),
@@ -1433,15 +1406,22 @@
     return jnp.where(step < groups, 1 - x, x) * 2 + jnp.where(step % groups < 2, 1 - c, c)
 
 
+def changes_of(refs):
+    qkv, out, hidden, vec = refs
+    return [
+        [qkv.at[k], out.at[k], hidden.at[k, 0], hidden.at[k, 1], vec.at[k]] for k in range(2)
+    ]
+
+
 def back_kernel(
     pm_ref, gm_ref, lse_ref, seg_ref, wa_hbm, xt_hbm, gbt_hbm, gb_hbm,
     accb_hbm, part_ref, vg_ref, bg_ref, *refs, sizes, chunk,
 ):
     weights, means, squares = refs[0:5], refs[5:10], refs[10:15]
-    grads, updates, norms, ig_ref = refs[15:20], refs[20:25], refs[25], refs[26]
-    gp, gsum, send, recv, slots, hslots, nslots, vec, hvec, load_sem, sa = refs[27:38]
-    wa_ref, xt_ref, gbt_ref, gb_ref, accb, inz_b, inz_c = refs[38:45]
-    bufs_b, bufs_a, acc = refs[45:49], refs[49:56], refs[49]
+    (grads, updates), norms, ig_ref = changes_of(refs[15:19]), refs[19], refs[20]
+    gp, gsum, send, recv, slots, hslots, nslots, vec, hvec, load_sem, sa = refs[21:32]
+    wa_ref, xt_ref, gbt_ref, gb_ref, accb, inz_b, inz_c = refs[32:39]
+    bufs_b, bufs_a, acc = refs[39:43], refs[43:50], refs[43]
     sb, sc = grads[2], grads[3]
     step = pl.program_id(0)
     groups, deep = sizes[1], sizes[0] // 2
@@ -1632,7 +1612,11 @@
     copies = 7 + 2 * deep + 4 + 2 * deep + 2 * (deep + 2) + 7 + deep
     small = [weights, means, squares]
     anywhere = pl.BlockSpec(memory_space=pl.ANY)
-    outs = [jax.ShapeDtypeStruct(weight.shape, F32) for weight in weights] * 2 + [
+    outs = [
+        jax.ShapeDtypeStruct((2,) + weights[0].shape, F32),
+        jax.ShapeDtypeStruct((2,) + weights[1].shape, F32),
+        jax.ShapeDtypeStruct((2, 2) + weights[2].shape, F32),
+        jax.ShapeDtypeStruct((2,) + weights[4].shape, F32),
         jax.ShapeDtypeStruct((8, 128), F32),
         jax.ShapeDtypeStruct((tokens, width), BF16),
     ]
@@ -1690,83 +1674,63 @@
 
 
 def apply_kernel(*refs):
-    sums, ins, passed = refs[0], refs[1:26], refs[26:28]
-    norms, outs, finals = refs[28], refs[29:44], refs[44:46]
-    held, kept, narrow, wide = refs[46:71], refs[71], refs[72], refs[73]
-    in_sem, out_sem = refs[74], refs[75]
-    loads = [pltpu.make_async_copy(ins[k], held[k], in_sem.at[k]) for k in range(25)]
-    result = pltpu.make_async_copy(passed[0], kept, in_sem.at[25])
-    gradient = pltpu.make_async_copy(passed[1], narrow, in_sem.at[26])
-    gradient.start()
-    order = [(i, k) for i in range(5) for k in (0, 3, 4, 1, 2)]
-    for i, k in order:
-        loads[5 * k + i].start()
-    result.start()
-    stores = []
-
-    def store(src, dst):
-        stores.append(pltpu.make_async_copy(src, dst, out_sem.at[len(stores)]))
+    (grads, updates), sums = changes_of(refs[0:4]), refs[4]
+    weights, means, squares = refs[5:10], refs[10:15], refs[15:20]
+    passed, outs, norms = refs[20:22], refs[22:37], refs[37]
+    wide, sem = refs[40], refs[41]
+    stores = [pltpu.make_async_copy(passed[0], refs[38], sem.at[0])]
+    stores[0].start()
+    rows = wide.shape[0] // 4
+    for k in range(4):
+        here = pl.ds(k * rows, rows)
+        wide[here] = passed[1][here].astype(F32)
+        stores.append(pltpu.make_async_copy(wide.at[here], refs[39].at[here], sem.at[1 + k]))
         stores[-1].start()
-
     roots = jnp.sqrt(sums[...])
     norms[...] = roots[0:2, 0:15]
     ratio = LEARN_RATE * roots[0:1] / (roots[1:2] + ADAM_EPS)
-    rows = wide.shape[0] // 4
-    gradient.wait()
-    for k in range(4):
-        here = pl.ds(k * rows, rows)
-        wide[here] = narrow[here].astype(F32)
-        store(wide.at[here], finals[1].at[here])
     for i in range(5):
-        for k in (0, 3, 4, 1, 2):
-            loads[5 * k + i].wait()
-        grad, update, weight, mean, square = (held[5 * k + i] for k in range(5))
-        value = grad[...]
-        mean[...] = MOMENT_DECAY * mean[...] + (1.0 - MOMENT_DECAY) * value
-        square[...] = MOMENT_DECAY * square[...] + (1.0 - MOMENT_DECAY) * value * value
+        grad = grads[i][...]
+        outs[3 * i][...] = MOMENT_DECAY * means[i][...] + (1.0 - MOMENT_DECAY) * grad
+        outs[3 * i + 1][...] = (
+            MOMENT_DECAY * squares[i][...] + (1.0 - MOMENT_DECAY) * grad * grad
+        )
+        target = outs[3 * i + 2]
         if i == 0:
             for k in range(3):
-                weight[k] = weight[k] - ratio[:, k : k + 1] * update[k]
+                target[k] = weights[i][k] - ratio[:, k : k + 1] * updates[i][k]
         elif i < 4:
-            weight[...] = weight[...] - ratio[:, 2 + i : 3 + i] * update[...]
+            target[...] = weights[i][...] - ratio[:, 2 + i : 3 + i] * updates[i][...]
         else:
-            for row in range(weight.shape[0]):
+            for row in range(target.shape[0]):
                 here = slice(row, row + 1)
                 step = ratio[:, 6 + min(row, 8) : 7 + min(row, 8)]
-                weight[here] = weight[here] - step * update[here]
-        store(mean, outs[3 * i])
-        store(square, outs[3 * i + 1])
-        store(weight, outs[3 * i + 2])
-    result.wait()
-    store(kept, finals[0])
+                target[here] = weights[i][here] - step * updates[i][here]
     for move in stores:
         move.wait()
 
 
-def apply(grads, updates, sums, weights, means, squares, passed):
-    inside, anywhere = pl.BlockSpec(memory_space=pltpu.VMEM), pl.BlockSpec(memory_space=pl.ANY)
-    shapes = [jax.ShapeDtypeStruct((2, 15), F32)]
+def apply(changes, sums, weights, means, squares, passed):
+    inside = pl.BlockSpec(memory_space=pltpu.VMEM)
+    shapes = []
     for weight in weights:
         shapes += [jax.ShapeDtypeStruct(weight.shape, F32)] * 3
+    shapes.append(jax.ShapeDtypeStruct((2, 15), F32))
     shapes += [jax.ShapeDtypeStruct(passed[0].shape, BF16)]
     shapes += [jax.ShapeDtypeStruct(passed[1].shape, F32)]
-    norms, *rest = pl.pallas_call(
+    anywhere = [pl.BlockSpec(memory_space=pl.ANY)] * 2
+    return pl.pallas_call(
         apply_kernel,
-        in_specs=[inside] + [anywhere] * 27,
-        out_specs=[inside] + [anywhere] * 17,
+        in_specs=[inside] * 22,
+        out_specs=[inside] * 16 + anywhere,
         out_shape=shapes,
-        scratch_shapes=[pltpu.VMEM(weight.shape, F32) for _ in range(5) for weight in weights]
-        + [
-            pltpu.VMEM(passed[0].shape, BF16),
-            pltpu.VMEM(passed[1].shape, BF16),
+        scratch_shapes=[
             pltpu.VMEM(passed[1].shape, F32),
-            pltpu.SemaphoreType.DMA((27,)),
-            pltpu.SemaphoreType.DMA((20,)),
+            pltpu.SemaphoreType.DMA((5,)),
         ],
         compiler_params=params(),
         name="apply",
-    )(sums, *grads, *updates, *weights, *means, *squares, *passed)
-    return rest[:15] + [norms] + rest[15:]
+    )(*changes, sums, *weights, *means, *squares, *passed)
 
 
 def make_body(sizes):
@@ -1785,7 +1749,7 @@
         weights = (qkv_weight, out_weight, inner_weight, outer_weight, vectors)
         old_means = (qkv_mean, out_mean, inner_mean, outer_mean, vector_mean)
         old_squares = (qkv_square, out_square, inner_square, outer_square, vector_square)
-        if sizes[0] % 2 == 0 and groups == 4 and qkv_weight.shape[1] % 96 == 0:
+        if sizes[0] % 2 == 0 and groups == 4 and qkv_weight.shape[1] == sum(A_ROWS[-1]):
             weights, old_means, old_squares = (
                 entry[:3] + (entry[3].T, entry[4]) for entry in (weights, old_means, old_squares)
             )
@@ -1801,7 +1765,7 @@
             )
             passed = (result, input_grad)
             new = list(
-                apply(changes[:5], changes[5:], sums, weights, old_means, old_squares, passed)
+                apply(changes, sums, weights, old_means, old_squares, passed)
             )
             new[9:12] = [entry.T for entry in new[9:12]]
             return tuple(new[16:]) + tuple(new[:16])

time: 209 us -> 215 us (1.029)
  Pallas kernels: 208 us -> 214 us
    pallas_call x1, Pallas kernels: 39.5 us -> 47.1 us  [layer(): pl.pallas_call(functools.partial(layer_kernel, sizes=sizes), grid=(2 * gr...]
where the time goes in v4:
time: 215 us
  Pallas kernels  214 us (100%)
    pallas_call x1, Pallas kernels, gather_attend(): pl.pallas_call(functools.partial(gather_attend_kernel, sizes=sizes, chunk...  85.9 us
    pallas_call x1, Pallas kernels, back(): pl.pallas_call(functools.partial(back_kernel, sizes=sizes, chunk=min(256,...  73.6 us
    pallas_call x1, Pallas kernels, layer(): pl.pallas_call(functools.partial(layer_kernel, sizes=sizes), grid=(2 * gr...  47.1 us
    pallas_call x1, Pallas kernels, apply(): pl.pallas_call(apply_kernel, in_specs=[inside] * 22, out_specs=[inside] *...  7.36 us

profile of v4, /device:TPU:0, one launch (start us, length us, event | category | flops | bytes accessed | tf_op | source)
XLA Modules:
  0.0 214.8 jit_solution(10663663787359969778)
XLA Ops:
  0.7 85.9 %gather_attend.1 = (bf16[2,2,4,2,96,768]{5,4,3,2,1,0:T(8,128)(2,1)}, bf16[2,2,4,2,96,768]{5,4,3,2,1,0:T(8,128)(2,1)}, bf16[2,2,4,2,96,768]{5,4,3,2,1,0:T(8,128)(...) custom-call(f32[3,96,192]{2,1,0:T(8,128)} %refs_5_.3, ...), custom_call_target="tpu_custom_call" | custom-call | tf_op jit(solution)/shard_map/gather_attend/pallas_call | solution.py:1121
  86.6 47.1 %layer.1 = (bf16[1024,768]{1,0:T(8,128)(2,1)}, f32[1024,768]{1,0:T(8,128)}, bf16[4,1024,256]{2,1,0:T(8,128)(2,1)}, bf16[768,1024]{1,0:T(8,128)(2,1)}, bf16[2,4,2...) custom-call(bf16[1024,768]{1,0:T(8,128)(2,1)} %cot_ref.1, ...), custom_call_target="tpu_custom_call" | custom-call | tf_op jit(solution)/shard_map/layer/pallas_call | solution.py:1355
  133.7 73.6 %back.1 = (f32[2,3,96,192]{3,2,1,0:T(8,128)}, f32[2,192,96]{2,1,0:T(8,128)}, f32[2,2,96,768]{3,2,1,0:T(8,128)}, f32[2,12,24]{2,1,0:T(8,128)}, f32[8,128]{1,0:T(8,128)}, /*index=5*/bf16[1024,768]{1,0:T(8,128)(2,1)}) custom-call(bf16[4,1024,768]{2,1,0:T(8,128)(2,1)} %get-tuple-element.63.pm_ref, bf16[4,1024,256]{2,1,0:T(8,128)(2,1)} %get-tuple-element.74.gm_ref, ...), custom_call_target="tpu_custom_call" | custom-call | tf_op jit(solution)/shard_map/back/pallas_call | solution.py:1623
  207.3 7.4 %apply.1 = (f32[3,96,192]{2,1,0:T(8,128)}, f32[3,96,192]{2,1,0:T(8,128)}, f32[3,96,192]{2,1,0:T(8,128)}, f32[192,96]{1,0:T(8,128)}, f32[192,96]{1,0:T(8,128)}, /...) custom-call(f32[2,3,96,192]{3,2,1,0:T(8,128)} %get-tuple-element.83., ...), custom_call_target="tpu_custom_call" | custom-call | tf_op jit(solution)/shard_map/apply/pallas_call | solution.py:1722

commit v5 on v4

--- a/solution.py
+++ b/solution.py
@@ -391,6 +391,16 @@
     def to_c(self):
         return {"tensor": self.x * 2 + 1 - self.c}
 
+    def far_z(self):
+        if self.deep != 4:
+            return list(range(1, self.deep))
+        z = self.z
+        return [
+            jnp.where(z == 0, 3, jnp.where(z == 3, 1, 2)),
+            jnp.where(z == 1, 3, jnp.where(z == 2, 1, 2)),
+            jnp.where(z < 2, 1, 3),
+        ]
+
     def from_z(self, step):
         return lax.rem(self.z + self.deep - step, self.deep)
 
@@ -512,7 +522,7 @@
     rows, first, later = pl.ds(start, count), pl.ds(start, half), pl.ds(start + half, half)
     own = own.at[rows]
     mine = whole.at[p.x, p.c, p.z, p.y, rows]
-    half_in = whole.at[:, p.c, :, :, rows]
+    line = whole.at[p.x, p.c, :, p.y, rows]
     ax = whole.at[p.x, p.c, :, p.y, first]
     ax_in = whole.at[1 - p.x, p.c, :, p.y, first]
     by = whole.at[p.x, p.c, :, p.y, later]
@@ -528,7 +538,7 @@
 
     def stage0():
         keep().start()
-        for j in range(1, deep):
+        for j in p.far_z():
             links.copy(kz + j, own, p.to_z(j), mine).start()
 
     def stage1():
@@ -537,27 +547,40 @@
             links.landed(kz + j, whole.at[p.x, p.c, p.from_z(j), p.y, rows], p.to_z(j))
         links.copy(ka, ax, p.to_x()).start()
         links.copy(kb, by, p.to_y()).start()
+        links.copy(ks, line, p.to_c()).start()
 
     def stage2():
         links.landed(ka, ax_in, p.to_x())
         links.copy(ka + 1, ay, p.to_y()).start()
+        links.copy(ks + 1, ax_in, p.to_c()).start()
         links.landed(kb, by_in, p.to_y())
         links.copy(kb + 1, bx, p.to_x()).start()
+        links.copy(ks + 2, by_in, p.to_c()).start()
 
     def stage3():
         links.landed(ka + 1, ay_in, p.to_y())
+        links.copy(ks + 3, ay_in, p.to_c()).start()
         links.landed(kb + 1, bx_in, p.to_x())
-        links.copy(ks, half_in, p.to_c()).start()
+        links.copy(ks + 4, bx_in, p.to_c()).start()
 
     def stage4():
-        links.landed(ks, whole.at[:, 1 - p.c, :, :, rows], p.to_c())
+        o = 1 - p.c
+        links.landed(ks, whole.at[p.x, o, :, p.y, rows], p.to_c())
+        links.landed(ks + 1, whole.at[1 - p.x, o, :, p.y, first], p.to_c())
+        links.landed(ks + 2, whole.at[p.x, o, :, 1 - p.y, later], p.to_c())
+        links.landed(ks + 3, whole.at[:, o, :, 1 - p.y, first], p.to_c())
+        links.landed(ks + 4, whole.at[1 - p.x, o, :, :, later], p.to_c())
         for j in range(1, deep):
             links.copy(kz + j, own, p.to_z(j), mine).wait_send()
         links.copy(ka, ax, p.to_x()).wait_send()
         links.copy(kb, by, p.to_y()).wait_send()
         links.copy(ka + 1, ay, p.to_y()).wait_send()
         links.copy(kb + 1, bx, p.to_x()).wait_send()
-        links.copy(ks, half_in, p.to_c()).wait_send()
+        links.copy(ks, line, p.to_c()).wait_send()
+        links.copy(ks + 1, ax_in, p.to_c()).wait_send()
+        links.copy(ks + 2, by_in, p.to_c()).wait_send()
+        links.copy(ks + 3, ay_in, p.to_c()).wait_send()
+        links.copy(ks + 4, bx_in, p.to_c()).wait_send()
 
     return [stage0, stage1, stage2, stage3, stage4]
 
@@ -592,7 +615,7 @@
         keep().wait()
         links.landed(base + 1, whole.at[1 - p.x, p.c, p.z, p.y, first], p.to_x())
         links.landed(base + 2, whole.at[p.x, p.c, p.z, 1 - p.y, later], p.to_y())
-        for j in range(1, deep):
+        for j in p.far_z():
             links.copy(kf + j, pair_f, p.to_z(j)).start()
             links.copy(kl + j, pair_l, p.to_z(j)).start()
 
@@ -903,8 +926,8 @@
     return outs + [jnp.stack([weight_norms, update_norms])]
 
 
-A_ROWS = ((0, 64), (64, 32))
-C_ROWS = ((0, 96),)
+A_PIECES = 3
+C_ROWS = ((0, 64), (64, 32))
 
 
 def own_first(order):
@@ -931,11 +954,12 @@
     lanes = pack_a.shape[1]
     length = tokens // 2
     tail = 256
+    count = pack_a.shape[0] // A_PIECES
     ga = [
-        gather_stages(place, links, n * each, pack_a, wa, *rows) for n, rows in enumerate(A_ROWS)
+        gather_stages(place, links, k * each, pack_a, wa, k * count, count) for k in range(A_PIECES)
     ]
-    gb = gather_stages(place, links, len(A_ROWS) * each, pack_b, wb)
-    more = (len(A_ROWS) + 1) * each
+    gb = gather_stages(place, links, A_PIECES * each, pack_b, wb)
+    more = (A_PIECES + 1) * each
     small = add_everywhere(place, links, more, full, slots)
     more += deep + 2
     gc = [
@@ -953,11 +977,9 @@
         return pltpu.make_async_copy(*pairs[k], out_sem.at[k])
 
     def project(piece):
-        start, count = A_ROWS[piece]
-        here, columns = pl.ds(start, count), pl.ds(start * sizes[0], count * sizes[0])
+        here = pl.ds(piece * count, count)
         for x in range(2):
-            weight = wa[x, place.c, :, :, here].reshape(sizes[0] * count, lanes)
-            part = dot(xp[:, columns], weight)
+            part = dot(xp[piece], wa[x, place.c, :, :, here].reshape(sizes[0] * count, lanes))
             proj_acc[x] = part if piece == 0 else proj_acc[x] + part
 
     @pl.when(step == 0)
@@ -965,16 +987,20 @@
         out_rows = out_ref[...].T
         pack_a[...] = spread(qkv_ref[0], qkv_ref[1], qkv_ref[2], out_rows).astype(BF16)
         place.greet()
-        for piece in ga:
-            piece[0]()
+        for k in range(A_PIECES):
+            ga[k][0]()
         pack_c[...] = outer_ref[...].astype(BF16)
         gc[0][0]()
+        gc[1][0]()
         pack_b[...] = inner_ref[...].astype(BF16)
         xt_ref[...] = x_ref[...].T
-        block = pack_a.shape[0]
-        for start, count in A_ROWS:
-            picked = [xt_ref[dp * block + start : dp * block + start + count] for dp in range(sizes[0])]
-            xp[:, start * sizes[0] : (start + count) * sizes[0]] = jnp.concatenate(picked, axis=0).T
+        each_dp = pack_a.shape[0]
+        for k in range(A_PIECES):
+            picked = [
+                xt_ref[dp * each_dp + k * count : dp * each_dp + (k + 1) * count]
+                for dp in range(sizes[0])
+            ]
+            xp[k] = jnp.concatenate(picked, axis=0).T
         full[...] = jnp.zeros_like(full)
         mine = vec_ref.shape[1]
         full[0 : vec_ref.shape[0], 0:mine] = vec_ref[...]
@@ -984,11 +1010,13 @@
         small[1]()
         ga[0][1]()
         small[2]()
+        ga[0][2]()
         ga[1][1]()
-        ga[0][2]()
         small[3]()
         gb[0]()
+        ga[2][1]()
         ga[1][2]()
+        ga[2][2]()
         ga[0][3]()
         project(0)
         small[4]()
@@ -1001,12 +1029,15 @@
         n1_ref[...] = x_ref[...].astype(F32) + full[4:5, :]
         ga[1][3]()
         project(1)
+        ga[2][3]()
+        project(2)
 
     @pl.when(step == groups)
     def _():
         gb[2]()
-        for piece in ga:
-            piece[4]()
+        gc[1][1]()
+        for k in range(A_PIECES):
+            ga[k][4]()
         keep(0).start()
 
     @pl.when(step == 1)
@@ -1018,15 +1049,18 @@
     def _():
         gb[4]()
         keep(1).start()
+        gc[1][2]()
 
     @pl.when(step == 3 * groups)
     def _():
         gc[0][3]()
+        gc[1][3]()
         keep(3).start()
 
     @pl.when(step == 3 * groups + 2)
     def _():
         gc[0][4]()
+        gc[1][4]()
         keep(2).start()
 
     @pl.when((step < groups) & (s == 0))
@@ -1055,6 +1089,7 @@
 
     @pl.when(step == 2 * groups)
     def _():
+        gc[0][2]()
         for r in range(tokens // 256):
             rows = slice(r * 256, (r + 1) * 256)
             normal_one, inverse_one = norm_parts(n1_ref[rows])
@@ -1067,7 +1102,6 @@
             nlt_ref[:, rows] = part.T
         for k in range(4, 7):
             keep(k).start()
-        gc[0][2]()
         gb[3]()
 
     @pl.when((step >= 2 * groups) & (step < 3 * groups))
@@ -1100,7 +1134,7 @@
 def gather_attend(weights, x, seg, sizes):
     qkv, out, inner, outer, vec = weights
     deep, groups = sizes[0] // 2, sizes[1]
-    copies = (len(A_ROWS) + 1) * (GATHER_COPIES + deep) + deep + 2
+    copies = (A_PIECES + 1) * (GATHER_COPIES + deep) + deep + 2
     copies += len(C_ROWS) * (GATHER_COPIES + 2 * deep)
     tokens, width = x.shape
     length = seg.shape[1]
@@ -1165,7 +1199,7 @@
             pltpu.VMEM((groups, 8, lanes), F32),
             pltpu.VMEM((tokens, width), BF16),
             pltpu.SemaphoreType.DMA((7,)),
-            pltpu.VMEM((tokens, width), BF16),
+            pltpu.VMEM((A_PIECES, tokens, width // A_PIECES), BF16),
             pltpu.VMEM((2, tokens, lanes), F32),
         ],
         compiler_params=params(collective_id=0, has_side_effects=True),
@@ -1749,7 +1783,7 @@
         weights = (qkv_weight, out_weight, inner_weight, outer_weight, vectors)
         old_means = (qkv_mean, out_mean, inner_mean, outer_mean, vector_mean)
         old_squares = (qkv_square, out_square, inner_square, outer_square, vector_square)
-        if sizes[0] % 2 == 0 and groups == 4 and qkv_weight.shape[1] == sum(A_ROWS[-1]):
+        if sizes[0] % 2 == 0 and groups == 4 and qkv_weight.shape[1] == sum(C_ROWS[-1]):
             weights, old_means, old_squares = (
                 entry[:3] + (entry[3].T, entry[4]) for entry in (weights, old_means, old_squares)
             )

time: 215 us -> 207 us (0.963)
  Pallas kernels: 214 us -> 206 us
    pallas_call x1, Pallas kernels: 47.1 us -> 41.6 us  [layer(): pl.pallas_call(functools.partial(layer_kernel, sizes=sizes), grid=(2 * gr...]
where the time goes in v5:
time: 207 us
  Pallas kernels  206 us (100%)
    pallas_call x1, Pallas kernels, gather_attend(): pl.pallas_call(functools.partial(gather_attend_kernel, sizes=sizes, chunk...  85.9 us
    pallas_call x1, Pallas kernels, back(): pl.pallas_call(functools.partial(back_kernel, sizes=sizes, chunk=min(256,...  71.6 us
    pallas_call x1, Pallas kernels, layer(): pl.pallas_call(functools.partial(layer_kernel, sizes=sizes), grid=(2 * gr...  41.6 us
    pallas_call x1, Pallas kernels, apply(): pl.pallas_call(apply_kernel, in_specs=[inside] * 22, out_specs=[inside] *...  7.36 us

profile of v5, /device:TPU:0, one launch (start us, length us, event | category | flops | bytes accessed | tf_op | source)
XLA Modules:
  0.0 207.3 jit_solution(8850105339263871423)
XLA Ops:
  0.7 85.9 %gather_attend.1 = (bf16[2,2,4,2,96,768]{5,4,3,2,1,0:T(8,128)(2,1)}, bf16[2,2,4,2,96,768]{5,4,3,2,1,0:T(8,128)(2,1)}, bf16[2,2,4,2,96,768]{5,4,3,2,1,0:T(8,128)(...) custom-call(f32[3,96,192]{2,1,0:T(8,128)} %refs_5_.3, ...), custom_call_target="tpu_custom_call" | custom-call | tf_op jit(solution)/shard_map/gather_attend/pallas_call | solution.py:1155
  86.5 41.6 %layer.1 = (bf16[1024,768]{1,0:T(8,128)(2,1)}, f32[1024,768]{1,0:T(8,128)}, bf16[4,1024,256]{2,1,0:T(8,128)(2,1)}, bf16[768,1024]{1,0:T(8,128)(2,1)}, bf16[2,4,2...) custom-call(bf16[1024,768]{1,0:T(8,128)(2,1)} %cot_ref.1, ...), custom_call_target="tpu_custom_call" | custom-call | tf_op jit(solution)/shard_map/layer/pallas_call | solution.py:1389
  128.2 71.6 %back.1 = (f32[2,3,96,192]{3,2,1,0:T(8,128)}, f32[2,192,96]{2,1,0:T(8,128)}, f32[2,2,96,768]{3,2,1,0:T(8,128)}, f32[2,12,24]{2,1,0:T(8,128)}, f32[8,128]{1,0:T(8,128)}, /*index=5*/bf16[1024,768]{1,0:T(8,128)(2,1)}) custom-call(bf16[4,1024,768]{2,1,0:T(8,128)(2,1)} %get-tuple-element.63.pm_ref, bf16[4,1024,256]{2,1,0:T(8,128)(2,1)} %get-tuple-element.74.gm_ref, ...), custom_call_target="tpu_custom_call" | custom-call | tf_op jit(solution)/shard_map/back/pallas_call | solution.py:1657
  199.8 7.4 %apply.1 = (f32[3,96,192]{2,1,0:T(8,128)}, f32[3,96,192]{2,1,0:T(8,128)}, f32[3,96,192]{2,1,0:T(8,128)}, f32[192,96]{1,0:T(8,128)}, f32[192,96]{1,0:T(8,128)}, /...) custom-call(f32[2,3,96,192]{3,2,1,0:T(8,128)} %get-tuple-element.83., ...), custom_call_target="tpu_custom_call" | custom-call | tf_op jit(solution)/shard_map/apply/pallas_call | solution.py:1756

commit v6 on v5

--- a/solution.py
+++ b/solution.py
@@ -499,7 +499,7 @@
         for k in range(1, 8):
             total = total + slots[k]
         own[...] = total
-        for j in range(1, deep):
+        for j in p.far_z():
             far(j).start()
         slots[8 + p.z] = total
 
@@ -789,13 +789,13 @@
         add_line(p, acc, near, p.y, first, ay_in.at[1])
         links.landed(base + 5, ax_in, p.to_x())
         add_line(p, acc, near, p.y, first, ax_in)
-        for j in range(1, deep):
+        for j in p.far_z():
             over_z(kf, j, first).start()
 
     def near3():
         links.landed(base + 6, by_in, p.to_y())
         add_line(p, acc, near, p.y, later, by_in)
-        for j in range(1, deep):
+        for j in p.far_z():
             over_z(kl, j, later).start()
 
     def near4():
@@ -825,7 +825,7 @@
         )
 
     def stage0():
-        for j in range(1, deep):
+        for j in place.far_z():
             send(j).start()
 
     def stage1():
@@ -1566,10 +1566,10 @@
                 line, lane = at // 256, slice(at % 256, at % 256 + HD)
                 hvec[line : line + 1, lane] = gsum[g, 0:1, Q_AT[h] : Q_AT[h] + HD]
                 hvec[3 + line : 4 + line, lane] = gsum[g, 0:1, V_AT[h] : V_AT[h] + HD]
-        small[0]()
+        a[2]()
         a[4]()
         a[5]()
-        a[2]()
+        small[0]()
         load(3).wait()
         load(4).wait()
         input_columns(0)

time: 207 us -> 208 us (level)
  no operation moved by 1% of the time
where the time goes in v6:
time: 208 us; the launch traced here: 207 us
  Pallas kernels  206 us (99%)
    pallas_call x1, Pallas kernels, gather_attend(): pl.pallas_call(functools.partial(gather_attend_kernel, sizes=sizes, chunk...  85.9 us
    pallas_call x1, Pallas kernels, back(): pl.pallas_call(functools.partial(back_kernel, sizes=sizes, chunk=min(256,...  71.6 us
    pallas_call x1, Pallas kernels, layer(): pl.pallas_call(functools.partial(layer_kernel, sizes=sizes), grid=(2 * gr...  41.6 us
    pallas_call x1, Pallas kernels, apply(): pl.pallas_call(apply_kernel, in_specs=[inside] * 22, out_specs=[inside] *...  7.36 us

profile of v6, /device:TPU:0, one launch (start us, length us, event | category | flops | bytes accessed | tf_op | source)
XLA Modules:
  0.0 207.3 jit_solution(1725979744271538606)
XLA Ops:
  0.7 85.9 %gather_attend.1 = (bf16[2,2,4,2,96,768]{5,4,3,2,1,0:T(8,128)(2,1)}, bf16[2,2,4,2,96,768]{5,4,3,2,1,0:T(8,128)(2,1)}, bf16[2,2,4,2,96,768]{5,4,3,2,1,0:T(8,128)(...) custom-call(f32[3,96,192]{2,1,0:T(8,128)} %refs_5_.3, ...), custom_call_target="tpu_custom_call" | custom-call | tf_op jit(solution)/shard_map/gather_attend/pallas_call | solution.py:1155
  86.5 41.6 %layer.1 = (bf16[1024,768]{1,0:T(8,128)(2,1)}, f32[1024,768]{1,0:T(8,128)}, bf16[4,1024,256]{2,1,0:T(8,128)(2,1)}, bf16[768,1024]{1,0:T(8,128)(2,1)}, bf16[2,4,2...) custom-call(bf16[1024,768]{1,0:T(8,128)(2,1)} %cot_ref.1, ...), custom_call_target="tpu_custom_call" | custom-call | tf_op jit(solution)/shard_map/layer/pallas_call | solution.py:1389
  128.2 71.6 %back.1 = (f32[2,3,96,192]{3,2,1,0:T(8,128)}, f32[2,192,96]{2,1,0:T(8,128)}, f32[2,2,96,768]{3,2,1,0:T(8,128)}, f32[2,12,24]{2,1,0:T(8,128)}, f32[8,128]{1,0:T(8,128)}, /*index=5*/bf16[1024,768]{1,0:T(8,128)(2,1)}) custom-call(bf16[4,1024,768]{2,1,0:T(8,128)(2,1)} %get-tuple-element.63.pm_ref, bf16[4,1024,256]{2,1,0:T(8,128)(2,1)} %get-tuple-element.74.gm_ref, ...), custom_call_target="tpu_custom_call" | custom-call | tf_op jit(solution)/shard_map/back/pallas_call | solution.py:1657
  199.8 7.4 %apply.1 = (f32[3,96,192]{2,1,0:T(8,128)}, f32[3,96,192]{2,1,0:T(8,128)}, f32[3,96,192]{2,1,0:T(8,128)}, f32[192,96]{1,0:T(8,128)}, f32[192,96]{1,0:T(8,128)}, /...) custom-call(f32[2,3,96,192]{3,2,1,0:T(8,128)} %get-tuple-element.83., ...), custom_call_target="tpu_custom_call" | custom-call | tf_op jit(solution)/shard_map/apply/pallas_call | solution.py:1756
